TPU v7x, 512 devices: a whole 4x4x16 slice. The times are simulated.
512 devices in a mesh: segment: 2 (over core), expert: 64 (over y, z), pair: 4 (over x).
Axes of the slice: x: 4, y: 4, z: 16, core: 2. Of those that a mesh axis runs over, the one named last changes fastest.
Arguments:
- acts: bfloat16 [2, 2, 12288, 768], P(None, None, 'expert', 'pair'), may hold values from -20 to 20
- cotangent: bfloat16 [2, 12288, 768], P(None, 'expert', 'pair'), may hold values from -6 to 6
- gates: float32 [2, 2, 12288], P(None, None, 'expert'), may hold values from 0.2 to 1
- owners: int32 [2, 2, 12288], P(None, None, 'expert'), may hold values from 0 to 63, as said below
- slots: int32 [2, 2, 12288], P(None, None, 'expert'), may hold values from 0 to 3
- w_in: bfloat16 [2, 64, 768, 3072], P('segment', 'expert', None, 'pair'), may hold values from -0.21875 to 0.21875
- w_out: bfloat16 [2, 64, 3072, 768], P('segment', 'expert', 'pair'), may hold values from -0.109375 to 0.109375
Outputs:
- grads: bfloat16 [2, 2, 12288, 768], P('segment', None, 'expert', 'pair')
- grad_in: bfloat16 [2, 64, 768, 3072], P('segment', 'expert', None, 'pair')
- grad_out: bfloat16 [2, 64, 3072, 768], P('segment', 'expert', 'pair')
Inputs may be any that keep to these rules, and one draw needn't show every extreme that they name: `owners`: within each aligned block of 192 tokens of one sublayer and micro-batch, no two tokens share both owner and slot. One expert, the same for all blocks of a draw, takes exactly 4 tokens of every block.
All inputs are finite; a program needn't handle non-finite values.
Results may differ from a plain program's by a relative error of at most 0.02.
Values may be sent and summed in bfloat16 or wider, within the bound.
No kernel may reach another device: no remote copies, remote signals or barrier semaphores. Data moves between devices by JAX's collectives and lax.ppermute only.
A program may use at most 64 MiB of HBM per device.

v0:
```python
import jax
import jax.numpy as jnp
from jax import lax
from jax.sharding import PartitionSpec as P


def from_behind(x, axis, by):
    count = lax.axis_size(axis)
    pairs = [(i, i + by) for i in range(count) if 0 <= i + by < count]
    return lax.ppermute(x, axis, pairs)


def gelu_value(pre_act):
    inner_arg = 0.7978845608 * (pre_act + 0.044715 * pre_act * pre_act * pre_act)
    return 0.5 * pre_act * (1.0 + jnp.tanh(inner_arg))


def gelu_slope(pre_act):
    inner_arg = 0.7978845608 * (pre_act + 0.044715 * pre_act * pre_act * pre_act)
    tangent = jnp.tanh(inner_arg)
    return 0.5 * (1.0 + tangent) + 0.5 * pre_act * (1.0 - tangent * tangent) * 0.7978845608 * (
        1.0 + 0.134145 * pre_act * pre_act
    )


def layer_pass(
    token_acts, upstream, gate_row, owner_row, slot_row, first_weights, second_weights, capacity
):
    tok_rows, feat_share = token_acts.shape
    expert_count = lax.axis_size("expert")
    pair_count = lax.axis_size("pair")
    width = feat_share * pair_count
    slot_rows = expert_count * capacity
    scaled = (gate_row[:, None] * upstream.astype(jnp.float32)).astype(jnp.bfloat16)
    target = owner_row * capacity + slot_row
    placing = (lax.broadcasted_iota(jnp.int32, (slot_rows, tok_rows), 0) == target[None, :]).astype(
        jnp.bfloat16
    )
    joined = jnp.concatenate([token_acts, scaled], axis=1)
    packed = jnp.dot(placing, joined, preferred_element_type=jnp.float32).astype(jnp.bfloat16)
    arrived = lax.all_to_all(
        packed.reshape(expert_count, capacity, 2 * feat_share),
        "expert",
        split_axis=0,
        concat_axis=0,
        tiled=True,
    )
    gathered = lax.all_gather(arrived.reshape(slot_rows, 2, feat_share), "pair", axis=2, tiled=True)
    slot_acts = gathered[:, 0]
    slot_grad = gathered[:, 1]
    act_float = slot_acts.astype(jnp.float32)
    scale_inv = lax.rsqrt(jnp.mean(act_float * act_float, axis=1) + 1e-06)
    normed = (act_float * scale_inv[:, None]).astype(jnp.bfloat16)
    pre_act = jnp.dot(normed, first_weights, preferred_element_type=jnp.float32)
    hidden = gelu_value(pre_act).astype(jnp.bfloat16)
    back_hidden = lax.dot_general(
        slot_grad, second_weights, (((1,), (1,)), ((), ())), preferred_element_type=jnp.float32
    )
    back_pre = (back_hidden * gelu_slope(pre_act)).astype(jnp.bfloat16)
    grad_first = lax.dot_general(
        normed, back_pre, (((0,), (0,)), ((), ())), preferred_element_type=jnp.float32
    )
    grad_second = lax.dot_general(
        hidden, slot_grad, (((0,), (0,)), ((), ())), preferred_element_type=jnp.float32
    )
    contract = (((1,), (1,)), ((), ()))
    half = first_weights.shape[1] // 2
    lower_part = lax.dot_general(
        back_pre[:, :half], first_weights[:, :half], contract, preferred_element_type=jnp.float32
    ).astype(jnp.bfloat16)
    upper_part = lax.dot_general(
        back_pre[:, half:], first_weights[:, half:], contract, preferred_element_type=jnp.float32
    ).astype(jnp.bfloat16)
    lower_part, upper_part = lax.optimization_barrier((lower_part, upper_part))
    partial_value = lower_part.astype(jnp.float32) + upper_part.astype(jnp.float32)
    summed = lax.psum(partial_value.astype(jnp.bfloat16), "pair").astype(jnp.float32)
    own_start = lax.axis_index("pair") * feat_share
    own_acts = lax.dynamic_slice_in_dim(act_float, own_start, feat_share, 1)
    inner = jnp.sum(summed * act_float, axis=1)
    own_sum = lax.dynamic_slice_in_dim(summed, own_start, feat_share, 1)
    branch = (
        scale_inv[:, None] * own_sum - (scale_inv**3 * inner / width)[:, None] * own_acts
    ).astype(jnp.bfloat16)
    returned = lax.all_to_all(
        branch.reshape(expert_count, capacity, feat_share),
        "expert",
        split_axis=0,
        concat_axis=0,
        tiled=True,
    )
    restored = lax.dot_general(
        placing,
        returned.reshape(slot_rows, feat_share),
        (((0,), (0,)), ((), ())),
        preferred_element_type=jnp.float32,
    )
    result = (upstream.astype(jnp.float32) + restored).astype(jnp.bfloat16)
    return (result, grad_first, grad_second)


def body(acts, cotangent, gates, owners, slots, w_in, w_out):
    segment_index = lax.axis_index("segment")
    micro_count = acts.shape[1]
    tok_rows = acts.shape[2]
    feat_share = acts.shape[3]
    expert_count = lax.axis_size("expert")
    capacity = max(2, (5 * tok_rows + 4 * expert_count - 1) // (4 * expert_count))
    own_first = w_in[0, 0]
    own_second = w_out[0, 0]
    layer_acts = lax.dynamic_index_in_dim(acts, segment_index, 0, False)
    layer_gates = lax.dynamic_index_in_dim(gates, segment_index, 0, False)
    layer_owners = lax.dynamic_index_in_dim(owners, segment_index, 0, False)
    layer_slots = lax.dynamic_index_in_dim(slots, segment_index, 0, False)
    first_total = jnp.zeros(own_first.shape, jnp.float32)
    second_total = jnp.zeros(own_second.shape, jnp.float32)
    results = jnp.zeros((micro_count, tok_rows, feat_share), jnp.bfloat16)
    received = jnp.zeros((tok_rows, feat_share), jnp.bfloat16)
    for tick in range(micro_count + 1):
        current = tick - 1 + segment_index
        usable = (current >= 0) & (current < micro_count)
        chosen = jnp.clip(current, 0, micro_count - 1)
        token_acts = lax.dynamic_index_in_dim(layer_acts, chosen, 0, False)
        gate_row = lax.dynamic_index_in_dim(layer_gates, chosen, 0, False)
        owner_row = lax.dynamic_index_in_dim(layer_owners, chosen, 0, False)
        slot_row = lax.dynamic_index_in_dim(layer_slots, chosen, 0, False)
        upstream = jnp.where(segment_index == 1, cotangent[min(tick, micro_count - 1)], received)
        result, grad_first, grad_second = layer_pass(
            token_acts, upstream, gate_row, owner_row, slot_row, own_first, own_second, capacity
        )
        weight_mask = usable.astype(jnp.float32)
        first_total = first_total + weight_mask * grad_first
        second_total = second_total + weight_mask * grad_second
        results = jnp.where(
            usable, lax.dynamic_update_index_in_dim(results, result, chosen, 0), results
        )
        if tick < micro_count:
            received = from_behind(result, "segment", -1)
    return (
        results[None],
        first_total.astype(jnp.bfloat16)[None, None],
        second_total.astype(jnp.bfloat16)[None, None],
    )


def solution(mesh):
    placed = (
        P(None, None, "expert", "pair"),
        P(None, "expert", "pair"),
        P(None, None, "expert"),
        P(None, None, "expert"),
        P(None, None, "expert"),
        P("segment", "expert", None, "pair"),
        P("segment", "expert", "pair", None),
    )
    return jax.shard_map(
        body,
        mesh=mesh,
        in_specs=placed,
        out_specs=(
            P("segment", None, "expert", "pair"),
            P("segment", "expert", None, "pair"),
            P("segment", "expert", "pair", None),
        ),
        check_vma=False,
    )
```

profile of v0, /device:TPU:1, one launch (start us, length us, event | category | flops | bytes accessed | tf_op | source)
XLA Modules:
  0.0 461.8 jit_solution(15888681186676555637)
XLA Ops:
  12.5 35.7 %all_to_all.30 = bf16[64,4,384]{2,1,0:T(4,128)(2,1)S(1)} all-to-all(bf16[64,4,384]{2,1,0:T(4,128)(2,1)S(1)} %reshape.185), channel_id=1, replica_groups=mesh['segment'=2,'expert'=64,'pair'=4] {'expert'}, dimensions={0} | all-to-all | bytes 393216 | tf_op jit(solution)/shard_map/all_to_all | solution.py:41
  48.9 11.4 %all_gather.9 = bf16[256,2,768]{0,1,2:T(2,128)(2,1)S(1)} all-gather(bf16[256,2,192]{0,1,2:T(2,128)(2,1)S(1)} %copy.19), channel_id=1, replica_groups=mesh['segment'=2,'expert'=64,'pair'=4] {'pair'}, dimensions={2}, use_global_device_ids=true | all-gather | bytes 983040 | tf_op jit(solution)/shard_map/all_gather | solution.py:48
  62.5 2.3 copy.28
  71.1 51.2 %all-reduce.4.cloned.1.call-done = bf16[256,768]{1,0:T(8,128)(2,1)} async-done(((bf16[256,768]{1,0:T(8,128)(2,1)}), bf16[256,768]{1,0:T(8,128)(2,1)}) %all-reduce.4.cloned.1.call-update) | async-done | bytes 393232 | tf_op jit(solution)/shard_map/psum | solution.py:76
  126.6 15.4 %all-to-all-start.1 = ((bf16[64,4,192]{2,1,0:T(4,128)(2,1)}), bf16[64,4,192]{2,1,0:T(4,128)(2,1)S(1)}, u32[]{:S(2)}, u32[]{:S(2)}) async-start(bf16[64,4,192]{2,1,0:T(4,128)(2,1)} %reshape.187), calls=%async_computation.1 | async-start | bytes 262144 | tf_op jit(solution)/shard_map/all_to_all | solution.py:84
  142.1 13.9 %all-to-all-done.1 = bf16[64,4,192]{2,1,0:T(4,128)(2,1)S(1)} async-done(((bf16[64,4,192]{2,1,0:T(4,128)(2,1)}), bf16[64,4,192]{2,1,0:T(4,128)(2,1)S(1)}, u32[]{:S(2)}, u32[]{:S(2)}) %all-to-all-start.1) | async-done | bytes 98336 | tf_op jit(solution)/shard_map/all_to_all | solution.py:84
  157.9 6.2 %collective-permute-start = (bf16[192,192]{1,0:T(8,128)(2,1)S(1)}, bf16[192,192]{1,0:T(8,128)(2,1)S(1)}, u32[]{:S(2)}, u32[]{:S(2)}) collective-permute-start(bf16[192,192]{1,0:T(8,128)(2,1)S(1)} %get-tuple-element.31), channel_id=1, source_target_pairs={{256,0},{257,1},{258,2},{259,3},{260,4},{261,5},{262,6},{263,7},{2... | collective-permute-start | bytes 221192 | tf_op jit(solution)/shard_map/ppermute | solution.py:10
  168.6 22.2 %all_to_all.31 = bf16[64,4,384]{2,1,0:T(4,128)(2,1)} all-to-all(bf16[64,4,384]{2,1,0:T(4,128)(2,1)S(1)} %reshape.189), channel_id=1, replica_groups=mesh['segment'=2,'expert'=64,'pair'=4] {'expert'}, dimensions={0} | all-to-all | bytes 393216 | tf_op jit(solution)/shard_map/all_to_all | solution.py:41
  192.9 12.6 %all_gather.10 = bf16[256,2,768]{0,1,2:T(2,128)(2,1)S(1)} all-gather(bf16[256,2,192]{0,1,2:T(2,128)(2,1)} %copy.22), channel_id=1, replica_groups=mesh['segment'=2,'expert'=64,'pair'=4] {'pair'}, dimensions={2}, use_global_device_ids=true | all-gather | bytes 983040 | tf_op jit(solution)/shard_map/all_gather | solution.py:48
  205.5 2.2 fusion.147
  211.4 2.9 copy.31
  218.9 49.0 %all-reduce.6.cloned.1.call-done = bf16[256,768]{1,0:T(8,128)(2,1)} async-done(((bf16[256,768]{1,0:T(8,128)(2,1)}), bf16[256,768]{1,0:T(8,128)(2,1)}) %all-reduce.6.cloned.1.call-update) | async-done | bytes 393232 | tf_op jit(solution)/shard_map/psum | solution.py:76
  273.7 15.6 %all-to-all-start.3 = ((bf16[64,4,192]{2,1,0:T(4,128)(2,1)}), bf16[64,4,192]{2,1,0:T(4,128)(2,1)}, u32[]{:S(2)}, u32[]{:S(2)}) async-start(bf16[64,4,192]{2,1,0:T(4,128)(2,1)} %reshape.191), calls=%async_computation.3 | async-start | bytes 262144 | tf_op jit(solution)/shard_map/all_to_all | solution.py:84
  289.3 13.8 %all-to-all-done.3 = bf16[64,4,192]{2,1,0:T(4,128)(2,1)} async-done(((bf16[64,4,192]{2,1,0:T(4,128)(2,1)}), bf16[64,4,192]{2,1,0:T(4,128)(2,1)}, u32[]{:S(2)}, u32[]{:S(2)}) %all-to-all-start.3) | async-done | bytes 98336 | tf_op jit(solution)/shard_map/all_to_all | solution.py:84
  306.7 6.9 %collective-permute-start.1 = (bf16[192,192]{1,0:T(8,128)(2,1)}, bf16[192,192]{1,0:T(8,128)(2,1)}, u32[]{:S(2)}, u32[]{:S(2)}) collective-permute-start(bf16[192,192]{1,0:T(8,128)(2,1)} %get-tuple-element.33), channel_id=1, source_target_pairs={{256,0},{257,1},{258,2},{259,3},{260,4},{261,5},{262,6},{263,7},{2... | collective-permute-start | bytes 221192 | tf_op jit(solution)/shard_map/ppermute | solution.py:10
  318.8 5.4 %all-to-all-start.4 = ((bf16[64,4,384]{2,1,0:T(4,128)(2,1)}), bf16[64,4,384]{2,1,0:T(4,128)(2,1)}, u32[]{:S(2)}, u32[]{:S(2)}) async-start(bf16[64,4,384]{2,1,0:T(4,128)(2,1)} %reshape.193), calls=%async_computation.4 | async-start | bytes 393216 | tf_op jit(solution)/shard_map/all_to_all | solution.py:41
  324.3 3.1 fusion.56
  331.7 9.4 %all-to-all-done.4 = bf16[64,4,384]{2,1,0:T(4,128)(2,1)} async-done(((bf16[64,4,384]{2,1,0:T(4,128)(2,1)}), bf16[64,4,384]{2,1,0:T(4,128)(2,1)}, u32[]{:S(2)}, u32[]{:S(2)}) %all-to-all-start.4) | async-done | bytes 196640 | tf_op jit(solution)/shard_map/all_to_all | solution.py:41
  342.7 12.4 %all_gather.11 = bf16[256,2,768]{0,1,2:T(2,128)(2,1)S(1)} all-gather(bf16[256,2,192]{0,1,2:T(2,128)(2,1)S(1)} %copy.25), channel_id=1, replica_groups=mesh['segment'=2,'expert'=64,'pair'=4] {'pair'}, dimensions={2}, use_global_device_ids=true | all-gather | bytes 983040 | tf_op jit(solution)/shard_map/all_gather | solution.py:48
  355.1 2.2 fusion.146
  371.2 45.8 %all-reduce.8.cloned.1.call-done = bf16[256,768]{1,0:T(8,128)(2,1)} async-done(((bf16[256,768]{1,0:T(8,128)(2,1)}), bf16[256,768]{1,0:T(8,128)(2,1)}) %all-reduce.8.cloned.1.call-update) | async-done | bytes 393232 | tf_op jit(solution)/shard_map/psum | solution.py:76
  423.0 15.6 %all-to-all-start.5 = ((bf16[64,4,192]{2,1,0:T(4,128)(2,1)}), bf16[64,4,192]{2,1,0:T(4,128)(2,1)}, u32[]{:S(2)}, u32[]{:S(2)}) async-start(bf16[64,4,192]{2,1,0:T(4,128)(2,1)} %reshape.195), calls=%async_computation.5 | async-start | bytes 262144 | tf_op jit(solution)/shard_map/all_to_all | solution.py:84
  438.6 3.8 fusion.1
  442.5 10.0 %all-to-all-done.5 = bf16[64,4,192]{2,1,0:T(4,128)(2,1)} async-done(((bf16[64,4,192]{2,1,0:T(4,128)(2,1)}), bf16[64,4,192]{2,1,0:T(4,128)(2,1)}, u32[]{:S(2)}, u32[]{:S(2)}) %all-to-all-start.5) | async-done | bytes 98336 | tf_op jit(solution)/shard_map/all_to_all | solution.py:84
  (126 shorter events, 78.4 us)
Async XLA Ops:
  7.2 60.5 %copy-start = (bf16[1,1,768,768]{3,2,1,0:T(8,128)(2,1)S(1)}, bf16[1,1,768,768]{3,2,1,0:T(8,128)(2,1)}, u32[]{:S(2)}) copy-start(bf16[1,1,768,768]{3,2,1,0:T(8,128)(2,1)} %param.13) | copy-start | bytes 3538948
  7.2 115.2 %all-reduce.4.cloned.1.call-start = ((), (), s32[]{:S(2)}) async-start(), calls=%async_computation.6 | async-start | bytes 786432 | tf_op jit(solution)/shard_map/psum | solution.py:76
  11.1 1.3 copy-start.21
  62.5 4.6 copy-start.1
  123.5 33.2 %copy-start.11 = (bf16[2,192,192]{2,1,0:T(8,128)(2,1)S(1)}, bf16[2,192,192]{2,1,0:T(8,128)(2,1)}, u32[]{:S(2)}) copy-start(bf16[2,192,192]{2,1,0:T(8,128)(2,1)} %param.8) | copy-start | bytes 442372
  124.6 41.1 %copy-start.20 = (s32[1,1,192]{2,1,0:T(1,128)S(1)}, s32[1,1,192]{2,1,0:T(1,128)}, u32[]{:S(2)}) copy-start(s32[1,1,192]{2,1,0:T(1,128)} %get-tuple-element.26) | copy-start | bytes 2308
  126.6 29.3 %all-to-all-start.1 = ((bf16[64,4,192]{2,1,0:T(4,128)(2,1)}), bf16[64,4,192]{2,1,0:T(4,128)(2,1)S(1)}, u32[]{:S(2)}, u32[]{:S(2)}) async-start(bf16[64,4,192]{2,1,0:T(4,128)(2,1)} %reshape.187), calls=%async_computation.1 | async-start | bytes 262144 | tf_op jit(solution)/shard_map/all_to_all | solution.py:84
  142.0 125.9 %all-reduce.6.cloned.1.call-start = ((), (), s32[]{:S(2)}) async-start(), calls=%async_computation.7 | async-start | bytes 786432 | tf_op jit(solution)/shard_map/psum | solution.py:76
  157.9 10.7 %copy-start.9 = (bf16[2,192,192]{2,1,0:T(8,128)(2,1)}, bf16[2,192,192]{2,1,0:T(8,128)(2,1)S(1)}, u32[]{:S(2)}) copy-start(bf16[2,192,192]{2,1,0:T(8,128)(2,1)S(1)} %get-tuple-element.30) | copy-start | bytes 442372
  157.9 7.1 %collective-permute-start = (bf16[192,192]{1,0:T(8,128)(2,1)S(1)}, bf16[192,192]{1,0:T(8,128)(2,1)S(1)}, u32[]{:S(2)}, u32[]{:S(2)}) collective-permute-start(bf16[192,192]{1,0:T(8,128)(2,1)S(1)} %get-tuple-element.31), channel_id=1, source_target_pairs={{256,0},{257,1},{258,2},{259,3},{260,4},{261,5},{262,6},{263,7},{2... | collective-permute-start | bytes 221192 | tf_op jit(solution)/shard_map/ppermute | solution.py:10
  270.1 45.1 %copy-start.18 = (s32[1,1,192]{2,1,0:T(1,128)S(1)}, s32[1,1,192]{2,1,0:T(1,128)}, u32[]{:S(2)}) copy-start(s32[1,1,192]{2,1,0:T(1,128)} %get-tuple-element.24) | copy-start | bytes 2308
  273.7 29.4 %all-to-all-start.3 = ((bf16[64,4,192]{2,1,0:T(4,128)(2,1)}), bf16[64,4,192]{2,1,0:T(4,128)(2,1)}, u32[]{:S(2)}, u32[]{:S(2)}) async-start(bf16[64,4,192]{2,1,0:T(4,128)(2,1)} %reshape.191), calls=%async_computation.3 | async-start | bytes 262144 | tf_op jit(solution)/shard_map/all_to_all | solution.py:84
  306.7 7.5 %collective-permute-start.1 = (bf16[192,192]{1,0:T(8,128)(2,1)}, bf16[192,192]{1,0:T(8,128)(2,1)}, u32[]{:S(2)}, u32[]{:S(2)}) collective-permute-start(bf16[192,192]{1,0:T(8,128)(2,1)} %get-tuple-element.33), channel_id=1, source_target_pairs={{256,0},{257,1},{258,2},{259,3},{260,4},{261,5},{262,6},{263,7},{2... | collective-permute-start | bytes 221192 | tf_op jit(solution)/shard_map/ppermute | solution.py:10
  318.8 22.4 %all-to-all-start.4 = ((bf16[64,4,384]{2,1,0:T(4,128)(2,1)}), bf16[64,4,384]{2,1,0:T(4,128)(2,1)}, u32[]{:S(2)}, u32[]{:S(2)}) async-start(bf16[64,4,384]{2,1,0:T(4,128)(2,1)} %reshape.193), calls=%async_computation.4 | async-start | bytes 393216 | tf_op jit(solution)/shard_map/all_to_all | solution.py:41
  324.2 92.8 %all-reduce.8.cloned.1.call-start = ((), (), s32[]{:S(2)}) async-start(), calls=%async_computation.8 | async-start | bytes 786432 | tf_op jit(solution)/shard_map/psum | solution.py:76
  324.3 3.1 copy-start.5
  327.4 2.2 copy-start.6
  327.4 2.2 copy-start.7
  363.2 2.0 copy-start.8
  366.9 2.5 copy-start.2
  367.6 1.9 copy-start.13
  418.2 20.4 %copy-start.3 = (f32[768,768]{1,0:T(8,128)S(1)}, f32[768,768]{1,0:T(8,128)}, u32[]{:S(2)}) copy-start(f32[768,768]{1,0:T(8,128)} %fusion.54) | copy-start | bytes 7077892
  423.0 29.4 %all-to-all-start.5 = ((bf16[64,4,192]{2,1,0:T(4,128)(2,1)}), bf16[64,4,192]{2,1,0:T(4,128)(2,1)}, u32[]{:S(2)}, u32[]{:S(2)}) async-start(bf16[64,4,192]{2,1,0:T(4,128)(2,1)} %reshape.195), calls=%async_computation.5 | async-start | bytes 262144 | tf_op jit(solution)/shard_map/all_to_all | solution.py:84
  438.6 14.8 %copy-start.19 = (s32[1,1,192]{2,1,0:T(1,128)S(1)}, s32[1,1,192]{2,1,0:T(1,128)}, u32[]{:S(2)}) copy-start(s32[1,1,192]{2,1,0:T(1,128)} %get-tuple-element.24) | copy-start | bytes 2308
  (7 other events, 6.1 us)
Sparse Core Ops, SparseCore 0:
  70.3 51.9 all-reduce.3
  218.1 49.7 all-reduce.5
  367.0 49.9 all-reduce.7
where the time goes:
time: 465 us; the launch traced here: 462 us
  waiting for transfers between devices  195 us (42%)
  blocking collectives  94.3 us (20%)
  starting transfers between devices  65.3 us (14%)
  local copies, waits for them, and re-layouts  39 us (8%)
  matrix products  32.9 us (7%)
  other arithmetic  21.4 us (5%)
  between operations  14.3 us (3%)
    psum x3, waiting for transfers between devices, layer_pass(): lax.psum(partial_value.astype(jnp.bfloat16), 'pair').astype(jnp.float32)  146 us
    all_to_all x2, blocking collectives, layer_pass(): lax.all_to_all(packed.reshape(expert_count, capacity, 2 * feat_share), 'e...  57.9 us
    all_to_all x3, starting transfers between devices, layer_pass(): lax.all_to_all(branch.reshape(expert_count, capacity, feat_share), 'exper...  46.6 us
    all_to_all x3, waiting for transfers between devices, layer_pass(): lax.all_to_all(branch.reshape(expert_count, capacity, feat_share), 'exper...  37.7 us
    all_gather x3, blocking collectives, layer_pass(): lax.all_gather(arrived.reshape(slot_rows, 2, feat_share), 'pair', axis=2,...  36.3 us
    unnamed x51, local copies, waits for them, and re-layouts  15.5 us
    ppermute x2, starting transfers between devices, from_behind(): return lax.ppermute(x, axis, pairs)  13.1 us
    all_to_all x1, waiting for transfers between devices, layer_pass(): lax.all_to_all(packed.reshape(expert_count, capacity, 2 * feat_share), 'e...  9.45 us
  transfers between devices with their start and end apart: 9, of which 9 were waited for; matrix products, arithmetic and copies ran while one was open for 4% of the time, Pallas kernels for 0%

commit v1 on v0

v1 whole, which is shorter than its diff:
```python
import jax
import jax.numpy as jnp
from jax import lax
from jax.sharding import PartitionSpec as P

BF = jnp.bfloat16
F32 = jnp.float32
SWAP = [(0, 1), (1, 0)]


def gelu_both(u):
    s = jnp.tanh(0.7978845608 * (u + 0.044715 * u * u * u))
    value = 0.5 * u * (1.0 + s)
    slope = 0.5 * (1.0 + s) + 0.5 * u * (1.0 - s * s) * 0.7978845608 * (1.0 + 0.134145 * u * u)
    return value, slope


def dot(a, b, ca, cb):
    return lax.dot_general(a, b, (((ca,), (cb,)), ((), ())), preferred_element_type=F32)


def one_hot(owner, slot, rows, cap):
    target = owner * cap + slot
    return (lax.broadcasted_iota(jnp.int32, (rows, target.shape[0]), 0) == target[None, :]).astype(BF)


def expert_a2a(x):
    return lax.all_to_all(x, "expert", split_axis=0, concat_axis=0, tiled=True)


def pair_a2a(x):
    return lax.all_to_all(x, "pair", split_axis=0, concat_axis=0, tiled=True)


def spread(rows, pairs):
    return pair_a2a(jnp.broadcast_to(rows[None], (pairs,) + rows.shape))


def full_rows(x):
    return jnp.transpose(x, (1, 0, 2)).reshape(x.shape[1], -1)


def expert_pass(acts, grad, w_in, w_out, pairs):
    rows, width = acts.shape
    share = width // pairs
    af = acts.astype(F32)
    inv = lax.rsqrt(jnp.mean(af * af, axis=1) + 1e-06)
    normed = (af * inv[:, None]).astype(BF)
    pre = dot(normed, w_in, 1, 0)
    value, slope = gelu_both(pre)
    hidden = value.astype(BF)
    back = (dot(grad, w_out, 1, 1) * slope).astype(BF)
    part = dot(back, w_in, 1, 1)
    inner = jnp.sum(part * af, axis=1)
    high = inner.astype(BF)
    low = (inner - high.astype(F32)).astype(BF)
    extra = jnp.stack([high, low], axis=1)
    parts = jnp.transpose(part.astype(BF).reshape(rows, pairs, share), (1, 0, 2))
    parts = jnp.concatenate([parts, jnp.broadcast_to(extra[None], (pairs, rows, 2))], axis=2)
    got = pair_a2a(parts)
    total = jnp.sum(got.astype(F32), axis=0)
    mine = total[:, :share]
    inner = total[:, share] + total[:, share + 1]
    own = lax.dynamic_slice_in_dim(af, lax.axis_index("pair") * share, share, 1)
    branch = (inv[:, None] * mine - (inv**3 * inner / width)[:, None] * own).astype(BF)
    return branch, normed, back, hidden


def body(acts, cotangent, gates, owners, slots, w_in, w_out):
    core = lax.axis_index("segment")
    experts = lax.axis_size("expert")
    pairs = lax.axis_size("pair")
    tok, share = acts.shape[2:]
    cap = max(2, (5 * tok + 4 * experts - 1) // (4 * experts))
    rows = experts * cap
    acts = lax.dynamic_index_in_dim(acts, core, 1, False)
    cot = lax.dynamic_index_in_dim(cotangent, core, 0, False)
    gates = lax.dynamic_index_in_dim(gates, core, 1, False)
    owners = lax.dynamic_index_in_dim(owners, core, 1, False)
    slots = lax.dynamic_index_in_dim(slots, core, 1, False)
    own_in, own_out = w_in[0, 0], w_out[0, 0]
    other_in = lax.ppermute(own_in, "segment", SWAP)
    other_out = lax.ppermute(own_out, "segment", SWAP)
    top = core == 1
    in1 = jnp.where(top, own_in, other_in)
    in0 = jnp.where(top, other_in, own_in)
    out1 = jnp.where(top, own_out, other_out)
    out0 = jnp.where(top, other_out, own_out)

    place1 = one_hot(owners[1], slots[1], rows, cap)
    place0 = one_hot(owners[0], slots[0], rows, cap)
    scaled1 = (gates[1][:, None] * cot.astype(F32)).astype(BF)
    packed1 = dot(place1, jnp.concatenate([acts[1], scaled1], axis=1), 1, 0).astype(BF)
    packed0 = dot(place0, acts[0], 1, 0).astype(BF)
    first = jnp.concatenate([packed1, packed0], axis=1)
    got = expert_a2a(first.reshape(experts, cap, 3 * share)).reshape(rows, 3 * share)
    got = spread(got, pairs)
    rows1 = full_rows(got[:, :, :share])
    grad1 = full_rows(got[:, :, share : 2 * share])
    rows0 = full_rows(got[:, :, 2 * share :])

    branch1, normed1, back1, hidden1 = expert_pass(rows1, grad1, in1, out1, pairs)
    home = expert_a2a(branch1.reshape(experts, cap, share)).reshape(rows, share)
    res1 = (cot.astype(F32) + dot(place1, home, 0, 0)).astype(BF)

    scaled0 = (gates[0][:, None] * res1.astype(F32)).astype(BF)
    packed = dot(place0, scaled0, 1, 0).astype(BF)
    got = expert_a2a(packed.reshape(experts, cap, share)).reshape(rows, share)
    grad0 = full_rows(spread(got, pairs))
    branch0, normed0, back0, hidden0 = expert_pass(rows0, grad0, in0, out0, pairs)
    home = expert_a2a(branch0.reshape(experts, cap, share)).reshape(rows, share)
    res0 = (res1.astype(F32) + dot(place0, home, 0, 0)).astype(BF)

    first1, second1 = dot(normed1, back1, 0, 0), dot(hidden1, grad1, 0, 0)
    first0, second0 = dot(normed0, back0, 0, 0), dot(hidden0, grad0, 0, 0)
    keep_first, give_first = jnp.where(top, first1, first0), jnp.where(top, first0, first1)
    keep_second, give_second = jnp.where(top, second1, second0), jnp.where(top, second0, second1)
    got_first = lax.ppermute(give_first.astype(BF), "segment", SWAP)
    got_second = lax.ppermute(give_second.astype(BF), "segment", SWAP)
    grad_in = (keep_first + got_first.astype(F32)).astype(BF)
    grad_out = (keep_second + got_second.astype(F32)).astype(BF)

    keep, give = jnp.where(top, res1, res0), jnp.where(top, res0, res1)
    came = lax.ppermute(give, "segment", SWAP)
    grads = jnp.stack([jnp.where(top, came, keep), jnp.where(top, keep, came)])
    return grads[None], grad_in[None, None], grad_out[None, None]


def solution(mesh):
    placed = (
        P(None, None, "expert", "pair"),
        P(None, "expert", "pair"),
        P(None, None, "expert"),
        P(None, None, "expert"),
        P(None, None, "expert"),
        P("segment", "expert", None, "pair"),
        P("segment", "expert", "pair", None),
    )
    return jax.shard_map(
        body,
        mesh=mesh,
        in_specs=placed,
        out_specs=(
            P("segment", None, "expert", "pair"),
            P("segment", "expert", None, "pair"),
            P("segment", "expert", "pair", None),
        ),
        check_vma=False,
    )
```

time: 465 us -> 226 us (0.49)
  waiting for transfers between devices: 195 us -> 46.9 us
  blocking collectives: 94.3 us -> 40.9 us
  local copies, waits for them, and re-layouts: 39 us -> 24.1 us
  between operations: 14.3 us -> 1.07 us
  matrix products: 32.9 us -> 25.8 us
    psum x3 -> x0, waiting for transfers between devices: 146 us -> none  [layer_pass(): lax.psum(partial_value.astype(jnp.bfloat16), 'pair').astype(jnp.float32)]
    all_gather x3 -> x0, blocking collectives: 36.3 us -> none  [layer_pass(): lax.all_gather(arrived.reshape(slot_rows, 2, feat_share), 'pair', axis=2,...]
    all_to_all x2 -> x1, blocking collectives: 57.9 us -> 40.9 us  [expert_a2a(): return lax.all_to_all(x, 'expert', split_axis=0, concat_axis=0, tiled=True)]
    all_to_all x4 -> x7, starting transfers between devices: 52.1 us -> 38 us  [the longest x3 21 us: expert_a2a(): return lax.all_to_all(x, 'expert', split_axis=0, concat_axis=0, tiled=True)]
    unnamed x51 -> x30, local copies, waits for them, and re-layouts: 15.5 us -> 2.14 us
    ppermute x2 -> x5, starting transfers between devices: 13.1 us -> 25.7 us  [the longest x1 10.3 us: body(): got_first = lax.ppermute(give_first.astype(BF), 'segment', SWAP)]
    convert_element_type x0 -> x8, local copies, waits for them, and re-layouts: none -> 11.7 us  [the longest x2 3.84 us: expert_pass(): part.astype(BF).reshape(rows, pairs, share)]
    convert_element_type x15 -> x8, other arithmetic: 15.9 us -> 6.81 us  [the longest x1 2.4 us: expert_pass(): af = acts.astype(F32)]
  transfers between devices with their start and end apart: 9 -> 12, of which waited for: 9 -> 7; matrix products, arithmetic and copies ran while one was open for 4% -> 14% of each run, Pallas kernels for 0% -> 0%
where the time goes in v1:
time: 226 us; the launch traced here: 225 us
  starting transfers between devices  63.7 us (28%)
  waiting for transfers between devices  46.9 us (21%)
  blocking collectives  40.9 us (18%)
  matrix products  25.8 us (11%)
  local copies, waits for them, and re-layouts  24.1 us (11%)
  other arithmetic  22.3 us (10%)
    all_to_all x1, blocking collectives, expert_a2a(): return lax.all_to_all(x, 'expert', split_axis=0, concat_axis=0, tiled=True)  40.9 us
    all_to_all x3, waiting for transfers between devices, expert_a2a(): return lax.all_to_all(x, 'expert', split_axis=0, concat_axis=0, tiled=True)  28.4 us
    dot_general x15, matrix products, dot(): lax.dot_general(a, b, (((ca,), (cb,)), ((), ())), preferred_element_type=...  25.8 us
    all_to_all x3, starting transfers between devices, expert_a2a(): return lax.all_to_all(x, 'expert', split_axis=0, concat_axis=0, tiled=True)  21 us
    all_to_all x4, waiting for transfers between devices, pair_a2a(): return lax.all_to_all(x, 'pair', split_axis=0, concat_axis=0, tiled=True)  17.5 us
    all_to_all x4, starting transfers between devices, pair_a2a(): return lax.all_to_all(x, 'pair', split_axis=0, concat_axis=0, tiled=True)  16.9 us
    ppermute x1, starting transfers between devices, body(): got_first = lax.ppermute(give_first.astype(BF), 'segment', SWAP)  10.3 us
    broadcast_in_dim x3, other arithmetic, body(): return (grads[None], grad_in[None, None], grad_out[None, None])  6.97 us
  transfers between devices with their start and end apart: 12, of which 7 were waited for; matrix products, arithmetic and copies ran while one was open for 14% of the time, Pallas kernels for 0%

profile of v1, /device:TPU:1, one launch (start us, length us, event | category | flops | bytes accessed | tf_op | source)
XLA Modules:
  0.0 224.8 jit_solution(16408815957943384718)
XLA Ops:
  5.5 40.9 %all_to_all.40 = bf16[64,4,576]{2,1,0:T(4,128)(2,1)S(1)} all-to-all(bf16[64,4,576]{2,1,0:T(4,128)(2,1)S(1)} %reshape.184), channel_id=1, replica_groups=mesh['segment'=2,'expert'=64,'pair'=4] {'expert'}, dimensions={0} | all-to-all | bytes 589824 | tf_op jit(solution)/shard_map/all_to_all | solution.py:28
  47.8 4.4 %all-to-all-start.1 = ((bf16[4,256,576]{1,2,0:T(8,128)(2,1)}), bf16[4,256,576]{1,2,0:T(8,128)(2,1)}, u32[]{:S(2)}, u32[]{:S(2)}) async-start(bf16[4,256,576]{1,2,0:T(8,128)(2,1)} %broadcast_in_dim.19), calls=%async_computation.1 | async-start | bytes 2359296 | tf_op jit(solution)/shard_map/all_to_all | solution.py:32
  52.2 4.7 %collective-permute-start.1 = (bf16[768,768]{1,0:T(8,128)(2,1)S(1)}, bf16[768,768]{1,0:T(8,128)(2,1)S(1)}, u32[]{:S(2)}, u32[]{:S(2)}) collective-permute-start(bf16[768,768]{1,0:T(8,128)(2,1)S(1)} %bitcast.87), channel_id=1, source_target_pairs={{0,256},{256,0},{1,257},{257,1},{2,258},{258,2},{3,259},{259,3},{4... | collective-permute-start | bytes 3538952 | tf_op jit(solution)/shard_map/ppermute | solution.py:82
  58.9 6.8 %all-to-all-done.1 = bf16[4,256,576]{1,2,0:T(8,128)(2,1)} async-done(((bf16[4,256,576]{1,2,0:T(8,128)(2,1)}), bf16[4,256,576]{1,2,0:T(8,128)(2,1)}, u32[]{:S(2)}, u32[]{:S(2)}) %all-to-all-start.1) | async-done | bytes 1179680 | tf_op jit(solution)/shard_map/all_to_all | solution.py:32
  82.1 4.1 %all-to-all-start.2 = ((bf16[4,256,194]{1,2,0:T(8,128)(2,1)}), bf16[4,256,194]{1,2,0:T(8,128)(2,1)}, u32[]{:S(2)}, u32[]{:S(2)}) async-start(bf16[4,256,194]{1,2,0:T(8,128)(2,1)} %pad_maximum_fusion), calls=%async_computation.2 | async-start | bytes 819200 | tf_op jit(solution)/shard_map/all_to_all | solution.py:32
  86.2 6.4 %all-to-all-done.2 = bf16[4,256,194]{1,2,0:T(8,128)(2,1)} async-done(((bf16[4,256,194]{1,2,0:T(8,128)(2,1)}), bf16[4,256,194]{1,2,0:T(8,128)(2,1)}, u32[]{:S(2)}, u32[]{:S(2)}) %all-to-all-start.2) | async-done | bytes 397344 | tf_op jit(solution)/shard_map/all_to_all | solution.py:32
  98.6 10.1 %all-to-all-start.3 = ((bf16[64,4,192]{2,1,0:T(4,128)(2,1)}), bf16[64,4,192]{2,1,0:T(4,128)(2,1)}, u32[]{:S(2)}, u32[]{:S(2)}) async-start(bf16[64,4,192]{2,1,0:T(4,128)(2,1)} %reshape.187), calls=%async_computation.3 | async-start | bytes 262144 | tf_op jit(solution)/shard_map/all_to_all | solution.py:28
  108.7 3.1 %fusion.40 = f32[768,768]{1,0:T(8,128)} fusion(bf16[256,768]{1,0:T(8,128)(2,1)} %copy-done.10, f32[256,768]{0,1:T(8,128)} %bitcast.95, f32[256]{0:T(256)S(1)} %add_rsqrt_fusion.1), kind=kOutput, calls=%fused_computation.79 | convolution fusion | flops 302383104 | bytes 3539968 | tf_op jit(solution)/shard_map/dot_general | solution.py:19
  111.8 10.6 %all-to-all-done.3 = bf16[64,4,192]{2,1,0:T(4,128)(2,1)} async-done(((bf16[64,4,192]{2,1,0:T(4,128)(2,1)}), bf16[64,4,192]{2,1,0:T(4,128)(2,1)}, u32[]{:S(2)}, u32[]{:S(2)}) %all-to-all-start.3) | async-done | bytes 98336 | tf_op jit(solution)/shard_map/all_to_all | solution.py:28
  130.8 5.7 %all-to-all-start.4 = ((bf16[64,4,192]{2,1,0:T(4,128)(2,1)}), bf16[64,4,192]{2,1,0:T(4,128)(2,1)}, u32[]{:S(2)}, u32[]{:S(2)}) async-start(bf16[64,4,192]{2,1,0:T(4,128)(2,1)} %reshape.189), calls=%async_computation.4 | async-start | bytes 262144 | tf_op jit(solution)/shard_map/all_to_all | solution.py:28
  139.1 11.2 %all-to-all-done.4 = bf16[64,4,192]{2,1,0:T(4,128)(2,1)} async-done(((bf16[64,4,192]{2,1,0:T(4,128)(2,1)}), bf16[64,4,192]{2,1,0:T(4,128)(2,1)}, u32[]{:S(2)}, u32[]{:S(2)}) %all-to-all-start.4) | async-done | bytes 98336 | tf_op jit(solution)/shard_map/all_to_all | solution.py:28
  152.3 4.1 %all-to-all-start.5 = ((bf16[4,256,192]{1,2,0:T(8,128)(2,1)}), bf16[4,256,192]{1,2,0:T(8,128)(2,1)}, u32[]{:S(2)}, u32[]{:S(2)}) async-start(bf16[4,256,192]{1,2,0:T(8,128)(2,1)} %broadcast_in_dim.22), calls=%async_computation.5 | async-start | bytes 786432 | tf_op jit(solution)/shard_map/all_to_all | solution.py:32
  158.3 4.4 %all-to-all-done.5 = bf16[4,256,192]{1,2,0:T(8,128)(2,1)} async-done(((bf16[4,256,192]{1,2,0:T(8,128)(2,1)}), bf16[4,256,192]{1,2,0:T(8,128)(2,1)}, u32[]{:S(2)}, u32[]{:S(2)}) %all-to-all-start.5) | async-done | bytes 393248 | tf_op jit(solution)/shard_map/all_to_all | solution.py:32
  162.7 3.0 %fusion.1 = bf16[256,768]{1,0:T(8,128)(2,1)S(1)} fusion(bf16[256,768]{0,1:T(8,128)(2,1)} %bitcast.21, bf16[768,768]{1,0:T(8,128)(2,1)} %collective-permute-done, pred[]{:T(512)S(6)} %eq.19, f32[256,768]{1,0:T(8,128)} %fusion.23, bf16[1,1,768,768]{3,2,1,0:T(8,128)(2,1)} %param.13), kind=kOutput, calls=%fused_computation.7 | convolution fusion | flops 306315264 | bytes 3932161 | tf_op jit(solution)/shard_map/dot_general | solution.py:19
  170.8 4.3 %all-to-all-start.6 = ((bf16[4,256,194]{1,2,0:T(8,128)(2,1)}), bf16[4,256,194]{1,2,0:T(8,128)(2,1)}, u32[]{:S(2)}, u32[]{:S(2)}) async-start(bf16[4,256,194]{1,2,0:T(8,128)(2,1)} %pad_maximum_fusion.1), calls=%async_computation.6 | async-start | bytes 819200 | tf_op jit(solution)/shard_map/all_to_all | solution.py:32
  175.1 3.3 %select_convert_fusion.1 = (bf16[768,768]{1,0:T(8,128)(2,1)}, f32[768,768]{1,0:T(8,128)}) fusion(f32[768,768]{1,0:T(8,128)} %fusion.40, pred[]{:T(512)S(6)} %eq.19, bf16[256,768]{1,0:T(8,128)(2,1)} %copy-done.11, f32[256,768]{0,1:T(8,128)S(1)} %bitcast.90, f32[256]{0:T(256)S(1)} %add_rsqrt_fusion), kind=kOutput, calls=%fused_computation.3 | convolution fusion | flops 302972928 | bytes 7078913 | tf_op jit(solution)/shard_map/dot_general | solution.py:19
  178.3 10.3 %collective-permute-start.3 = (bf16[768,768]{1,0:T(8,128)(2,1)}, bf16[768,768]{1,0:T(8,128)(2,1)}, u32[]{:S(2)}, u32[]{:S(2)}) collective-permute-start(bf16[768,768]{1,0:T(8,128)(2,1)} %get-tuple-element.20), channel_id=1, source_target_pairs={{0,256},{256,0},{1,257},{257,1},{2,258},{258,2},{3,259},{259,3},{4... | collective-permute-start | bytes 3538952 | tf_op jit(solution)/shard_map/ppermute | solution.py:118
  192.1 5.2 %all-to-all-start.7 = ((bf16[64,4,192]{2,1,0:T(4,128)(2,1)}), bf16[64,4,192]{2,1,0:T(4,128)(2,1)S(1)}, u32[]{:S(2)}, u32[]{:S(2)}) async-start(bf16[64,4,192]{2,1,0:T(4,128)(2,1)} %reshape.192), calls=%async_computation.7 | async-start | bytes 262144 | tf_op jit(solution)/shard_map/all_to_all | solution.py:28
  197.3 3.8 %select_convert_fusion = (bf16[768,768]{1,0:T(8,128)(2,1)}, f32[768,768]{1,0:T(8,128)}) fusion(f32[768,768]{1,0:T(8,128)S(1)} %fusion.24, pred[]{:T(512)S(6)} %eq.19, bf16[256,768]{0,1:T(8,128)(2,1)} %bitcast.21, f32[256,768]{1,0:T(8,128)} %fusion.23), kind=kOutput, calls=%fused_computation.1 | convolution fusion | flops 304349184 | bytes 7077889 | tf_op jit(solution)/shard_map/dot_general | solution.py:19
  201.2 3.5 %collective-permute-start.4 = (bf16[768,768]{1,0:T(8,128)(2,1)}, bf16[768,768]{1,0:T(8,128)(2,1)}, u32[]{:S(2)}, u32[]{:S(2)}) collective-permute-start(bf16[768,768]{1,0:T(8,128)(2,1)} %get-tuple-element.22), channel_id=1, source_target_pairs={{0,256},{256,0},{1,257},{257,1},{2,258},{258,2},{3,259},{259,3},{4... | collective-permute-start | bytes 3538952 | tf_op jit(solution)/shard_map/ppermute | solution.py:119
  204.7 6.6 %all-to-all-done.7 = bf16[64,4,192]{2,1,0:T(4,128)(2,1)S(1)} async-done(((bf16[64,4,192]{2,1,0:T(4,128)(2,1)}), bf16[64,4,192]{2,1,0:T(4,128)(2,1)S(1)}, u32[]{:S(2)}, u32[]{:S(2)}) %all-to-all-start.7) | async-done | bytes 98336 | tf_op jit(solution)/shard_map/all_to_all | solution.py:28
  211.6 5.3 %collective-permute-start.2 = (bf16[192,192]{1,0:T(8,128)(2,1)S(1)}, bf16[192,192]{1,0:T(8,128)(2,1)S(1)}, u32[]{:S(2)}, u32[]{:S(2)}) collective-permute-start(bf16[192,192]{1,0:T(8,128)(2,1)S(1)} %get-tuple-element.18), channel_id=1, source_target_pairs={{0,256},{256,0},{1,257},{257,1},{2,258},{258,2},{3,259},{259,3},{4... | collective-permute-start | bytes 221192 | tf_op jit(solution)/shard_map/ppermute | solution.py:124
  218.6 3.6 %fusion.2 = bf16[1,1,768,768]{3,2,1,0:T(8,128)(2,1)} fusion(bf16[768,768]{1,0:T(8,128)(2,1)} %collective-permute-done.3, f32[768,768]{1,0:T(8,128)} %fusion.40, f32[768,768]{1,0:T(8,128)} %get-tuple-element.21, pred[]{:T(512)S(6)} %eq.19), kind=kLoop, calls=%fused_computation.12 | loop fusion | flops 2359296 | bytes 7077889 | tf_op jit(solution)/shard_map/broadcast_in_dim | solution.py:126
  222.2 2.7 %fusion.3 = bf16[1,1,768,768]{3,2,1,0:T(8,128)(2,1)} fusion(bf16[768,768]{1,0:T(8,128)(2,1)} %collective-permute-done.4, f32[768,768]{1,0:T(8,128)S(1)} %fusion.24, f32[768,768]{1,0:T(8,128)S(1)} %copy-done.5, pred[]{:T(512)S(6)} %eq.19), kind=kLoop, calls=%fused_computation.13 | loop fusion | flops 2359296 | bytes 7077889 | tf_op jit(solution)/shard_map/broadcast_in_dim | solution.py:126
  (95 shorter events, 55.7 us)
Async XLA Ops:
  47.8 4.4 %copy-start.1 = (bf16[1,1,768,768]{3,2,1,0:T(8,128)(2,1)S(1)}, bf16[1,1,768,768]{3,2,1,0:T(8,128)(2,1)}, u32[]{:S(2)}) copy-start(bf16[1,1,768,768]{3,2,1,0:T(8,128)(2,1)} %param.12) | copy-start | bytes 3538948
  47.8 17.8 %all-to-all-start.1 = ((bf16[4,256,576]{1,2,0:T(8,128)(2,1)}), bf16[4,256,576]{1,2,0:T(8,128)(2,1)}, u32[]{:S(2)}, u32[]{:S(2)}) async-start(bf16[4,256,576]{1,2,0:T(8,128)(2,1)} %broadcast_in_dim.19), calls=%async_computation.1 | async-start | bytes 2359296 | tf_op jit(solution)/shard_map/all_to_all | solution.py:32
  52.2 19.4 %collective-permute-start.1 = (bf16[768,768]{1,0:T(8,128)(2,1)S(1)}, bf16[768,768]{1,0:T(8,128)(2,1)S(1)}, u32[]{:S(2)}, u32[]{:S(2)}) collective-permute-start(bf16[768,768]{1,0:T(8,128)(2,1)S(1)} %bitcast.87), channel_id=1, source_target_pairs={{0,256},{256,0},{1,257},{257,1},{2,258},{258,2},{3,259},{259,3},{4... | collective-permute-start | bytes 3538952 | tf_op jit(solution)/shard_map/ppermute | solution.py:82
  57.0 16.9 %collective-permute-start = (bf16[768,768]{1,0:T(8,128)(2,1)}, bf16[768,768]{1,0:T(8,128)(2,1)}, u32[]{:S(2)}, u32[]{:S(2)}) collective-permute-start(bf16[768,768]{1,0:T(8,128)(2,1)} %bitcast.115), channel_id=1, source_target_pairs={{0,256},{256,0},{1,257},{257,1},{2,258},{258,2},{3,259},{259,3},{4... | collective-permute-start | bytes 3538952 | tf_op jit(solution)/shard_map/ppermute | solution.py:83
  71.6 2.2 copy-start.9
  71.7 2.2 copy-start.14
  71.7 66.1 %copy-start.3 = (bf16[768,768]{1,0:T(8,128)(2,1)}, bf16[768,768]{1,0:T(8,128)(2,1)S(1)}, u32[]{:S(2)}) copy-start(bf16[768,768]{1,0:T(8,128)(2,1)S(1)} %collective-permute-done.1) | copy-start | bytes 3538948
  73.9 1.4 copy-start.8
  75.3 1.3 copy-start.10
  82.1 10.5 %all-to-all-start.2 = ((bf16[4,256,194]{1,2,0:T(8,128)(2,1)}), bf16[4,256,194]{1,2,0:T(8,128)(2,1)}, u32[]{:S(2)}, u32[]{:S(2)}) async-start(bf16[4,256,194]{1,2,0:T(8,128)(2,1)} %pad_maximum_fusion), calls=%async_computation.2 | async-start | bytes 819200 | tf_op jit(solution)/shard_map/all_to_all | solution.py:32
  98.6 23.9 %all-to-all-start.3 = ((bf16[64,4,192]{2,1,0:T(4,128)(2,1)}), bf16[64,4,192]{2,1,0:T(4,128)(2,1)}, u32[]{:S(2)}, u32[]{:S(2)}) async-start(bf16[64,4,192]{2,1,0:T(4,128)(2,1)} %reshape.187), calls=%async_computation.3 | async-start | bytes 262144 | tf_op jit(solution)/shard_map/all_to_all | solution.py:28
  130.8 19.6 %all-to-all-start.4 = ((bf16[64,4,192]{2,1,0:T(4,128)(2,1)}), bf16[64,4,192]{2,1,0:T(4,128)(2,1)}, u32[]{:S(2)}, u32[]{:S(2)}) async-start(bf16[64,4,192]{2,1,0:T(4,128)(2,1)} %reshape.189), calls=%async_computation.4 | async-start | bytes 262144 | tf_op jit(solution)/shard_map/all_to_all | solution.py:28
  152.3 10.4 %all-to-all-start.5 = ((bf16[4,256,192]{1,2,0:T(8,128)(2,1)}), bf16[4,256,192]{1,2,0:T(8,128)(2,1)}, u32[]{:S(2)}, u32[]{:S(2)}) async-start(bf16[4,256,192]{1,2,0:T(8,128)(2,1)} %broadcast_in_dim.22), calls=%async_computation.5 | async-start | bytes 786432 | tf_op jit(solution)/shard_map/all_to_all | solution.py:32
  162.7 3.0 %copy-start.2 = (bf16[1,1,768,768]{3,2,1,0:T(8,128)(2,1)S(1)}, bf16[1,1,768,768]{3,2,1,0:T(8,128)(2,1)}, u32[]{:S(2)}) copy-start(bf16[1,1,768,768]{3,2,1,0:T(8,128)(2,1)} %param.12) | copy-start | bytes 3538948
  162.7 3.0 %copy-start.4 = (bf16[768,768]{1,0:T(8,128)(2,1)S(1)}, bf16[768,768]{1,0:T(8,128)(2,1)}, u32[]{:S(2)}) copy-start(bf16[768,768]{1,0:T(8,128)(2,1)} %copy-done.3) | copy-start | bytes 3538948
  162.7 3.0 %copy-start.7 = (f32[256,768]{1,0:T(8,128)S(1)}, f32[256,768]{1,0:T(8,128)}, u32[]{:S(2)}) copy-start(f32[256,768]{1,0:T(8,128)} %copy.30) | copy-start | bytes 2359300
  165.7 1.3 copy-start.11
  170.8 17.8 %all-to-all-start.6 = ((bf16[4,256,194]{1,2,0:T(8,128)(2,1)}), bf16[4,256,194]{1,2,0:T(8,128)(2,1)}, u32[]{:S(2)}, u32[]{:S(2)}) async-start(bf16[4,256,194]{1,2,0:T(8,128)(2,1)} %pad_maximum_fusion.1), calls=%async_computation.6 | async-start | bytes 819200 | tf_op jit(solution)/shard_map/all_to_all | solution.py:32
  178.3 40.2 %collective-permute-start.3 = (bf16[768,768]{1,0:T(8,128)(2,1)}, bf16[768,768]{1,0:T(8,128)(2,1)}, u32[]{:S(2)}, u32[]{:S(2)}) collective-permute-start(bf16[768,768]{1,0:T(8,128)(2,1)} %get-tuple-element.20), channel_id=1, source_target_pairs={{0,256},{256,0},{1,257},{257,1},{2,258},{258,2},{3,259},{259,3},{4... | collective-permute-start | bytes 3538952 | tf_op jit(solution)/shard_map/ppermute | solution.py:118
  192.1 19.2 %all-to-all-start.7 = ((bf16[64,4,192]{2,1,0:T(4,128)(2,1)}), bf16[64,4,192]{2,1,0:T(4,128)(2,1)S(1)}, u32[]{:S(2)}, u32[]{:S(2)}) async-start(bf16[64,4,192]{2,1,0:T(4,128)(2,1)} %reshape.192), calls=%async_computation.7 | async-start | bytes 262144 | tf_op jit(solution)/shard_map/all_to_all | solution.py:28
  197.3 14.0 %copy-start.13 = (bf16[192,192]{1,0:T(8,128)(2,1)S(1)}, bf16[192,192]{1,0:T(8,128)(2,1)}, u32[]{:S(2)}) copy-start(bf16[192,192]{1,0:T(8,128)(2,1)} %copy-done.12) | copy-start | bytes 221188
  201.2 21.0 %collective-permute-start.4 = (bf16[768,768]{1,0:T(8,128)(2,1)}, bf16[768,768]{1,0:T(8,128)(2,1)}, u32[]{:S(2)}, u32[]{:S(2)}) collective-permute-start(bf16[768,768]{1,0:T(8,128)(2,1)} %get-tuple-element.22), channel_id=1, source_target_pairs={{0,256},{256,0},{1,257},{257,1},{2,258},{258,2},{3,259},{259,3},{4... | collective-permute-start | bytes 3538952 | tf_op jit(solution)/shard_map/ppermute | solution.py:119
  211.6 6.2 %collective-permute-start.2 = (bf16[192,192]{1,0:T(8,128)(2,1)S(1)}, bf16[192,192]{1,0:T(8,128)(2,1)S(1)}, u32[]{:S(2)}, u32[]{:S(2)}) collective-permute-start(bf16[192,192]{1,0:T(8,128)(2,1)S(1)} %get-tuple-element.18), channel_id=1, source_target_pairs={{0,256},{256,0},{1,257},{257,1},{2,258},{258,2},{3,259},{259,3},{4... | collective-permute-start | bytes 221192 | tf_op jit(solution)/shard_map/ppermute | solution.py:124
  218.6 3.6 %copy-start.5 = (f32[768,768]{1,0:T(8,128)S(1)}, f32[768,768]{1,0:T(8,128)}, u32[]{:S(2)}) copy-start(f32[768,768]{1,0:T(8,128)} %get-tuple-element.23) | copy-start | bytes 7077892
  (3 other events, 2.6 us)

commit v2 on v1

v2 whole, which is shorter than its diff:
```python
import functools

import jax
import jax.numpy as jnp
from jax import lax
from jax.experimental import pallas as pl
from jax.experimental.pallas import tpu as pltpu
from jax.sharding import Mesh, PartitionSpec as P

BF = jnp.bfloat16
F32 = jnp.float32
I32 = jnp.int32
SWAP = [(0, 1), (1, 0)]

NY, NZ, NX = 4, 16, 4
CAP = 4
TOK = 192
SHARE = 192
WIDTH = SHARE * NX
HID = 768
LOW = 128
ZROWS = NY * CAP + NY * CAP // 2
YROWS = NZ * CAP + NZ * CAP // 2
ALL = NZ * ZROWS


def dot(a, b, ca=1, cb=0):
    return lax.dot_general(a, b, (((ca,), (cb,)), ((), ())), preferred_element_type=F32)


def hot(cond):
    return jnp.where(cond, 1.0, 0.0).astype(BF)


def iota(shape, dim):
    return lax.broadcasted_iota(I32, shape, dim)


def column(row):
    n = row.shape[1]
    eye = iota((n, n), 0) == iota((n, n), 1)
    return jnp.sum(jnp.where(eye, row.astype(F32), 0.0), axis=1, keepdims=True)


def targets(owner, slot):
    base = (owner & (NZ - 1)) * ZROWS
    y = owner >> 4
    return base + y * CAP + slot, base + NY * CAP + y * 2 + (slot >> 1), slot & 1


def pack(values, owner, slot):
    low_at, high_at, odd = targets(owner, slot)
    at = iota((ALL, TOK), 0)
    low = hot(at == low_at)
    even_hot = hot((at == high_at) & (odd == 0))
    odd_hot = hot((at == high_at) & (odd == 1))
    out = []
    for v in values:
        high = v[:, LOW:]
        none = jnp.zeros_like(high)
        out.append(
            dot(low, v[:, :LOW])
            + dot(even_hot, jnp.concatenate([high, none], axis=1))
            + dot(odd_hot, jnp.concatenate([none, high], axis=1))
        )
    return out


def unpack(rows, owner, slot):
    low_at, high_at, odd = (column(t).astype(I32) for t in targets(owner, slot))
    at = iota((TOK, ALL), 1)
    low = dot(hot(at == low_at), rows)
    even_rows = dot(hot((at == high_at) & (odd == 0)), rows)
    odd_rows = dot(hot((at == high_at) & (odd == 1)), rows)
    high = even_rows[:, : SHARE - LOW] + odd_rows[:, SHARE - LOW :]
    return jnp.concatenate([low, high], axis=1)


def row_of(ref, layer, core):
    return jnp.where(core == 0, ref[layer, 0:1, :], ref[layer, 1:2, :])


def start_kernel(core_ref, acts, cot, gates, owners, slots, out, tok, gate_v, owner_v, slot_v, sems):
    core = core_ref[0]
    copies = [
        pltpu.make_async_copy(src, dst, sems.at[k])
        for k, (src, dst) in enumerate(
            [
                (owners, owner_v),
                (slots, slot_v),
                (gates, gate_v),
                (cot.at[core], tok.at[0]),
                (acts.at[1, core], tok.at[1]),
                (acts.at[0, core], tok.at[2]),
            ]
        )
    ]
    for copy in copies:
        copy.start()
    for copy in copies:
        copy.wait()
    gate = column(row_of(gate_v, 1, core))
    scaled = (gate * tok[0].astype(F32)).astype(BF)
    first = pack([tok[1], scaled], row_of(owner_v, 1, core), row_of(slot_v, 1, core))
    second = pack([tok[2]], row_of(owner_v, 0, core), row_of(slot_v, 0, core))
    parts = [p.reshape(NZ, ZROWS, LOW) for p in first + second]
    out[...] = jnp.concatenate(parts, axis=1).reshape(3 * ALL, LOW).astype(BF)


def spread_kernel(count, rows, out):
    shape = (NY, YROWS, ALL)
    y, k, at = iota(shape, 0), iota(shape, 1), iota(shape, 2)
    z = (k & 31) >> 1
    half = k & 1
    low = z * ZROWS + y * CAP + half * 2 + (k >> 5)
    high = z * ZROWS + NY * CAP + y * 2 + half
    move = hot((at == jnp.where(k < NZ * CAP, low, high)).reshape(ALL, ALL))
    value = rows[...].astype(F32).reshape(NZ, count * ZROWS, LOW)
    for a in range(count):
        part = value[:, a * ZROWS : (a + 1) * ZROWS].reshape(ALL, LOW).astype(BF)
        moved = dot(move, part).astype(BF)
        for j in range(NY):
            for i in range(NX):
                out[j * NX + i, a * YROWS : (a + 1) * YROWS, :] = moved[j * YROWS : (j + 1) * YROWS]


def gather_kernel(parts, out):
    shape = (NZ, ZROWS, ALL)
    z, k, at = iota(shape, 0), iota(shape, 1), iota(shape, 2)
    low = (k >> 2) * YROWS + (k & 1) * 32 + z * 2 + ((k & 3) >> 1)
    k2 = k - NY * CAP
    high = (k2 >> 1) * YROWS + NZ * CAP + z * 2 + (k2 & 1)
    move = hot((at == jnp.where(k < NY * CAP, low, high)).reshape(ALL, ALL))
    sums = []
    for j in range(NY):
        total = parts[j * NX].astype(F32)
        for i in range(1, NX):
            total = total + parts[j * NX + i].astype(F32)
        sums.append(total)
    out[...] = dot(move, jnp.concatenate(sums, axis=0).astype(BF)).astype(BF)


def assemble(ref, first):
    rows = []
    for j in range(NY):
        cols = []
        for i in range(NX):
            low = ref[j * NX + i, first : first + 64, :]
            high = ref[j * NX + i, first + 64 : first + YROWS, :]
            cols.append(low)
            cols.append(jnp.concatenate([high[:, :64], high[:, 64:]], axis=0))
        rows.append(jnp.concatenate(cols, axis=1))
    return jnp.concatenate(rows, axis=0)


def fetch(core, layer, own, other, into, sem):
    @pl.when(core == layer)
    def _():
        pltpu.make_async_copy(own, into, sem).start()

    @pl.when(core != layer)
    def _():
        pltpu.make_async_copy(other, into, sem).start()

    return pltpu.make_async_copy(own, into, sem)


def expert_kernel(
    layer, acts_at, grad_at, core_ref, acts_ref, grad_ref, own_in, other_in, own_out, other_out,
    out, kept_out, in_ref, out_ref, kept, sems,
):
    core = core_ref[0]
    first = fetch(core, layer, own_in, other_in, in_ref, sems.at[0])
    second = fetch(core, layer, own_out, other_out, out_ref, sems.at[1])
    saves = [pltpu.make_async_copy(kept.at[k], kept_out.at[k], sems.at[2 + k]) for k in range(4)]

    def save(k, value):
        kept[k] = value
        saves[k].start()

    x = assemble(acts_ref, acts_at).astype(F32)
    grad = assemble(grad_ref, grad_at)
    save(3, grad)
    inv = lax.rsqrt(jnp.mean(x * x, axis=1, keepdims=True) + 1e-06)
    normed = (x * inv).astype(BF)
    save(0, normed)
    first.wait()
    u = dot(normed, in_ref[...])
    square = u * u
    s = jnp.tanh(0.7978845608 * (u + 0.044715 * square * u))
    save(2, (0.5 * u * (1.0 + s)).astype(BF))
    slope = 0.5 * (1.0 + s) + 0.5 * u * (1.0 - s * s) * 0.7978845608 * (1.0 + 0.134145 * square)
    second.wait()
    back = (dot(grad, out_ref[...], 1, 1) * slope).astype(BF)
    save(1, back)
    part = dot(back, in_ref[...], 1, 1)
    inner = jnp.sum(part * x, axis=1, keepdims=True)
    branch = (inv * part - (inv * inv * inv * inner * (1.0 / WIDTH)) * x).astype(BF)
    for j in range(NY):
        for i in range(NX):
            at = i * SHARE
            block = branch[j * 64 : (j + 1) * 64]
            out[j * NX + i, 0:64, :] = block[:, at : at + LOW]
            out[j * NX + i, 64:YROWS, :] = jnp.concatenate(
                [block[:32, at + LOW : at + SHARE], block[32:, at + LOW : at + SHARE]], axis=1
            )
    for copy in saves:
        copy.wait()


def weight_kernel(core_ref, kept1, came1, kept0, came0, first, second, mark, rows, sums, sems):
    core = core_ref[0]
    half = NY * NZ * CAP
    for index, sources in enumerate([(kept0, came0), (kept1, came1)]):

        @pl.when(core == index)
        def _():
            for k in range(4):
                for n, src in enumerate(sources):
                    pltpu.make_async_copy(src.at[k], rows.at[k, n * half : (n + 1) * half], sems.at[2 * k + n]).start()

    def product(k, at, dst):
        for i in (k, k + 1):
            for n in range(2):
                pltpu.make_async_copy(kept1.at[i], rows.at[i, n * half : (n + 1) * half], sems.at[2 * i + n]).wait()
        sums[at] = dot(rows[k], rows[k + 1], 0, 0).astype(BF)
        copy = pltpu.make_async_copy(sums.at[at], dst, sems.at[8 + at])
        copy.start()
        return copy

    stores = [product(0, 0, first), product(2, 1, second)]
    mark[...] = jnp.zeros_like(mark)
    for copy in stores:
        copy.wait()


def middle_kernel(core_ref, rows, cot, gates, owners, slots, result, out):
    core = core_ref[0]
    branch = unpack(rows[...], row_of(owners, 1, core), row_of(slots, 1, core))
    res = (cot[core].astype(F32) + branch).astype(BF)
    result[...] = res
    gate = column(row_of(gates, 0, core))
    scaled = (gate * res.astype(F32)).astype(BF)
    (packed,) = pack([scaled], row_of(owners, 0, core), row_of(slots, 0, core))
    out[...] = packed.astype(BF)


def end_kernel(core_ref, rows, above, owners, slots, mark, keep, give):
    core = core_ref[0]
    branch = unpack(rows[...], row_of(owners, 0, core), row_of(slots, 0, core))
    res = (above[...].astype(F32) + branch).astype(BF)
    keep[...] = jnp.where(core == 0, res, above[...])
    give[...] = jnp.where(core == 0, above[...], res)


VM = pl.BlockSpec(memory_space=pltpu.VMEM)
SM = pl.BlockSpec(memory_space=pltpu.SMEM)
HB = pl.BlockSpec(memory_space=pltpu.HBM)


def call(kernel, ins, outs, name, scratch=(), mib=16, cost=None, places=None):
    return pl.pallas_call(
        kernel,
        in_specs=list(ins),
        out_specs=places or [VM] * len(outs),
        out_shape=[jax.ShapeDtypeStruct(o, BF) for o in outs],
        scratch_shapes=list(scratch),
        compiler_params=pltpu.CompilerParams(vmem_limit_bytes=mib << 20),
        cost_estimate=cost and pl.CostEstimate(flops=cost[0], bytes_accessed=cost[1], transcendentals=0),
        name=name,
    )


def a2a(x, axis):
    return lax.all_to_all(x, axis, split_axis=0, concat_axis=0, tiled=True)


def over_z(x):
    return a2a(x.reshape(NZ, -1, LOW), "z").reshape(-1, LOW)


def over_yx(x):
    return a2a(x, ("y", "pair"))


def expert(layer, acts_at, grad_at, core, acts, grad, weights):
    rows = (NY * NZ * CAP, WIDTH)
    return call(
        functools.partial(expert_kernel, layer, acts_at, grad_at),
        [SM, VM, VM] + [HB] * 4,
        [(NY * NX, YROWS, LOW), (4,) + rows],
        "expert",
        [
            pltpu.VMEM((WIDTH, HID), BF),
            pltpu.VMEM((HID, WIDTH), BF),
            pltpu.VMEM((4,) + rows, BF),
            pltpu.SemaphoreType.DMA((6,)),
        ],
        places=[VM, HB],
    )(core, acts, grad, *weights)


def body(acts, cotangent, gates, owners, slots, w_in, w_out):
    index = lax.axis_index("segment")
    top = index == 1
    core = index.astype(I32).reshape(1)
    own_in, own_out = w_in[0, 0], w_out[0, 0]
    other_in = lax.ppermute(own_in, "segment", SWAP)
    other_out = lax.ppermute(own_out, "segment", SWAP)
    weights = (own_in, other_in, own_out, other_out)

    table = (2, 2, TOK)
    (packed,) = call(
        start_kernel, [SM] + [HB] * 5, [(3 * ALL, LOW)], "start",
        [pltpu.VMEM((3, TOK, SHARE), BF), pltpu.VMEM(table, F32), pltpu.VMEM(table, I32),
         pltpu.VMEM(table, I32), pltpu.SemaphoreType.DMA((6,))], mib=60,
    )(core, acts, cotangent, gates, owners, slots)
    (sent,) = call(functools.partial(spread_kernel, 3), [VM], [(NY * NX, 3 * YROWS, LOW)], "spread3")(
        over_z(packed)
    )
    saved = over_yx(sent)
    parts, kept1 = expert(1, 0, YROWS, core, saved, saved, weights)
    came1 = lax.ppermute(kept1, "segment", [(0, 1)])
    (rows,) = call(gather_kernel, [VM], [(ALL, LOW)], "gather")(over_yx(parts))
    res1, packed = call(middle_kernel, [SM] + [VM] * 5, [(TOK, SHARE), (ALL, LOW)], "middle")(
        core, over_z(rows), cotangent, gates, owners, slots
    )
    (sent,) = call(functools.partial(spread_kernel, 1), [VM], [(NY * NX, YROWS, LOW)], "spread1")(
        over_z(packed)
    )
    parts, kept0 = expert(0, 2 * YROWS, 0, core, saved, over_yx(sent), weights)
    (rows,) = call(gather_kernel, [VM], [(ALL, LOW)], "gather")(over_yx(parts))

    came0 = lax.ppermute(kept0, "segment", [(1, 0)])
    grad_in, grad_out, mark = call(
        weight_kernel, [SM] + [HB] * 4, [(WIDTH, HID), (HID, WIDTH), (16, 128)], "weight",
        [pltpu.VMEM((4, 2 * NY * NZ * CAP, WIDTH), BF), pltpu.VMEM((2, WIDTH, HID), BF), pltpu.SemaphoreType.DMA((10,))],
        mib=24, cost=(2 * 10**9, 6 * 10**6), places=[HB, HB, VM],
    )(core, kept1, came1, kept0, came0)
    mine, other = call(end_kernel, [SM] + [VM] * 5, [(TOK, SHARE)] * 2, "end")(
        core, over_z(rows), res1, owners, slots, mark
    )
    got = lax.ppermute(other, "segment", SWAP)
    grads = jnp.stack([jnp.where(top, got, mine), jnp.where(top, mine, got)])
    return grads[None], grad_in[None, None], grad_out[None, None]


def solution(mesh):
    fine = Mesh(mesh.devices.reshape(2, NY, NZ, NX), ("segment", "y", "z", "pair"))
    e = ("y", "z")
    placed = (
        P(None, None, e, "pair"),
        P(None, e, "pair"),
        P(None, None, e),
        P(None, None, e),
        P(None, None, e),
        P("segment", e, None, "pair"),
        P("segment", e, "pair", None),
    )
    return jax.shard_map(
        body,
        mesh=fine,
        in_specs=placed,
        out_specs=(
            P("segment", None, e, "pair"),
            P("segment", e, None, "pair"),
            P("segment", e, "pair", None),
        ),
        check_vma=False,
    )
```

time: 226 us -> 180 us (0.80)
  blocking collectives: 40.9 us -> 70.1 us
  matrix products: 25.8 us -> 0 us
  other arithmetic: 22.3 us -> 0.73 us
  local copies, waits for them, and re-layouts: 24.1 us -> 4.4 us
  Pallas kernels: 0 us -> 19.3 us
  starting transfers between devices: 63.7 us -> 47.6 us
  waiting for transfers between devices: 46.9 us -> 36.2 us
    all_to_all x1 -> x4, blocking collectives: 40.9 us -> 70.1 us  [a2a(): return lax.all_to_all(x, axis, split_axis=0, concat_axis=0, tiled=True)]
    dot_general x15 -> x0, matrix products: 25.8 us -> none  [dot(): lax.dot_general(a, b, (((ca,), (cb,)), ((), ())), preferred_element_type=...]
    pallas_call x0 -> x10, Pallas kernels: none -> 19.3 us  [the longest x2 9.33 us: expert(): call(functools.partial(expert_kernel, layer, acts_at, grad_at), [SM, VM,...]
    convert_element_type x8 -> x0, local copies, waits for them, and re-layouts: 11.7 us -> none  [the longest x2 3.84 us: expert_pass(): part.astype(BF).reshape(rows, pairs, share)]
    all_to_all x7 -> x4, waiting for transfers between devices: 45.9 us -> 35.2 us  [a2a(): return lax.all_to_all(x, axis, split_axis=0, concat_axis=0, tiled=True)]
    all_to_all x7 -> x4, starting transfers between devices: 38 us -> 30.4 us  [a2a(): return lax.all_to_all(x, axis, split_axis=0, concat_axis=0, tiled=True)]
    convert_element_type x8 -> x0, other arithmetic: 6.81 us -> none  [the longest x1 2.4 us: expert_pass(): af = acts.astype(F32)]
    ppermute x3, starting transfers between devices: 19.1 us -> 12.5 us  [the longest x1 7 us: body(): came0 = lax.ppermute(kept0, 'segment', [(1, 0)])]
  transfers between devices with their start and end apart: 12 -> 9, of which waited for: 7 -> 5; matrix products, arithmetic and copies ran while one was open for 14% -> 0% of each run, Pallas kernels for 0% -> 6%
where the time goes in v2:
time: 180 us; the launch traced here: 179 us
  blocking collectives  70.1 us (39%)
  starting transfers between devices  47.6 us (26%)
  waiting for transfers between devices  36.2 us (20%)
  Pallas kernels  19.3 us (11%)
  local copies, waits for them, and re-layouts  4.4 us (2%)
    all_to_all x4, blocking collectives, a2a(): return lax.all_to_all(x, axis, split_axis=0, concat_axis=0, tiled=True)  70.1 us
    all_to_all x4, waiting for transfers between devices, a2a(): return lax.all_to_all(x, axis, split_axis=0, concat_axis=0, tiled=True)  35.2 us
    all_to_all x4, starting transfers between devices, a2a(): return lax.all_to_all(x, axis, split_axis=0, concat_axis=0, tiled=True)  30.4 us
    pallas_call x2, Pallas kernels, expert(): call(functools.partial(expert_kernel, layer, acts_at, grad_at), [SM, VM,...  9.33 us
    ppermute x1, starting transfers between devices, body(): came0 = lax.ppermute(kept0, 'segment', [(1, 0)])  7 us
    pallas_call x1, Pallas kernels, body(): call(weight_kernel, [SM] + [HB] * 4, [(WIDTH, HID), (HID, WIDTH), (16, 12...  4.52 us
    unnamed x24, local copies, waits for them, and re-layouts  4.4 us
    ppermute x1, starting transfers between devices, body(): got = lax.ppermute(other, 'segment', SWAP)  4.2 us
  transfers between devices with their start and end apart: 9, of which 5 were waited for; matrix products, arithmetic and copies ran while one was open for 0% of the time, Pallas kernels for 6%

profile of v2, /device:TPU:1, one launch (start us, length us, event | category | flops | bytes accessed | tf_op | source)
XLA Modules:
  0.0 179.3 jit_solution(12824388797132788592)
XLA Ops:
  0.6 2.5 %start.1 = bf16[1152,128]{1,0:T(8,128)(2,1)} custom-call(s32[1]{0:T(128)} %bitcast.core_ref, bf16[2,2,192,192]{3,2,1,0:T(8,128)(2,1)} %acts.1, bf16[2,192,192]{2,1,0:T(8,128)(2,1)} %cot.3, f32[2,2,192]{2,1,0:T(2,128)} %gates.3, s32[2,2,192]{2,1,0:T(2,128)} %owners.5, s32[2,2,192]{2,1,0:T(2,128)} %slots.5), custom_call_target="tpu_custom_call" | custom-call | tf_op jit(solution)/shard_map/start/pallas_call | solution.py:313
  3.2 15.7 %all-to-all-start = ((bf16[16,72,128]{2,1,0:T(8,128)(2,1)}), bf16[16,72,128]{2,1,0:T(8,128)(2,1)S(1)}, u32[]{:S(2)}, u32[]{:S(2)}) async-start(bf16[16,72,128]{2,1,0:T(8,128)(2,1)} %bitcast.31), calls=%async_computation | async-start | bytes 589824 | tf_op jit(solution)/shard_map/all_to_all | solution.py:275
  19.0 2.9 %collective-permute-start = (bf16[768,768]{1,0:T(8,128)(2,1)S(1)}, bf16[768,768]{1,0:T(8,128)(2,1)}, u32[]{:S(2)}, u32[]{:S(2)}) collective-permute-start(bf16[768,768]{1,0:T(8,128)(2,1)S(1)} %bitcast.19), channel_id=1, source_target_pairs={{0,256},{256,0},{1,257},{257,1},{2,258},{258,2},{3,259},{259,3},{4... | collective-permute-start | bytes 3538952 | tf_op jit(solution)/shard_map/ppermute | solution.py:308
  21.8 1.9 %collective-permute-start.1 = (bf16[768,768]{1,0:T(8,128)(2,1)}, bf16[768,768]{1,0:T(8,128)(2,1)}, u32[]{:S(2)}, u32[]{:S(2)}) collective-permute-start(bf16[768,768]{1,0:T(8,128)(2,1)} %bitcast.22), channel_id=1, source_target_pairs={{0,256},{256,0},{1,257},{257,1},{2,258},{258,2},{3,259},{259,3},{4... | collective-permute-start | bytes 3538952 | tf_op jit(solution)/shard_map/ppermute | solution.py:309
  23.8 8.9 %all-to-all-done = bf16[16,72,128]{2,1,0:T(8,128)(2,1)S(1)} async-done(((bf16[16,72,128]{2,1,0:T(8,128)(2,1)}), bf16[16,72,128]{2,1,0:T(8,128)(2,1)S(1)}, u32[]{:S(2)}, u32[]{:S(2)}) %all-to-all-start) | async-done | bytes 294944 | tf_op jit(solution)/shard_map/all_to_all | solution.py:275
  33.1 1.0 copy-done.2
  34.1 6.9 %all-to-all-start.1 = ((bf16[16,288,128]{2,1,0:T(8,128)(2,1)}), bf16[16,288,128]{2,1,0:T(8,128)(2,1)S(1)}, u32[]{:S(2)}, u32[]{:S(2)}) async-start(bf16[16,288,128]{2,1,0:T(8,128)(2,1)} %copy-done.2), calls=%async_computation.1 | async-start | bytes 2359296 | tf_op jit(solution)/shard_map/all_to_all | solution.py:275
  41.0 13.4 %all-to-all-done.1.acts_ref.grad_ref = bf16[16,288,128]{2,1,0:T(8,128)(2,1)S(1)} async-done(((bf16[16,288,128]{2,1,0:T(8,128)(2,1)}), bf16[16,288,128]{2,1,0:T(8,128)(2,1)S(1)}, u32[]{:S(2)}, u32[]{:S(2)}) %all-to-all-start.1) | async-done | bytes 1179680 | tf_op jit(solution)/shard_map/all_to_all | solution.py:275
  54.5 4.4 %expert.2 = (bf16[16,96,128]{2,1,0:T(8,128)(2,1)S(1)}, bf16[4,256,768]{2,1,0:T(8,128)(2,1)S(1)}) custom-call(s32[1]{0:T(128)} %bitcast.core_ref, bf16[16,288,128]{2,1,0:T(8,128)(2,1)S(1)} %all-to-all-done.1.acts_ref.grad_ref, bf16[16,288,128]{2,1,0:T(8,128)(2,1)S(1)} %all-to-all-done.1.acts_ref.grad_ref, bf16[768,768]{1,0:T(8,128)(2,1)S(1)} %bitcast.20, ...), custom_call_target="tpu_custom_call" | custom-call | tf_op jit(solution)/shard_map/expert/pallas_call | solution.py:288
  58.9 1.2 copy-done.10
  60.1 11.0 %all_to_all.40.parts = bf16[16,96,128]{2,1,0:T(8,128)(2,1)S(1)} all-to-all(bf16[16,96,128]{2,1,0:T(8,128)(2,1)S(1)} %get-tuple-element.14), channel_id=1, replica_groups=mesh['segment'=2,'y'=4,'z'=16,'pair'=4] {'y','pair'}, dimensions={0} | all-to-all | bytes 786432 | tf_op jit(solution)/shard_map/all_to_all | solution.py:275
  71.3 30.8 %all_to_all.41 = bf16[16,24,128]{2,1,0:T(8,128)(2,1)S(1)} all-to-all(bf16[16,24,128]{2,1,0:T(8,128)(2,1)S(1)} %bitcast.28), channel_id=1, replica_groups=mesh['segment'=2,'y'=4,'z'=16,'pair'=4] {'z'}, dimensions={0} | all-to-all | bytes 196608 | tf_op jit(solution)/shard_map/all_to_all | solution.py:275
  102.9 15.1 %all_to_all.42 = bf16[16,24,128]{2,1,0:T(8,128)(2,1)S(1)} all-to-all(bf16[16,24,128]{2,1,0:T(8,128)(2,1)S(1)} %bitcast.30), channel_id=1, replica_groups=mesh['segment'=2,'y'=4,'z'=16,'pair'=4] {'z'}, dimensions={0} | all-to-all | bytes 196608 | tf_op jit(solution)/shard_map/all_to_all | solution.py:275
  119.0 4.2 %all-to-all-start.5 = ((bf16[16,96,128]{2,1,0:T(8,128)(2,1)}), bf16[16,96,128]{2,1,0:T(8,128)(2,1)}, u32[]{:S(2)}, u32[]{:S(2)}) async-start(bf16[16,96,128]{2,1,0:T(8,128)(2,1)} %copy-done.3), calls=%async_computation.5 | async-start | bytes 786432 | tf_op jit(solution)/shard_map/all_to_all | solution.py:275
  123.2 1.3 collective-permute-start.2
  124.5 7.0 %all-to-all-done.5.grad_ref = bf16[16,96,128]{2,1,0:T(8,128)(2,1)} async-done(((bf16[16,96,128]{2,1,0:T(8,128)(2,1)}), bf16[16,96,128]{2,1,0:T(8,128)(2,1)}, u32[]{:S(2)}, u32[]{:S(2)}) %all-to-all-start.5) | async-done | bytes 393248 | tf_op jit(solution)/shard_map/all_to_all | solution.py:275
  131.5 4.9 %expert.3 = (bf16[16,96,128]{2,1,0:T(8,128)(2,1)S(1)}, bf16[4,256,768]{2,1,0:T(8,128)(2,1)}) custom-call(s32[1]{0:T(128)} %bitcast.core_ref, bf16[16,288,128]{2,1,0:T(8,128)(2,1)S(1)} %all-to-all-done.1.acts_ref.grad_ref, bf16[16,96,128]{2,1,0:T(8,128)(2,1)} %all-to-all-done.5.grad_ref, bf16[768,768]{1,0:T(8,128)(2,1)S(1)} %bitcast.21, ...), custom_call_target="tpu_custom_call" | custom-call | tf_op jit(solution)/shard_map/expert/pallas_call | solution.py:288
  136.4 7.0 %collective-permute-start.3 = (bf16[4,256,768]{2,1,0:T(8,128)(2,1)}, bf16[4,256,768]{2,1,0:T(8,128)(2,1)S(1)}, u32[]{:S(2)}, u32[]{:S(2)}) collective-permute-start(bf16[4,256,768]{2,1,0:T(8,128)(2,1)} %get-tuple-element.19.kept0), channel_id=1, source_target_pairs={{256,0},{257,1},{258,2},{259,3},{260,4},{261,5},{262,6},{263,7},{2... | collective-permute-start | bytes 4718600 | tf_op jit(solution)/shard_map/ppermute | solution.py:334
  143.4 13.3 %all_to_all.43.parts = bf16[16,96,128]{2,1,0:T(8,128)(2,1)S(1)} all-to-all(bf16[16,96,128]{2,1,0:T(8,128)(2,1)S(1)} %get-tuple-element.16), channel_id=1, replica_groups=mesh['segment'=2,'y'=4,'z'=16,'pair'=4] {'y','pair'}, dimensions={0} | all-to-all | bytes 786432 | tf_op jit(solution)/shard_map/all_to_all | solution.py:275
  157.6 3.5 %all-to-all-start.7 = ((bf16[16,24,128]{2,1,0:T(8,128)(2,1)}), bf16[16,24,128]{2,1,0:T(8,128)(2,1)S(1)}, u32[]{:S(2)}, u32[]{:S(2)}) async-start(bf16[16,24,128]{2,1,0:T(8,128)(2,1)} %bitcast.9), calls=%async_computation.7 | async-start | bytes 196608 | tf_op jit(solution)/shard_map/all_to_all | solution.py:275
  161.2 1.4 copy-done.11
  162.6 4.5 %weight.1 = (bf16[768,768]{1,0:T(8,128)(2,1)}, bf16[768,768]{1,0:T(8,128)(2,1)}, bf16[16,128]{1,0:T(8,128)(2,1)S(1)}) custom-call(s32[1]{0:T(128)} %bitcast.core_ref, bf16[4,256,768]{2,1,0:T(8,128)(2,1)S(1)} %copy-done.11, bf16[4,256,768]{2,1,0:T(8,128)(2,1)} %collective-permute-done.2.came1, bf16[4,256,768]{2,1,0:T(8,128)(2,1)} %get-tuple-element.19.kept0, ...), custom_call_target="tpu_custom_call" | custom-call | flops 2000000000 | bytes 6000000 | tf_op jit(solution)/shard_map/weight/pallas_call | solution.py:335
  167.1 5.9 %all-to-all-done.7 = bf16[16,24,128]{2,1,0:T(8,128)(2,1)S(1)} async-done(((bf16[16,24,128]{2,1,0:T(8,128)(2,1)}), bf16[16,24,128]{2,1,0:T(8,128)(2,1)S(1)}, u32[]{:S(2)}, u32[]{:S(2)}) %all-to-all-start.7) | async-done | bytes 98336 | tf_op jit(solution)/shard_map/all_to_all | solution.py:275
  173.4 4.2 %collective-permute-start.4 = (bf16[192,192]{1,0:T(8,128)(2,1)S(1)}, bf16[192,192]{1,0:T(8,128)(2,1)S(1)}, u32[]{:S(2)}, u32[]{:S(2)}) collective-permute-start(bf16[192,192]{1,0:T(8,128)(2,1)S(1)} %get-tuple-element.21), channel_id=1, source_target_pairs={{0,256},{256,0},{1,257},{257,1},{2,258},{258,2},{3,259},{259,3},{4... | collective-permute-start | bytes 221192 | tf_op jit(solution)/shard_map/ppermute | solution.py:343
  (34 shorter events, 5.4 us)
Async XLA Ops:
  0.6 18.3 %copy-start = (bf16[1,1,768,768]{3,2,1,0:T(8,128)(2,1)S(1)}, bf16[1,1,768,768]{3,2,1,0:T(8,128)(2,1)}, u32[]{:S(2)}) copy-start(bf16[1,1,768,768]{3,2,1,0:T(8,128)(2,1)} %param.12) | copy-start | bytes 3538948
  3.2 29.5 %all-to-all-start = ((bf16[16,72,128]{2,1,0:T(8,128)(2,1)}), bf16[16,72,128]{2,1,0:T(8,128)(2,1)S(1)}, u32[]{:S(2)}, u32[]{:S(2)}) async-start(bf16[16,72,128]{2,1,0:T(8,128)(2,1)} %bitcast.31), calls=%async_computation | async-start | bytes 589824 | tf_op jit(solution)/shard_map/all_to_all | solution.py:275
  19.0 22.1 %collective-permute-start = (bf16[768,768]{1,0:T(8,128)(2,1)S(1)}, bf16[768,768]{1,0:T(8,128)(2,1)}, u32[]{:S(2)}, u32[]{:S(2)}) collective-permute-start(bf16[768,768]{1,0:T(8,128)(2,1)S(1)} %bitcast.19), channel_id=1, source_target_pairs={{0,256},{256,0},{1,257},{257,1},{2,258},{258,2},{3,259},{259,3},{4... | collective-permute-start | bytes 3538952 | tf_op jit(solution)/shard_map/ppermute | solution.py:308
  21.8 19.2 %collective-permute-start.1 = (bf16[768,768]{1,0:T(8,128)(2,1)}, bf16[768,768]{1,0:T(8,128)(2,1)}, u32[]{:S(2)}, u32[]{:S(2)}) collective-permute-start(bf16[768,768]{1,0:T(8,128)(2,1)} %bitcast.22), channel_id=1, source_target_pairs={{0,256},{256,0},{1,257},{257,1},{2,258},{258,2},{3,259},{259,3},{4... | collective-permute-start | bytes 3538952 | tf_op jit(solution)/shard_map/ppermute | solution.py:309
  33.1 1.0 copy-start.2
  34.1 20.4 %copy-start.1 = (bf16[1,1,768,768]{3,2,1,0:T(8,128)(2,1)S(1)}, bf16[1,1,768,768]{3,2,1,0:T(8,128)(2,1)}, u32[]{:S(2)}) copy-start(bf16[1,1,768,768]{3,2,1,0:T(8,128)(2,1)} %param.13) | copy-start | bytes 3538948
  34.1 20.4 %all-to-all-start.1 = ((bf16[16,288,128]{2,1,0:T(8,128)(2,1)}), bf16[16,288,128]{2,1,0:T(8,128)(2,1)S(1)}, u32[]{:S(2)}, u32[]{:S(2)}) async-start(bf16[16,288,128]{2,1,0:T(8,128)(2,1)} %copy-done.2), calls=%async_computation.1 | async-start | bytes 2359296 | tf_op jit(solution)/shard_map/all_to_all | solution.py:275
  58.9 1.2 copy-start.10
  60.1 42.0 %copy-start.4 = (bf16[2,192,192]{2,1,0:T(8,128)(2,1)S(1)}, bf16[2,192,192]{2,1,0:T(8,128)(2,1)}, u32[]{:S(2)}) copy-start(bf16[2,192,192]{2,1,0:T(8,128)(2,1)} %cot.3) | copy-start | bytes 442372
  60.1 42.0 %copy-start.7 = (s32[2,2,192]{2,1,0:T(2,128)S(1)}, s32[2,2,192]{2,1,0:T(2,128)}, u32[]{:S(2)}) copy-start(s32[2,2,192]{2,1,0:T(2,128)} %owners.5) | copy-start | bytes 9220
  60.1 42.0 %copy-start.8 = (s32[2,2,192]{2,1,0:T(2,128)S(1)}, s32[2,2,192]{2,1,0:T(2,128)}, u32[]{:S(2)}) copy-start(s32[2,2,192]{2,1,0:T(2,128)} %slots.5) | copy-start | bytes 9220
  60.1 42.0 %copy-start.9 = (f32[2,2,192]{2,1,0:T(2,128)S(1)}, f32[2,2,192]{2,1,0:T(2,128)}, u32[]{:S(2)}) copy-start(f32[2,2,192]{2,1,0:T(2,128)} %gates.3) | copy-start | bytes 9220
  102.9 15.1 %copy-start.5 = (bf16[192,192]{1,0:T(8,128)(2,1)}, bf16[192,192]{1,0:T(8,128)(2,1)S(1)}, u32[]{:S(2)}) copy-start(bf16[192,192]{1,0:T(8,128)(2,1)S(1)} %get-tuple-element.17.above) | copy-start | bytes 221188
  118.2 0.7 copy-start.3
  119.0 12.5 %all-to-all-start.5 = ((bf16[16,96,128]{2,1,0:T(8,128)(2,1)}), bf16[16,96,128]{2,1,0:T(8,128)(2,1)}, u32[]{:S(2)}, u32[]{:S(2)}) async-start(bf16[16,96,128]{2,1,0:T(8,128)(2,1)} %copy-done.3), calls=%async_computation.5 | async-start | bytes 786432 | tf_op jit(solution)/shard_map/all_to_all | solution.py:275
  123.2 37.9 %collective-permute-start.2 = (bf16[4,256,768]{2,1,0:T(8,128)(2,1)}, bf16[4,256,768]{2,1,0:T(8,128)(2,1)}, u32[]{:S(2)}, u32[]{:S(2)}) collective-permute-start(bf16[4,256,768]{2,1,0:T(8,128)(2,1)} %copy-done.10), channel_id=1, source_target_pairs={{0,256},{1,257},{2,258},{3,259},{4,260},{5,261},{6,262},{7,263},{8... | collective-permute-start | bytes 4718600 | tf_op jit(solution)/shard_map/ppermute | solution.py:323
  136.4 24.7 %collective-permute-start.3 = (bf16[4,256,768]{2,1,0:T(8,128)(2,1)}, bf16[4,256,768]{2,1,0:T(8,128)(2,1)S(1)}, u32[]{:S(2)}, u32[]{:S(2)}) collective-permute-start(bf16[4,256,768]{2,1,0:T(8,128)(2,1)} %get-tuple-element.19.kept0), channel_id=1, source_target_pairs={{256,0},{257,1},{258,2},{259,3},{260,4},{261,5},{262,6},{263,7},{2... | collective-permute-start | bytes 4718600 | tf_op jit(solution)/shard_map/ppermute | solution.py:334
  157.6 15.4 %all-to-all-start.7 = ((bf16[16,24,128]{2,1,0:T(8,128)(2,1)}), bf16[16,24,128]{2,1,0:T(8,128)(2,1)S(1)}, u32[]{:S(2)}, u32[]{:S(2)}) async-start(bf16[16,24,128]{2,1,0:T(8,128)(2,1)} %bitcast.9), calls=%async_computation.7 | async-start | bytes 196608 | tf_op jit(solution)/shard_map/all_to_all | solution.py:275
  161.1 11.9 %copy-start.6 = (bf16[192,192]{1,0:T(8,128)(2,1)S(1)}, bf16[192,192]{1,0:T(8,128)(2,1)}, u32[]{:S(2)}) copy-start(bf16[192,192]{1,0:T(8,128)(2,1)} %copy-done.5) | copy-start | bytes 221188
  161.1 1.4 copy-start.11
  173.4 5.1 %collective-permute-start.4 = (bf16[192,192]{1,0:T(8,128)(2,1)S(1)}, bf16[192,192]{1,0:T(8,128)(2,1)S(1)}, u32[]{:S(2)}, u32[]{:S(2)}) collective-permute-start(bf16[192,192]{1,0:T(8,128)(2,1)S(1)} %get-tuple-element.21), channel_id=1, source_target_pairs={{0,256},{256,0},{1,257},{257,1},{2,258},{258,2},{3,259},{259,3},{4... | collective-permute-start | bytes 221192 | tf_op jit(solution)/shard_map/ppermute | solution.py:343

commit v3 on v2

--- a/solution.py
+++ b/solution.py
@@ -153,47 +153,19 @@
     return jnp.concatenate(rows, axis=0)
 
 
-def fetch(core, layer, own, other, into, sem):
-    @pl.when(core == layer)
-    def _():
-        pltpu.make_async_copy(own, into, sem).start()
-
-    @pl.when(core != layer)
-    def _():
-        pltpu.make_async_copy(other, into, sem).start()
-
-    return pltpu.make_async_copy(own, into, sem)
-
-
-def expert_kernel(
-    layer, acts_at, grad_at, core_ref, acts_ref, grad_ref, own_in, other_in, own_out, other_out,
-    out, kept_out, in_ref, out_ref, kept, sems,
-):
-    core = core_ref[0]
-    first = fetch(core, layer, own_in, other_in, in_ref, sems.at[0])
-    second = fetch(core, layer, own_out, other_out, out_ref, sems.at[1])
-    saves = [pltpu.make_async_copy(kept.at[k], kept_out.at[k], sems.at[2 + k]) for k in range(4)]
-
-    def save(k, value):
-        kept[k] = value
-        saves[k].start()
-
-    x = assemble(acts_ref, acts_at).astype(F32)
-    grad = assemble(grad_ref, grad_at)
+def expert_step(x, grad, w_in, w_out, out, save):
     save(3, grad)
     inv = lax.rsqrt(jnp.mean(x * x, axis=1, keepdims=True) + 1e-06)
     normed = (x * inv).astype(BF)
     save(0, normed)
-    first.wait()
-    u = dot(normed, in_ref[...])
+    u = dot(normed, w_in[...])
     square = u * u
     s = jnp.tanh(0.7978845608 * (u + 0.044715 * square * u))
     save(2, (0.5 * u * (1.0 + s)).astype(BF))
     slope = 0.5 * (1.0 + s) + 0.5 * u * (1.0 - s * s) * 0.7978845608 * (1.0 + 0.134145 * square)
-    second.wait()
-    back = (dot(grad, out_ref[...], 1, 1) * slope).astype(BF)
+    back = (dot(grad, w_out[...], 1, 1) * slope).astype(BF)
     save(1, back)
-    part = dot(back, in_ref[...], 1, 1)
+    part = dot(back, w_in[...], 1, 1)
     inner = jnp.sum(part * x, axis=1, keepdims=True)
     branch = (inv * part - (inv * inv * inv * inner * (1.0 / WIDTH)) * x).astype(BF)
     for j in range(NY):
@@ -204,25 +176,74 @@
             out[j * NX + i, 64:YROWS, :] = jnp.concatenate(
                 [block[:32, at + LOW : at + SHARE], block[32:, at + LOW : at + SHARE]], axis=1
             )
-    for copy in saves:
-        copy.wait()
-
-
-def weight_kernel(core_ref, kept1, came1, kept0, came0, first, second, mark, rows, sums, sems):
-    core = core_ref[0]
+
+
+def upper_kernel(core_ref, saved, own_in, other_in, own_out, other_out, out, *kept):
+    def run(w_in, w_out):
+        def save(k, value):
+            kept[k][...] = value
+
+        expert_step(assemble(saved, 0).astype(F32), assemble(saved, YROWS), w_in, w_out, out, save)
+
+    @pl.when(core_ref[0] == 1)
+    def _():
+        run(own_in, own_out)
+
+    @pl.when(core_ref[0] != 1)
+    def _():
+        run(other_in, other_out)
+
+
+def lower_kernel(
+    core_ref, saved, came, n1, b1, h1, g1, own_in, other_in, own_out, other_out,
+    out, k0, k1, k2, k3, give, kept, sems,
+):
+    keep, above = (k0, k1, k2, k3), (n1, b1, h1, g1)
+
+    def run(w_in, w_out, save):
+        expert_step(assemble(saved, 2 * YROWS).astype(F32), assemble(came, 0), w_in, w_out, out, save)
+
+    @pl.when(core_ref[0] == 0)
+    def _():
+        copies = [pltpu.make_async_copy(above[k], give.at[k], sems.at[k]) for k in range(4)]
+        for copy in copies:
+            copy.start()
+
+        def save(k, value):
+            keep[k][...] = value
+
+        run(own_in, own_out, save)
+        for copy in copies:
+            copy.wait()
+
+    @pl.when(core_ref[0] != 0)
+    def _():
+        copies = [pltpu.make_async_copy(kept.at[k], give.at[k], sems.at[k]) for k in range(4)]
+
+        def save(k, value):
+            kept[k] = value
+            copies[k].start()
+            keep[k][...] = above[k][...]
+
+        run(other_in, other_out, save)
+        for copy in copies:
+            copy.wait()
+
+
+def weight_kernel(k0, k1, k2, k3, came, first, second, mark, rows, sums, sems):
     half = NY * NZ * CAP
-    for index, sources in enumerate([(kept0, came0), (kept1, came1)]):
-
-        @pl.when(core == index)
-        def _():
-            for k in range(4):
-                for n, src in enumerate(sources):
-                    pltpu.make_async_copy(src.at[k], rows.at[k, n * half : (n + 1) * half], sems.at[2 * k + n]).start()
+    loads = [
+        [pltpu.make_async_copy(src, rows.at[k, n * half : (n + 1) * half], sems.at[2 * k + n])
+         for n, src in enumerate([(k0, k1, k2, k3)[k], came.at[k]])]
+        for k in range(4)
+    ]
+    for pair in loads:
+        for copy in pair:
+            copy.start()
 
     def product(k, at, dst):
-        for i in (k, k + 1):
-            for n in range(2):
-                pltpu.make_async_copy(kept1.at[i], rows.at[i, n * half : (n + 1) * half], sems.at[2 * i + n]).wait()
+        for copy in loads[k] + loads[k + 1]:
+            copy.wait()
         sums[at] = dot(rows[k], rows[k + 1], 0, 0).astype(BF)
         copy = pltpu.make_async_copy(sums.at[at], dst, sems.at[8 + at])
         copy.start()
@@ -283,23 +304,6 @@
     return a2a(x, ("y", "pair"))
 
 
-def expert(layer, acts_at, grad_at, core, acts, grad, weights):
-    rows = (NY * NZ * CAP, WIDTH)
-    return call(
-        functools.partial(expert_kernel, layer, acts_at, grad_at),
-        [SM, VM, VM] + [HB] * 4,
-        [(NY * NX, YROWS, LOW), (4,) + rows],
-        "expert",
-        [
-            pltpu.VMEM((WIDTH, HID), BF),
-            pltpu.VMEM((HID, WIDTH), BF),
-            pltpu.VMEM((4,) + rows, BF),
-            pltpu.SemaphoreType.DMA((6,)),
-        ],
-        places=[VM, HB],
-    )(core, acts, grad, *weights)
-
-
 def body(acts, cotangent, gates, owners, slots, w_in, w_out):
     index = lax.axis_index("segment")
     top = index == 1
@@ -315,12 +319,12 @@
         [pltpu.VMEM((3, TOK, SHARE), BF), pltpu.VMEM(table, F32), pltpu.VMEM(table, I32),
          pltpu.VMEM(table, I32), pltpu.SemaphoreType.DMA((6,))], mib=60,
     )(core, acts, cotangent, gates, owners, slots)
-    (sent,) = call(functools.partial(spread_kernel, 3), [VM], [(NY * NX, 3 * YROWS, LOW)], "spread3")(
+    (sent,) = call(functools.partial(spread_kernel, 3), [VM], [(NY * NX, 3 * YROWS, LOW)], "spread3", mib=16)(
         over_z(packed)
     )
     saved = over_yx(sent)
-    parts, kept1 = expert(1, 0, YROWS, core, saved, saved, weights)
-    came1 = lax.ppermute(kept1, "segment", [(0, 1)])
+    blocks, wide = (NY * NX, YROWS, LOW), (NY * NZ * CAP, WIDTH)
+    parts, *kept1 = call(upper_kernel, [SM] + [VM] * 5, [blocks] + [wide] * 4, "upper")(core, saved, *weights)
     (rows,) = call(gather_kernel, [VM], [(ALL, LOW)], "gather")(over_yx(parts))
     res1, packed = call(middle_kernel, [SM] + [VM] * 5, [(TOK, SHARE), (ALL, LOW)], "middle")(
         core, over_z(rows), cotangent, gates, owners, slots
@@ -328,15 +332,18 @@
     (sent,) = call(functools.partial(spread_kernel, 1), [VM], [(NY * NX, YROWS, LOW)], "spread1")(
         over_z(packed)
     )
-    parts, kept0 = expert(0, 2 * YROWS, 0, core, saved, over_yx(sent), weights)
+    parts, *keep, give = call(
+        lower_kernel, [SM] + [VM] * 10, [blocks] + [wide] * 4 + [(4,) + wide], "lower",
+        [pltpu.VMEM((4,) + wide, BF), pltpu.SemaphoreType.DMA((4,))], places=[VM] * 5 + [HB],
+    )(core, saved, over_yx(sent), *kept1, *weights)
+    came = lax.ppermute(give, "segment", SWAP)
     (rows,) = call(gather_kernel, [VM], [(ALL, LOW)], "gather")(over_yx(parts))
 
-    came0 = lax.ppermute(kept0, "segment", [(1, 0)])
     grad_in, grad_out, mark = call(
-        weight_kernel, [SM] + [HB] * 4, [(WIDTH, HID), (HID, WIDTH), (16, 128)], "weight",
+        weight_kernel, [HB] * 5, [(WIDTH, HID), (HID, WIDTH), (16, 128)], "weight",
         [pltpu.VMEM((4, 2 * NY * NZ * CAP, WIDTH), BF), pltpu.VMEM((2, WIDTH, HID), BF), pltpu.SemaphoreType.DMA((10,))],
-        mib=24, cost=(2 * 10**9, 6 * 10**6), places=[HB, HB, VM],
-    )(core, kept1, came1, kept0, came0)
+        mib=16, cost=(2 * 10**9, 6 * 10**6), places=[HB, HB, VM],
+    )(*keep, came)
     mine, other = call(end_kernel, [SM] + [VM] * 5, [(TOK, SHARE)] * 2, "end")(
         core, over_z(rows), res1, owners, slots, mark
     )

time: 180 us -> 176 us (0.978)
  blocking collectives: 70.1 us -> 80.5 us
  waiting for transfers between devices: 36.2 us -> 27.4 us
  starting transfers between devices: 47.6 us -> 43.2 us
    all_to_all x4 -> x5, blocking collectives: 70.1 us -> 80.5 us  [a2a(): return lax.all_to_all(x, axis, split_axis=0, concat_axis=0, tiled=True)]
    all_to_all x4 -> x3, waiting for transfers between devices: 35.2 us -> 26.5 us  [a2a(): return lax.all_to_all(x, axis, split_axis=0, concat_axis=0, tiled=True)]
    all_to_all x4 -> x3, starting transfers between devices: 30.4 us -> 26.2 us  [a2a(): return lax.all_to_all(x, axis, split_axis=0, concat_axis=0, tiled=True)]
    pallas_call x3, Pallas kernels: 13.8 us -> 12 us  [the longest x1 4.62 us: body(): call(weight_kernel, [HB] * 5, [(WIDTH, HID), (HID, WIDTH), (16, 128)], 'w...]
    ppermute x2 -> x1, starting transfers between devices: 8.29 us -> 7.56 us  [body(): came = lax.ppermute(give, 'segment', SWAP)]
    unnamed x24 -> x32, local copies, waits for them, and re-layouts: 4.4 us -> 3.77 us
  transfers between devices with their start and end apart: 9 -> 7, of which waited for: 5 -> 4; matrix products, arithmetic and copies ran while one was open for 0% -> 0% of each run, Pallas kernels for 6% -> 4%
where the time goes in v3:
time: 176 us; the launch traced here: 175 us
  blocking collectives  80.5 us (46%)
  starting transfers between devices  43.2 us (25%)
  waiting for transfers between devices  27.4 us (16%)
  Pallas kernels  18.5 us (11%)
  local copies, waits for them, and re-layouts  3.77 us (2%)
    all_to_all x5, blocking collectives, a2a(): return lax.all_to_all(x, axis, split_axis=0, concat_axis=0, tiled=True)  80.5 us
    all_to_all x3, waiting for transfers between devices, a2a(): return lax.all_to_all(x, axis, split_axis=0, concat_axis=0, tiled=True)  26.5 us
    all_to_all x3, starting transfers between devices, a2a(): return lax.all_to_all(x, axis, split_axis=0, concat_axis=0, tiled=True)  26.2 us
    ppermute x1, starting transfers between devices, body(): came = lax.ppermute(give, 'segment', SWAP)  7.56 us
    ppermute x1, starting transfers between devices, body(): got = lax.ppermute(other, 'segment', SWAP)  4.69 us
    pallas_call x1, Pallas kernels, body(): call(weight_kernel, [HB] * 5, [(WIDTH, HID), (HID, WIDTH), (16, 128)], 'w...  4.62 us
    pallas_call x1, Pallas kernels, body(): call(lower_kernel, [SM] + [VM] * 10, [blocks] + [wide] * 4 + [(4,) + wide...  3.88 us
    unnamed x32, local copies, waits for them, and re-layouts  3.77 us
  transfers between devices with their start and end apart: 7, of which 4 were waited for; matrix products, arithmetic and copies ran while one was open for 0% of the time, Pallas kernels for 4%

profile of v3, /device:TPU:1, one launch (start us, length us, event | category | flops | bytes accessed | tf_op | source)
XLA Modules:
  0.0 175.0 jit_solution(15334767287636662695)
XLA Ops:
  0.6 2.5 %start.1 = bf16[1152,128]{1,0:T(8,128)(2,1)} custom-call(s32[1]{0:T(128)} %bitcast.core_ref, bf16[2,2,192,192]{3,2,1,0:T(8,128)(2,1)} %acts.1, bf16[2,192,192]{2,1,0:T(8,128)(2,1)} %cot.3, f32[2,2,192]{2,1,0:T(2,128)} %gates.3, s32[2,2,192]{2,1,0:T(2,128)} %owners.5, s32[2,2,192]{2,1,0:T(2,128)} %slots.5), custom_call_target="tpu_custom_call" | custom-call | tf_op jit(solution)/shard_map/start/pallas_call | solution.py:317
  3.2 15.7 %all-to-all-start = ((bf16[16,72,128]{2,1,0:T(8,128)(2,1)}), bf16[16,72,128]{2,1,0:T(8,128)(2,1)S(1)}, u32[]{:S(2)}, u32[]{:S(2)}) async-start(bf16[16,72,128]{2,1,0:T(8,128)(2,1)} %bitcast.31), calls=%async_computation | async-start | bytes 589824 | tf_op jit(solution)/shard_map/all_to_all | solution.py:296
  19.0 2.9 %collective-permute-start = (bf16[768,768]{1,0:T(8,128)(2,1)S(1)}, bf16[768,768]{1,0:T(8,128)(2,1)}, u32[]{:S(2)}, u32[]{:S(2)}) collective-permute-start(bf16[768,768]{1,0:T(8,128)(2,1)S(1)} %bitcast.19), channel_id=1, source_target_pairs={{0,256},{256,0},{1,257},{257,1},{2,258},{258,2},{3,259},{259,3},{4... | collective-permute-start | bytes 3538952 | tf_op jit(solution)/shard_map/ppermute | solution.py:312
  21.8 1.9 %collective-permute-start.1 = (bf16[768,768]{1,0:T(8,128)(2,1)}, bf16[768,768]{1,0:T(8,128)(2,1)}, u32[]{:S(2)}, u32[]{:S(2)}) collective-permute-start(bf16[768,768]{1,0:T(8,128)(2,1)} %bitcast.22), channel_id=1, source_target_pairs={{0,256},{256,0},{1,257},{257,1},{2,258},{258,2},{3,259},{259,3},{4... | collective-permute-start | bytes 3538952 | tf_op jit(solution)/shard_map/ppermute | solution.py:313
  23.8 8.9 %all-to-all-done = bf16[16,72,128]{2,1,0:T(8,128)(2,1)S(1)} async-done(((bf16[16,72,128]{2,1,0:T(8,128)(2,1)}), bf16[16,72,128]{2,1,0:T(8,128)(2,1)S(1)}, u32[]{:S(2)}, u32[]{:S(2)}) %all-to-all-start) | async-done | bytes 294944 | tf_op jit(solution)/shard_map/all_to_all | solution.py:296
  32.7 1.4 spread3.1
  34.1 6.9 %all-to-all-start.1 = ((bf16[16,288,128]{2,1,0:T(8,128)(2,1)}), bf16[16,288,128]{2,1,0:T(8,128)(2,1)S(1)}, u32[]{:S(2)}, u32[]{:S(2)}) async-start(bf16[16,288,128]{2,1,0:T(8,128)(2,1)} %spread3.1), calls=%async_computation.1 | async-start | bytes 2359296 | tf_op jit(solution)/shard_map/all_to_all | solution.py:296
  41.0 13.4 %all-to-all-done.1.saved = bf16[16,288,128]{2,1,0:T(8,128)(2,1)S(1)} async-done(((bf16[16,288,128]{2,1,0:T(8,128)(2,1)}), bf16[16,288,128]{2,1,0:T(8,128)(2,1)S(1)}, u32[]{:S(2)}, u32[]{:S(2)}) %all-to-all-start.1) | async-done | bytes 1179680 | tf_op jit(solution)/shard_map/all_to_all | solution.py:296
  54.5 3.5 %upper.1 = (bf16[16,96,128]{2,1,0:T(8,128)(2,1)S(1)}, bf16[256,768]{1,0:T(8,128)(2,1)S(1)}, bf16[256,768]{1,0:T(8,128)(2,1)S(1)}, bf16[256,768]{1,0:T(8,128)(2,1)S(1)}, bf16[256,768]{1,0:T(8,128)(2,1)S(1)}) custom-call(s32[1]{0:T(128)} %bitcast.core_ref, bf16[16,288,128]{2,1,0:T(8,128)(2,1)S(1)} %all-to-all-done.1.saved, bf16[768,768]{1,0:T(8,128)(2,1)S(1)} %bitcast.20, ...), custom_call_target="tpu_custom_call" | custom-call | tf_op jit(solution)/shard_map/upper/pallas_call | solution.py:327
  58.0 11.0 %all_to_all.40.parts = bf16[16,96,128]{2,1,0:T(8,128)(2,1)S(1)} all-to-all(bf16[16,96,128]{2,1,0:T(8,128)(2,1)S(1)} %get-tuple-element.21), channel_id=1, replica_groups=mesh['segment'=2,'y'=4,'z'=16,'pair'=4] {'y','pair'}, dimensions={0} | all-to-all | bytes 786432 | tf_op jit(solution)/shard_map/all_to_all | solution.py:296
  69.2 30.5 %all_to_all.41 = bf16[16,24,128]{2,1,0:T(8,128)(2,1)S(1)} all-to-all(bf16[16,24,128]{2,1,0:T(8,128)(2,1)S(1)} %bitcast.28), channel_id=1, replica_groups=mesh['segment'=2,'y'=4,'z'=16,'pair'=4] {'z'}, dimensions={0} | all-to-all | bytes 196608 | tf_op jit(solution)/shard_map/all_to_all | solution.py:296
  100.5 15.1 %all_to_all.42 = bf16[16,24,128]{2,1,0:T(8,128)(2,1)S(1)} all-to-all(bf16[16,24,128]{2,1,0:T(8,128)(2,1)S(1)} %bitcast.30), channel_id=1, replica_groups=mesh['segment'=2,'y'=4,'z'=16,'pair'=4] {'z'}, dimensions={0} | all-to-all | bytes 196608 | tf_op jit(solution)/shard_map/all_to_all | solution.py:296
  115.9 11.6 %all_to_all.43.came = bf16[16,96,128]{2,1,0:T(8,128)(2,1)S(1)} all-to-all(bf16[16,96,128]{2,1,0:T(8,128)(2,1)S(1)} %spread1.1), channel_id=1, replica_groups=mesh['segment'=2,'y'=4,'z'=16,'pair'=4] {'y','pair'}, dimensions={0} | all-to-all | bytes 786432 | tf_op jit(solution)/shard_map/all_to_all | solution.py:296
  127.5 3.9 %lower.1 = (bf16[16,96,128]{2,1,0:T(8,128)(2,1)S(1)}, bf16[256,768]{1,0:T(8,128)(2,1)S(1)}, bf16[256,768]{1,0:T(8,128)(2,1)S(1)}, bf16[256,768]{1,0:T(8,128)(2,1...) custom-call(s32[1]{0:T(128)} %bitcast.core_ref, bf16[16,288,128]{2,1,0:T(8,128)(2,1)S(1)} %all-to-all-done.1.saved, ...), custom_call_target="tpu_custom_call" | custom-call | tf_op jit(solution)/shard_map/lower/pallas_call | solution.py:335
  132.2 7.6 %collective-permute-start.2 = (bf16[4,256,768]{2,1,0:T(8,128)(2,1)}, bf16[4,256,768]{2,1,0:T(8,128)(2,1)S(1)}, u32[]{:S(2)}, u32[]{:S(2)}) collective-permute-start(bf16[4,256,768]{2,1,0:T(8,128)(2,1)} %get-tuple-element.33), channel_id=1, source_target_pairs={{0,256},{256,0},{1,257},{257,1},{2,258},{258,2},{3,259},{259,3},{4... | collective-permute-start | bytes 4718600 | tf_op jit(solution)/shard_map/ppermute | solution.py:339
  139.7 12.3 %all_to_all.44.parts = bf16[16,96,128]{2,1,0:T(8,128)(2,1)S(1)} all-to-all(bf16[16,96,128]{2,1,0:T(8,128)(2,1)S(1)} %get-tuple-element.27), channel_id=1, replica_groups=mesh['segment'=2,'y'=4,'z'=16,'pair'=4] {'y','pair'}, dimensions={0} | all-to-all | bytes 786432 | tf_op jit(solution)/shard_map/all_to_all | solution.py:296
  152.9 3.5 %all-to-all-start.7 = ((bf16[16,24,128]{2,1,0:T(8,128)(2,1)}), bf16[16,24,128]{2,1,0:T(8,128)(2,1)S(1)}, u32[]{:S(2)}, u32[]{:S(2)}) async-start(bf16[16,24,128]{2,1,0:T(8,128)(2,1)} %bitcast.9), calls=%async_computation.7 | async-start | bytes 196608 | tf_op jit(solution)/shard_map/all_to_all | solution.py:296
  156.5 1.0 copy-done.9
  157.4 1.0 copy-done.11
  158.4 1.0 copy-done.13
  159.4 4.6 %weight.1 = (bf16[768,768]{1,0:T(8,128)(2,1)}, bf16[768,768]{1,0:T(8,128)(2,1)}, bf16[16,128]{1,0:T(8,128)(2,1)S(1)}) custom-call(bf16[256,768]{1,0:T(8,128)(2,1)S(1)} %copy-done.9, bf16[256,768]{1,0:T(8,128)(2,1)S(1)} %copy-done.11, bf16[256,768]{1,0:T(8,128)(2,1)S(1)} %copy-done.13, bf16[256,768]{1,0:T(8,128)(2,1)S(1)} %copy-done.15, ...), custom_call_target="tpu_custom_call" | custom-call | flops 2000000000 | bytes 6000000 | tf_op jit(solution)/shard_map/weight/pallas_call | solution.py:342
  164.1 4.1 %all-to-all-done.7 = bf16[16,24,128]{2,1,0:T(8,128)(2,1)S(1)} async-done(((bf16[16,24,128]{2,1,0:T(8,128)(2,1)}), bf16[16,24,128]{2,1,0:T(8,128)(2,1)S(1)}, u32[]{:S(2)}, u32[]{:S(2)}) %all-to-all-start.7) | async-done | bytes 98336 | tf_op jit(solution)/shard_map/all_to_all | solution.py:296
  168.6 4.7 %collective-permute-start.3 = (bf16[192,192]{1,0:T(8,128)(2,1)S(1)}, bf16[192,192]{1,0:T(8,128)(2,1)S(1)}, u32[]{:S(2)}, u32[]{:S(2)}) collective-permute-start(bf16[192,192]{1,0:T(8,128)(2,1)S(1)} %get-tuple-element.35), channel_id=1, source_target_pairs={{0,256},{256,0},{1,257},{257,1},{2,258},{258,2},{3,259},{259,3},{4... | collective-permute-start | bytes 221192 | tf_op jit(solution)/shard_map/ppermute | solution.py:350
  173.3 0.9 collective-permute-done.3
  (39 shorter events, 4.1 us)
Async XLA Ops:
  0.6 18.3 %copy-start = (bf16[1,1,768,768]{3,2,1,0:T(8,128)(2,1)S(1)}, bf16[1,1,768,768]{3,2,1,0:T(8,128)(2,1)}, u32[]{:S(2)}) copy-start(bf16[1,1,768,768]{3,2,1,0:T(8,128)(2,1)} %param.12) | copy-start | bytes 3538948
  3.2 29.5 %all-to-all-start = ((bf16[16,72,128]{2,1,0:T(8,128)(2,1)}), bf16[16,72,128]{2,1,0:T(8,128)(2,1)S(1)}, u32[]{:S(2)}, u32[]{:S(2)}) async-start(bf16[16,72,128]{2,1,0:T(8,128)(2,1)} %bitcast.31), calls=%async_computation | async-start | bytes 589824 | tf_op jit(solution)/shard_map/all_to_all | solution.py:296
  19.0 22.1 %collective-permute-start = (bf16[768,768]{1,0:T(8,128)(2,1)S(1)}, bf16[768,768]{1,0:T(8,128)(2,1)}, u32[]{:S(2)}, u32[]{:S(2)}) collective-permute-start(bf16[768,768]{1,0:T(8,128)(2,1)S(1)} %bitcast.19), channel_id=1, source_target_pairs={{0,256},{256,0},{1,257},{257,1},{2,258},{258,2},{3,259},{259,3},{4... | collective-permute-start | bytes 3538952 | tf_op jit(solution)/shard_map/ppermute | solution.py:312
  21.8 19.2 %collective-permute-start.1 = (bf16[768,768]{1,0:T(8,128)(2,1)}, bf16[768,768]{1,0:T(8,128)(2,1)}, u32[]{:S(2)}, u32[]{:S(2)}) collective-permute-start(bf16[768,768]{1,0:T(8,128)(2,1)} %bitcast.22), channel_id=1, source_target_pairs={{0,256},{256,0},{1,257},{257,1},{2,258},{258,2},{3,259},{259,3},{4... | collective-permute-start | bytes 3538952 | tf_op jit(solution)/shard_map/ppermute | solution.py:313
  34.1 20.4 %copy-start.1 = (bf16[1,1,768,768]{3,2,1,0:T(8,128)(2,1)S(1)}, bf16[1,1,768,768]{3,2,1,0:T(8,128)(2,1)}, u32[]{:S(2)}) copy-start(bf16[1,1,768,768]{3,2,1,0:T(8,128)(2,1)} %param.13) | copy-start | bytes 3538948
  34.1 20.4 %all-to-all-start.1 = ((bf16[16,288,128]{2,1,0:T(8,128)(2,1)}), bf16[16,288,128]{2,1,0:T(8,128)(2,1)S(1)}, u32[]{:S(2)}, u32[]{:S(2)}) async-start(bf16[16,288,128]{2,1,0:T(8,128)(2,1)} %spread3.1), calls=%async_computation.1 | async-start | bytes 2359296 | tf_op jit(solution)/shard_map/all_to_all | solution.py:296
  58.0 41.8 %copy-start.2 = (bf16[2,192,192]{2,1,0:T(8,128)(2,1)S(1)}, bf16[2,192,192]{2,1,0:T(8,128)(2,1)}, u32[]{:S(2)}) copy-start(bf16[2,192,192]{2,1,0:T(8,128)(2,1)} %cot.3) | copy-start | bytes 442372
  58.0 41.8 %copy-start.5 = (s32[2,2,192]{2,1,0:T(2,128)S(1)}, s32[2,2,192]{2,1,0:T(2,128)}, u32[]{:S(2)}) copy-start(s32[2,2,192]{2,1,0:T(2,128)} %owners.5) | copy-start | bytes 9220
  58.0 41.8 %copy-start.6 = (s32[2,2,192]{2,1,0:T(2,128)S(1)}, s32[2,2,192]{2,1,0:T(2,128)}, u32[]{:S(2)}) copy-start(s32[2,2,192]{2,1,0:T(2,128)} %slots.5) | copy-start | bytes 9220
  58.0 41.8 %copy-start.7 = (f32[2,2,192]{2,1,0:T(2,128)S(1)}, f32[2,2,192]{2,1,0:T(2,128)}, u32[]{:S(2)}) copy-start(f32[2,2,192]{2,1,0:T(2,128)} %gates.3) | copy-start | bytes 9220
  100.5 15.1 %copy-start.3 = (bf16[192,192]{1,0:T(8,128)(2,1)}, bf16[192,192]{1,0:T(8,128)(2,1)S(1)}, u32[]{:S(2)}) copy-start(bf16[192,192]{1,0:T(8,128)(2,1)S(1)} %get-tuple-element.28.above) | copy-start | bytes 221188
  131.4 0.7 copy-start.14
  132.2 20.7 %copy-start.8 = (bf16[256,768]{1,0:T(8,128)(2,1)}, bf16[256,768]{1,0:T(8,128)(2,1)S(1)}, u32[]{:S(2)}) copy-start(bf16[256,768]{1,0:T(8,128)(2,1)S(1)} %get-tuple-element.29.k0) | copy-start | bytes 1179652
  132.2 20.7 %copy-start.10 = (bf16[256,768]{1,0:T(8,128)(2,1)}, bf16[256,768]{1,0:T(8,128)(2,1)S(1)}, u32[]{:S(2)}) copy-start(bf16[256,768]{1,0:T(8,128)(2,1)S(1)} %get-tuple-element.30.k1) | copy-start | bytes 1179652
  132.2 20.7 %copy-start.12 = (bf16[256,768]{1,0:T(8,128)(2,1)}, bf16[256,768]{1,0:T(8,128)(2,1)S(1)}, u32[]{:S(2)}) copy-start(bf16[256,768]{1,0:T(8,128)(2,1)S(1)} %get-tuple-element.31.k2) | copy-start | bytes 1179652
  132.2 24.3 %copy-start.15 = (bf16[256,768]{1,0:T(8,128)(2,1)S(1)}, bf16[256,768]{1,0:T(8,128)(2,1)}, u32[]{:S(2)}) copy-start(bf16[256,768]{1,0:T(8,128)(2,1)} %copy-done.14) | copy-start | bytes 1179652
  132.2 24.3 %collective-permute-start.2 = (bf16[4,256,768]{2,1,0:T(8,128)(2,1)}, bf16[4,256,768]{2,1,0:T(8,128)(2,1)S(1)}, u32[]{:S(2)}, u32[]{:S(2)}) collective-permute-start(bf16[4,256,768]{2,1,0:T(8,128)(2,1)} %get-tuple-element.33), channel_id=1, source_target_pairs={{0,256},{256,0},{1,257},{257,1},{2,258},{258,2},{3,259},{259,3},{4... | collective-permute-start | bytes 4718600 | tf_op jit(solution)/shard_map/ppermute | solution.py:339
  152.9 15.3 %all-to-all-start.7 = ((bf16[16,24,128]{2,1,0:T(8,128)(2,1)}), bf16[16,24,128]{2,1,0:T(8,128)(2,1)S(1)}, u32[]{:S(2)}, u32[]{:S(2)}) async-start(bf16[16,24,128]{2,1,0:T(8,128)(2,1)} %bitcast.9), calls=%async_computation.7 | async-start | bytes 196608 | tf_op jit(solution)/shard_map/all_to_all | solution.py:296
  156.4 1.0 copy-start.9
  157.4 1.0 copy-start.11
  158.4 1.0 copy-start.13
  159.4 8.7 %copy-start.4 = (bf16[192,192]{1,0:T(8,128)(2,1)S(1)}, bf16[192,192]{1,0:T(8,128)(2,1)}, u32[]{:S(2)}) copy-start(bf16[192,192]{1,0:T(8,128)(2,1)} %copy-done.3) | copy-start | bytes 221188
  168.6 5.6 %collective-permute-start.3 = (bf16[192,192]{1,0:T(8,128)(2,1)S(1)}, bf16[192,192]{1,0:T(8,128)(2,1)S(1)}, u32[]{:S(2)}, u32[]{:S(2)}) collective-permute-start(bf16[192,192]{1,0:T(8,128)(2,1)S(1)} %get-tuple-element.35), channel_id=1, source_target_pairs={{0,256},{256,0},{1,257},{257,1},{2,258},{258,2},{3,259},{259,3},{4... | collective-permute-start | bytes 221192 | tf_op jit(solution)/shard_map/ppermute | solution.py:350

commit v4 on v3

--- a/solution.py
+++ b/solution.py
@@ -17,6 +17,7 @@
 TOK = 192
 SHARE = 192
 WIDTH = SHARE * NX
+FIRST = NZ // 2
 HID = 768
 LOW = 128
 ZROWS = NY * CAP + NY * CAP // 2
@@ -43,7 +44,7 @@
 
 
 def targets(owner, slot):
-    base = (owner & (NZ - 1)) * ZROWS
+    base = ((owner + FIRST) & (NZ - 1)) * ZROWS
     y = owner >> 4
     return base + y * CAP + slot, base + NY * CAP + y * 2 + (slot >> 1), slot & 1
 
@@ -292,16 +293,14 @@
     )
 
 
-def a2a(x, axis):
-    return lax.all_to_all(x, axis, split_axis=0, concat_axis=0, tiled=True)
-
-
 def over_z(x):
-    return a2a(x.reshape(NZ, -1, LOW), "z").reshape(-1, LOW)
+    ring = [[(FIRST + k) % NZ for k in range(NZ)]]
+    x = x.reshape(NZ, -1, LOW)
+    return lax.all_to_all(x, "z", 0, 0, axis_index_groups=ring, tiled=True).reshape(-1, LOW)
 
 
 def over_yx(x):
-    return a2a(x, ("y", "pair"))
+    return lax.all_to_all(x, ("y", "pair"), 0, 0, tiled=True)
 
 
 def body(acts, cotangent, gates, owners, slots, w_in, w_out):

time: 176 us -> 174 us (0.989)
  blocking collectives: 80.5 us -> 68.9 us
  starting transfers between devices: 43.2 us -> 53.7 us
    all_to_all x3, starting transfers between devices: 26.2 us -> 37.9 us  [the longest x2 31 us: over_z(): lax.all_to_all(x, 'z', 0, 0, axis_index_groups=ring, tiled=True)]
    all_to_all x5, blocking collectives: 80.5 us -> 68.9 us  [the longest x3 36.9 us: over_yx(): return lax.all_to_all(x, ('y', 'pair'), 0, 0, tiled=True)]
  transfers between devices with their start and end apart: 7 -> 7, of which waited for: 4 -> 3; matrix products, arithmetic and copies ran while one was open for 0% -> 0% of each run, Pallas kernels for 4% -> 4%
where the time goes in v4:
time: 174 us; the launch traced here: 173 us
  blocking collectives  68.9 us (40%)
  starting transfers between devices  53.7 us (31%)
  waiting for transfers between devices  26.6 us (15%)
  Pallas kernels  18.5 us (11%)
  local copies, waits for them, and re-layouts  3.77 us (2%)
    all_to_all x3, blocking collectives, over_yx(): return lax.all_to_all(x, ('y', 'pair'), 0, 0, tiled=True)  36.9 us
    all_to_all x2, blocking collectives, over_z(): lax.all_to_all(x, 'z', 0, 0, axis_index_groups=ring, tiled=True)  32 us
    all_to_all x2, starting transfers between devices, over_z(): lax.all_to_all(x, 'z', 0, 0, axis_index_groups=ring, tiled=True)  31 us
    all_to_all x1, waiting for transfers between devices, over_yx(): return lax.all_to_all(x, ('y', 'pair'), 0, 0, tiled=True)  17 us
    all_to_all x2, waiting for transfers between devices, over_z(): lax.all_to_all(x, 'z', 0, 0, axis_index_groups=ring, tiled=True)  8.67 us
    ppermute x1, starting transfers between devices, body(): came = lax.ppermute(give, 'segment', SWAP)  7.13 us
    all_to_all x1, starting transfers between devices, over_yx(): return lax.all_to_all(x, ('y', 'pair'), 0, 0, tiled=True)  6.89 us
    pallas_call x1, Pallas kernels, body(): call(weight_kernel, [HB] * 5, [(WIDTH, HID), (HID, WIDTH), (16, 128)], 'w...  4.62 us
  transfers between devices with their start and end apart: 7, of which 3 were waited for; matrix products, arithmetic and copies ran while one was open for 0% of the time, Pallas kernels for 4%

profile of v4, /device:TPU:1, one launch (start us, length us, event | category | flops | bytes accessed | tf_op | source)
XLA Modules:
  0.0 173.1 jit_solution(12341570907708419151)
XLA Ops:
  0.6 2.5 %start.1 = bf16[1152,128]{1,0:T(8,128)(2,1)} custom-call(s32[1]{0:T(128)} %bitcast.core_ref, bf16[2,2,192,192]{3,2,1,0:T(8,128)(2,1)} %acts.1, bf16[2,192,192]{2,1,0:T(8,128)(2,1)} %cot.3, f32[2,2,192]{2,1,0:T(2,128)} %gates.3, s32[2,2,192]{2,1,0:T(2,128)} %owners.5, s32[2,2,192]{2,1,0:T(2,128)} %slots.5), custom_call_target="tpu_custom_call" | custom-call | tf_op jit(solution)/shard_map/start/pallas_call | solution.py:316
  3.2 19.1 %all-to-all-start = ((bf16[16,72,128]{2,1,0:T(8,128)(2,1)}), bf16[16,72,128]{2,1,0:T(8,128)(2,1)S(1)}, u32[]{:S(2)}, u32[]{:S(2)}) async-start(bf16[16,72,128]{2,1,0:T(8,128)(2,1)} %bitcast.31), calls=%async_computation | async-start | bytes 589824 | tf_op jit(solution)/shard_map/all_to_all | solution.py:299
  22.3 3.1 %collective-permute-start = (bf16[768,768]{1,0:T(8,128)(2,1)S(1)}, bf16[768,768]{1,0:T(8,128)(2,1)}, u32[]{:S(2)}, u32[]{:S(2)}) collective-permute-start(bf16[768,768]{1,0:T(8,128)(2,1)S(1)} %bitcast.19), channel_id=1, source_target_pairs={{0,256},{256,0},{1,257},{257,1},{2,258},{258,2},{3,259},{259,3},{4... | collective-permute-start | bytes 3538952 | tf_op jit(solution)/shard_map/ppermute | solution.py:311
  25.5 1.9 %collective-permute-start.1 = (bf16[768,768]{1,0:T(8,128)(2,1)}, bf16[768,768]{1,0:T(8,128)(2,1)}, u32[]{:S(2)}, u32[]{:S(2)}) collective-permute-start(bf16[768,768]{1,0:T(8,128)(2,1)} %bitcast.22), channel_id=1, source_target_pairs={{0,256},{256,0},{1,257},{257,1},{2,258},{258,2},{3,259},{259,3},{4... | collective-permute-start | bytes 3538952 | tf_op jit(solution)/shard_map/ppermute | solution.py:312
  27.4 8.7 %all-to-all-done = bf16[16,72,128]{2,1,0:T(8,128)(2,1)S(1)} async-done(((bf16[16,72,128]{2,1,0:T(8,128)(2,1)}), bf16[16,72,128]{2,1,0:T(8,128)(2,1)S(1)}, u32[]{:S(2)}, u32[]{:S(2)}) %all-to-all-start) | async-done | bytes 294944 | tf_op jit(solution)/shard_map/all_to_all | solution.py:299
  36.1 1.4 spread3.1
  37.5 6.9 %all-to-all-start.1 = ((bf16[16,288,128]{2,1,0:T(8,128)(2,1)}), bf16[16,288,128]{2,1,0:T(8,128)(2,1)S(1)}, u32[]{:S(2)}, u32[]{:S(2)}) async-start(bf16[16,288,128]{2,1,0:T(8,128)(2,1)} %spread3.1), calls=%async_computation.1 | async-start | bytes 2359296 | tf_op jit(solution)/shard_map/all_to_all | solution.py:303
  44.4 17.0 %all-to-all-done.1.saved = bf16[16,288,128]{2,1,0:T(8,128)(2,1)S(1)} async-done(((bf16[16,288,128]{2,1,0:T(8,128)(2,1)}), bf16[16,288,128]{2,1,0:T(8,128)(2,1)S(1)}, u32[]{:S(2)}, u32[]{:S(2)}) %all-to-all-start.1) | async-done | bytes 1179680 | tf_op jit(solution)/shard_map/all_to_all | solution.py:303
  61.4 3.5 %upper.1 = (bf16[16,96,128]{2,1,0:T(8,128)(2,1)S(1)}, bf16[256,768]{1,0:T(8,128)(2,1)S(1)}, bf16[256,768]{1,0:T(8,128)(2,1)S(1)}, bf16[256,768]{1,0:T(8,128)(2,1)S(1)}, bf16[256,768]{1,0:T(8,128)(2,1)S(1)}) custom-call(s32[1]{0:T(128)} %bitcast.core_ref, bf16[16,288,128]{2,1,0:T(8,128)(2,1)S(1)} %all-to-all-done.1.saved, bf16[768,768]{1,0:T(8,128)(2,1)S(1)} %bitcast.20, ...), custom_call_target="tpu_custom_call" | custom-call | tf_op jit(solution)/shard_map/upper/pallas_call | solution.py:326
  65.0 13.0 %all_to_all.40.parts = bf16[16,96,128]{2,1,0:T(8,128)(2,1)S(1)} all-to-all(bf16[16,96,128]{2,1,0:T(8,128)(2,1)S(1)} %get-tuple-element.21), channel_id=1, replica_groups=mesh['segment'=2,'y'=4,'z'=16,'pair'=4] {'y','pair'}, dimensions={0} | all-to-all | bytes 786432 | tf_op jit(solution)/shard_map/all_to_all | solution.py:303
  78.3 16.9 %all_to_all.41 = bf16[16,24,128]{2,1,0:T(8,128)(2,1)S(1)} all-to-all(bf16[16,24,128]{2,1,0:T(8,128)(2,1)S(1)} %bitcast.28), channel_id=1, replica_groups={{32,36,40,44,48,52,56,60,0,4,8,12,16,20,24,28},{33,37,41,45,49,53,57,61..., dimensions={0} | all-to-all | bytes 196608 | tf_op jit(solution)/shard_map/all_to_all | solution.py:299
  95.9 15.1 %all_to_all.42 = bf16[16,24,128]{2,1,0:T(8,128)(2,1)S(1)} all-to-all(bf16[16,24,128]{2,1,0:T(8,128)(2,1)S(1)} %bitcast.30), channel_id=1, replica_groups={{32,36,40,44,48,52,56,60,0,4,8,12,16,20,24,28},{33,37,41,45,49,53,57,61..., dimensions={0} | all-to-all | bytes 196608 | tf_op jit(solution)/shard_map/all_to_all | solution.py:299
  111.3 11.6 %all_to_all.43.came = bf16[16,96,128]{2,1,0:T(8,128)(2,1)S(1)} all-to-all(bf16[16,96,128]{2,1,0:T(8,128)(2,1)S(1)} %spread1.1), channel_id=1, replica_groups=mesh['segment'=2,'y'=4,'z'=16,'pair'=4] {'y','pair'}, dimensions={0} | all-to-all | bytes 786432 | tf_op jit(solution)/shard_map/all_to_all | solution.py:303
  122.9 3.9 %lower.1 = (bf16[16,96,128]{2,1,0:T(8,128)(2,1)S(1)}, bf16[256,768]{1,0:T(8,128)(2,1)S(1)}, bf16[256,768]{1,0:T(8,128)(2,1)S(1)}, bf16[256,768]{1,0:T(8,128)(2,1...) custom-call(s32[1]{0:T(128)} %bitcast.core_ref, bf16[16,288,128]{2,1,0:T(8,128)(2,1)S(1)} %all-to-all-done.1.saved, ...), custom_call_target="tpu_custom_call" | custom-call | tf_op jit(solution)/shard_map/lower/pallas_call | solution.py:334
  127.5 7.1 %collective-permute-start.2 = (bf16[4,256,768]{2,1,0:T(8,128)(2,1)}, bf16[4,256,768]{2,1,0:T(8,128)(2,1)S(1)}, u32[]{:S(2)}, u32[]{:S(2)}) collective-permute-start(bf16[4,256,768]{2,1,0:T(8,128)(2,1)} %get-tuple-element.33), channel_id=1, source_target_pairs={{0,256},{256,0},{1,257},{257,1},{2,258},{258,2},{3,259},{259,3},{4... | collective-permute-start | bytes 4718600 | tf_op jit(solution)/shard_map/ppermute | solution.py:338
  134.7 12.3 %all_to_all.44.parts = bf16[16,96,128]{2,1,0:T(8,128)(2,1)S(1)} all-to-all(bf16[16,96,128]{2,1,0:T(8,128)(2,1)S(1)} %get-tuple-element.27), channel_id=1, replica_groups=mesh['segment'=2,'y'=4,'z'=16,'pair'=4] {'y','pair'}, dimensions={0} | all-to-all | bytes 786432 | tf_op jit(solution)/shard_map/all_to_all | solution.py:303
  146.9 0.9 gather.3
  147.8 11.9 %all-to-all-start.7 = ((bf16[16,24,128]{2,1,0:T(8,128)(2,1)}), bf16[16,24,128]{2,1,0:T(8,128)(2,1)S(1)}, u32[]{:S(2)}, u32[]{:S(2)}) async-start(bf16[16,24,128]{2,1,0:T(8,128)(2,1)} %bitcast.9), calls=%async_computation.7 | async-start | bytes 196608 | tf_op jit(solution)/shard_map/all_to_all | solution.py:299
  159.7 1.0 copy-done.9
  160.7 1.0 copy-done.11
  161.7 1.0 copy-done.13
  162.7 4.6 %weight.1 = (bf16[768,768]{1,0:T(8,128)(2,1)}, bf16[768,768]{1,0:T(8,128)(2,1)}, bf16[16,128]{1,0:T(8,128)(2,1)S(1)}) custom-call(bf16[256,768]{1,0:T(8,128)(2,1)S(1)} %copy-done.9, bf16[256,768]{1,0:T(8,128)(2,1)S(1)} %copy-done.11, bf16[256,768]{1,0:T(8,128)(2,1)S(1)} %copy-done.13, bf16[256,768]{1,0:T(8,128)(2,1)S(1)} %copy-done.15, ...), custom_call_target="tpu_custom_call" | custom-call | flops 2000000000 | bytes 6000000 | tf_op jit(solution)/shard_map/weight/pallas_call | solution.py:341
  167.8 3.6 %collective-permute-start.3 = (bf16[192,192]{1,0:T(8,128)(2,1)S(1)}, bf16[192,192]{1,0:T(8,128)(2,1)S(1)}, u32[]{:S(2)}, u32[]{:S(2)}) collective-permute-start(bf16[192,192]{1,0:T(8,128)(2,1)S(1)} %get-tuple-element.35), channel_id=1, source_target_pairs={{0,256},{256,0},{1,257},{257,1},{2,258},{258,2},{3,259},{259,3},{4... | collective-permute-start | bytes 221192 | tf_op jit(solution)/shard_map/ppermute | solution.py:349
  171.4 0.9 collective-permute-done.3
  (39 shorter events, 3.2 us)
Async XLA Ops:
  0.6 21.7 %copy-start = (bf16[1,1,768,768]{3,2,1,0:T(8,128)(2,1)S(1)}, bf16[1,1,768,768]{3,2,1,0:T(8,128)(2,1)}, u32[]{:S(2)}) copy-start(bf16[1,1,768,768]{3,2,1,0:T(8,128)(2,1)} %param.12) | copy-start | bytes 3538948
  3.2 32.9 %all-to-all-start = ((bf16[16,72,128]{2,1,0:T(8,128)(2,1)}), bf16[16,72,128]{2,1,0:T(8,128)(2,1)S(1)}, u32[]{:S(2)}, u32[]{:S(2)}) async-start(bf16[16,72,128]{2,1,0:T(8,128)(2,1)} %bitcast.31), calls=%async_computation | async-start | bytes 589824 | tf_op jit(solution)/shard_map/all_to_all | solution.py:299
  22.3 22.1 %collective-permute-start = (bf16[768,768]{1,0:T(8,128)(2,1)S(1)}, bf16[768,768]{1,0:T(8,128)(2,1)}, u32[]{:S(2)}, u32[]{:S(2)}) collective-permute-start(bf16[768,768]{1,0:T(8,128)(2,1)S(1)} %bitcast.19), channel_id=1, source_target_pairs={{0,256},{256,0},{1,257},{257,1},{2,258},{258,2},{3,259},{259,3},{4... | collective-permute-start | bytes 3538952 | tf_op jit(solution)/shard_map/ppermute | solution.py:311
  25.5 18.9 %collective-permute-start.1 = (bf16[768,768]{1,0:T(8,128)(2,1)}, bf16[768,768]{1,0:T(8,128)(2,1)}, u32[]{:S(2)}, u32[]{:S(2)}) collective-permute-start(bf16[768,768]{1,0:T(8,128)(2,1)} %bitcast.22), channel_id=1, source_target_pairs={{0,256},{256,0},{1,257},{257,1},{2,258},{258,2},{3,259},{259,3},{4... | collective-permute-start | bytes 3538952 | tf_op jit(solution)/shard_map/ppermute | solution.py:312
  37.5 23.9 %copy-start.1 = (bf16[1,1,768,768]{3,2,1,0:T(8,128)(2,1)S(1)}, bf16[1,1,768,768]{3,2,1,0:T(8,128)(2,1)}, u32[]{:S(2)}) copy-start(bf16[1,1,768,768]{3,2,1,0:T(8,128)(2,1)} %param.13) | copy-start | bytes 3538948
  37.5 23.9 %all-to-all-start.1 = ((bf16[16,288,128]{2,1,0:T(8,128)(2,1)}), bf16[16,288,128]{2,1,0:T(8,128)(2,1)S(1)}, u32[]{:S(2)}, u32[]{:S(2)}) async-start(bf16[16,288,128]{2,1,0:T(8,128)(2,1)} %spread3.1), calls=%async_computation.1 | async-start | bytes 2359296 | tf_op jit(solution)/shard_map/all_to_all | solution.py:303
  64.9 30.2 %copy-start.2 = (bf16[2,192,192]{2,1,0:T(8,128)(2,1)S(1)}, bf16[2,192,192]{2,1,0:T(8,128)(2,1)}, u32[]{:S(2)}) copy-start(bf16[2,192,192]{2,1,0:T(8,128)(2,1)} %cot.3) | copy-start | bytes 442372
  64.9 30.2 %copy-start.5 = (s32[2,2,192]{2,1,0:T(2,128)S(1)}, s32[2,2,192]{2,1,0:T(2,128)}, u32[]{:S(2)}) copy-start(s32[2,2,192]{2,1,0:T(2,128)} %owners.5) | copy-start | bytes 9220
  64.9 30.2 %copy-start.6 = (s32[2,2,192]{2,1,0:T(2,128)S(1)}, s32[2,2,192]{2,1,0:T(2,128)}, u32[]{:S(2)}) copy-start(s32[2,2,192]{2,1,0:T(2,128)} %slots.5) | copy-start | bytes 9220
  64.9 30.2 %copy-start.7 = (f32[2,2,192]{2,1,0:T(2,128)S(1)}, f32[2,2,192]{2,1,0:T(2,128)}, u32[]{:S(2)}) copy-start(f32[2,2,192]{2,1,0:T(2,128)} %gates.3) | copy-start | bytes 9220
  95.9 15.1 %copy-start.3 = (bf16[192,192]{1,0:T(8,128)(2,1)}, bf16[192,192]{1,0:T(8,128)(2,1)S(1)}, u32[]{:S(2)}) copy-start(bf16[192,192]{1,0:T(8,128)(2,1)S(1)} %get-tuple-element.28.above) | copy-start | bytes 221188
  126.8 0.7 copy-start.14
  127.5 20.3 %copy-start.8 = (bf16[256,768]{1,0:T(8,128)(2,1)}, bf16[256,768]{1,0:T(8,128)(2,1)S(1)}, u32[]{:S(2)}) copy-start(bf16[256,768]{1,0:T(8,128)(2,1)S(1)} %get-tuple-element.29.k0) | copy-start | bytes 1179652
  127.5 20.3 %copy-start.10 = (bf16[256,768]{1,0:T(8,128)(2,1)}, bf16[256,768]{1,0:T(8,128)(2,1)S(1)}, u32[]{:S(2)}) copy-start(bf16[256,768]{1,0:T(8,128)(2,1)S(1)} %get-tuple-element.30.k1) | copy-start | bytes 1179652
  127.5 20.3 %copy-start.12 = (bf16[256,768]{1,0:T(8,128)(2,1)}, bf16[256,768]{1,0:T(8,128)(2,1)S(1)}, u32[]{:S(2)}) copy-start(bf16[256,768]{1,0:T(8,128)(2,1)S(1)} %get-tuple-element.31.k2) | copy-start | bytes 1179652
  127.5 32.2 %copy-start.15 = (bf16[256,768]{1,0:T(8,128)(2,1)S(1)}, bf16[256,768]{1,0:T(8,128)(2,1)}, u32[]{:S(2)}) copy-start(bf16[256,768]{1,0:T(8,128)(2,1)} %copy-done.14) | copy-start | bytes 1179652
  127.5 32.2 %collective-permute-start.2 = (bf16[4,256,768]{2,1,0:T(8,128)(2,1)}, bf16[4,256,768]{2,1,0:T(8,128)(2,1)S(1)}, u32[]{:S(2)}, u32[]{:S(2)}) collective-permute-start(bf16[4,256,768]{2,1,0:T(8,128)(2,1)} %get-tuple-element.33), channel_id=1, source_target_pairs={{0,256},{256,0},{1,257},{257,1},{2,258},{258,2},{3,259},{259,3},{4... | collective-permute-start | bytes 4718600 | tf_op jit(solution)/shard_map/ppermute | solution.py:338
  147.8 19.5 %all-to-all-start.7 = ((bf16[16,24,128]{2,1,0:T(8,128)(2,1)}), bf16[16,24,128]{2,1,0:T(8,128)(2,1)S(1)}, u32[]{:S(2)}, u32[]{:S(2)}) async-start(bf16[16,24,128]{2,1,0:T(8,128)(2,1)} %bitcast.9), calls=%async_computation.7 | async-start | bytes 196608 | tf_op jit(solution)/shard_map/all_to_all | solution.py:299
  159.7 1.0 copy-start.9
  160.7 1.0 copy-start.11
  161.7 1.0 copy-start.13
  162.7 4.6 %copy-start.4 = (bf16[192,192]{1,0:T(8,128)(2,1)S(1)}, bf16[192,192]{1,0:T(8,128)(2,1)}, u32[]{:S(2)}) copy-start(bf16[192,192]{1,0:T(8,128)(2,1)} %copy-done.3) | copy-start | bytes 221188
  167.8 4.5 %collective-permute-start.3 = (bf16[192,192]{1,0:T(8,128)(2,1)S(1)}, bf16[192,192]{1,0:T(8,128)(2,1)S(1)}, u32[]{:S(2)}, u32[]{:S(2)}) collective-permute-start(bf16[192,192]{1,0:T(8,128)(2,1)S(1)} %get-tuple-element.35), channel_id=1, source_target_pairs={{0,256},{256,0},{1,257},{257,1},{2,258},{258,2},{3,259},{259,3},{4... | collective-permute-start | bytes 221192 | tf_op jit(solution)/shard_map/ppermute | solution.py:349

commit v5 on v4

--- a/solution.py
+++ b/solution.py
@@ -159,14 +159,14 @@
     inv = lax.rsqrt(jnp.mean(x * x, axis=1, keepdims=True) + 1e-06)
     normed = (x * inv).astype(BF)
     save(0, normed)
-    u = dot(normed, w_in[...])
+    u = dot(normed, w_in())
     square = u * u
     s = jnp.tanh(0.7978845608 * (u + 0.044715 * square * u))
     save(2, (0.5 * u * (1.0 + s)).astype(BF))
     slope = 0.5 * (1.0 + s) + 0.5 * u * (1.0 - s * s) * 0.7978845608 * (1.0 + 0.134145 * square)
-    back = (dot(grad, w_out[...], 1, 1) * slope).astype(BF)
+    back = (dot(grad, w_out(), 1, 1) * slope).astype(BF)
     save(1, back)
-    part = dot(back, w_in[...], 1, 1)
+    part = dot(back, w_in(), 1, 1)
     inner = jnp.sum(part * x, axis=1, keepdims=True)
     branch = (inv * part - (inv * inv * inv * inner * (1.0 / WIDTH)) * x).astype(BF)
     for j in range(NY):
@@ -179,25 +179,42 @@
             )
 
 
-def upper_kernel(core_ref, saved, own_in, other_in, own_out, other_out, out, *kept):
+def held(ref):
+    return lambda: ref[...]
+
+
+def fetched(source, buffer, sem):
+    copy = pltpu.make_async_copy(source, buffer, sem)
+    copy.start()
+    pending = [copy]
+
+    def value():
+        if pending:
+            pending.pop().wait()
+        return buffer[...]
+
+    return value
+
+
+def upper_kernel(core_ref, saved, own_in, other_in, own_out, other_out, out, k0, k1, k2, k3, in_buf, out_buf, sems):
     def run(w_in, w_out):
         def save(k, value):
-            kept[k][...] = value
+            (k0, k1, k2, k3)[k][...] = value
 
         expert_step(assemble(saved, 0).astype(F32), assemble(saved, YROWS), w_in, w_out, out, save)
 
     @pl.when(core_ref[0] == 1)
     def _():
-        run(own_in, own_out)
+        run(held(own_in), held(own_out))
 
     @pl.when(core_ref[0] != 1)
     def _():
-        run(other_in, other_out)
+        run(fetched(other_in, in_buf, sems.at[0]), fetched(other_out, out_buf, sems.at[1]))
 
 
 def lower_kernel(
     core_ref, saved, came, n1, b1, h1, g1, own_in, other_in, own_out, other_out,
-    out, k0, k1, k2, k3, give, kept, sems,
+    out, k0, k1, k2, k3, give, kept, in_buf, out_buf, sems,
 ):
     keep, above = (k0, k1, k2, k3), (n1, b1, h1, g1)
 
@@ -213,12 +230,13 @@
         def save(k, value):
             keep[k][...] = value
 
-        run(own_in, own_out, save)
+        run(held(own_in), held(own_out), save)
         for copy in copies:
             copy.wait()
 
     @pl.when(core_ref[0] != 0)
     def _():
+        w_in, w_out = fetched(other_in, in_buf, sems.at[4]), fetched(other_out, out_buf, sems.at[5])
         copies = [pltpu.make_async_copy(kept.at[k], give.at[k], sems.at[k]) for k in range(4)]
 
         def save(k, value):
@@ -226,7 +244,7 @@
             copies[k].start()
             keep[k][...] = above[k][...]
 
-        run(other_in, other_out, save)
+        run(w_in, w_out, save)
         for copy in copies:
             copy.wait()
 
@@ -251,7 +269,7 @@
         return copy
 
     stores = [product(0, 0, first), product(2, 1, second)]
-    mark[...] = jnp.zeros_like(mark)
+    mark[0] = 0
     for copy in stores:
         copy.wait()
 
@@ -285,7 +303,7 @@
         kernel,
         in_specs=list(ins),
         out_specs=places or [VM] * len(outs),
-        out_shape=[jax.ShapeDtypeStruct(o, BF) for o in outs],
+        out_shape=[o if hasattr(o, "dtype") else jax.ShapeDtypeStruct(o, BF) for o in outs],
         scratch_shapes=list(scratch),
         compiler_params=pltpu.CompilerParams(vmem_limit_bytes=mib << 20),
         cost_estimate=cost and pl.CostEstimate(flops=cost[0], bytes_accessed=cost[1], transcendentals=0),
@@ -323,7 +341,10 @@
     )
     saved = over_yx(sent)
     blocks, wide = (NY * NX, YROWS, LOW), (NY * NZ * CAP, WIDTH)
-    parts, *kept1 = call(upper_kernel, [SM] + [VM] * 5, [blocks] + [wide] * 4, "upper")(core, saved, *weights)
+    parts, *kept1 = call(
+        upper_kernel, [SM, VM] + [VM, HB] * 2, [blocks] + [wide] * 4, "upper",
+        [pltpu.VMEM((WIDTH, HID), BF), pltpu.VMEM((HID, WIDTH), BF), pltpu.SemaphoreType.DMA((2,))],
+    )(core, saved, *weights)
     (rows,) = call(gather_kernel, [VM], [(ALL, LOW)], "gather")(over_yx(parts))
     res1, packed = call(middle_kernel, [SM] + [VM] * 5, [(TOK, SHARE), (ALL, LOW)], "middle")(
         core, over_z(rows), cotangent, gates, owners, slots
@@ -332,18 +353,19 @@
         over_z(packed)
     )
     parts, *keep, give = call(
-        lower_kernel, [SM] + [VM] * 10, [blocks] + [wide] * 4 + [(4,) + wide], "lower",
-        [pltpu.VMEM((4,) + wide, BF), pltpu.SemaphoreType.DMA((4,))], places=[VM] * 5 + [HB],
+        lower_kernel, [SM] + [VM] * 6 + [VM, HB] * 2, [blocks] + [wide] * 4 + [(4,) + wide], "lower",
+        [pltpu.VMEM((4,) + wide, BF), pltpu.VMEM((WIDTH, HID), BF), pltpu.VMEM((HID, WIDTH), BF),
+         pltpu.SemaphoreType.DMA((6,))], places=[VM] * 5 + [HB],
     )(core, saved, over_yx(sent), *kept1, *weights)
     came = lax.ppermute(give, "segment", SWAP)
     (rows,) = call(gather_kernel, [VM], [(ALL, LOW)], "gather")(over_yx(parts))
 
     grad_in, grad_out, mark = call(
-        weight_kernel, [HB] * 5, [(WIDTH, HID), (HID, WIDTH), (16, 128)], "weight",
+        weight_kernel, [HB] * 5, [(WIDTH, HID), (HID, WIDTH), jax.ShapeDtypeStruct((1,), I32)], "weight",
         [pltpu.VMEM((4, 2 * NY * NZ * CAP, WIDTH), BF), pltpu.VMEM((2, WIDTH, HID), BF), pltpu.SemaphoreType.DMA((10,))],
-        mib=16, cost=(2 * 10**9, 6 * 10**6), places=[HB, HB, VM],
+        mib=56, cost=(2 * 10**9, 6 * 10**6), places=[HB, HB, SM],
     )(*keep, came)
-    mine, other = call(end_kernel, [SM] + [VM] * 5, [(TOK, SHARE)] * 2, "end")(
+    mine, other = call(end_kernel, [SM] + [VM] * 4 + [SM], [(TOK, SHARE)] * 2, "end")(
         core, over_z(rows), res1, owners, slots, mark
     )
     got = lax.ppermute(other, "segment", SWAP)

time: 174 us -> 170 us (0.977)
  local copies, waits for them, and re-layouts: 3.77 us -> 1.96 us
    unnamed x32 -> x26, local copies, waits for them, and re-layouts: 3.77 us -> 1.96 us
where the time goes in v5:
time: 170 us; the launch traced here: 169 us
  blocking collectives  67.2 us (40%)
  starting transfers between devices  53.5 us (31%)
  waiting for transfers between devices  26.6 us (16%)
  Pallas kernels  18 us (11%)
  local copies, waits for them, and re-layouts  1.96 us (1%)
    all_to_all x3, blocking collectives, over_yx(): return lax.all_to_all(x, ('y', 'pair'), 0, 0, tiled=True)  35.7 us
    all_to_all x2, blocking collectives, over_z(): lax.all_to_all(x, 'z', 0, 0, axis_index_groups=ring, tiled=True)  31.4 us
    all_to_all x2, starting transfers between devices, over_z(): lax.all_to_all(x, 'z', 0, 0, axis_index_groups=ring, tiled=True)  31 us
    all_to_all x1, waiting for transfers between devices, over_yx(): return lax.all_to_all(x, ('y', 'pair'), 0, 0, tiled=True)  17 us
    all_to_all x2, waiting for transfers between devices, over_z(): lax.all_to_all(x, 'z', 0, 0, axis_index_groups=ring, tiled=True)  8.67 us
    ppermute x1, starting transfers between devices, body(): came = lax.ppermute(give, 'segment', SWAP)  7 us
    all_to_all x1, starting transfers between devices, over_yx(): return lax.all_to_all(x, ('y', 'pair'), 0, 0, tiled=True)  6.89 us
    pallas_call x1, Pallas kernels, body(): call(weight_kernel, [HB] * 5, [(WIDTH, HID), (HID, WIDTH), jax.ShapeDtype...  5.02 us
  transfers between devices with their start and end apart: 7, of which 3 were waited for; matrix products, arithmetic and copies ran while one was open for 0% of the time, Pallas kernels for 4%

profile of v5, /device:TPU:1, one launch (start us, length us, event | category | flops | bytes accessed | tf_op | source)
XLA Modules:
  0.0 168.9 jit_solution(2312432902503177793)
XLA Ops:
  0.6 2.5 %start.1 = bf16[1152,128]{1,0:T(8,128)(2,1)} custom-call(s32[1]{0:T(128)} %bitcast.core_ref, bf16[2,2,192,192]{3,2,1,0:T(8,128)(2,1)} %acts.1, bf16[2,192,192]{2,1,0:T(8,128)(2,1)} %cot.3, f32[2,2,192]{2,1,0:T(2,128)} %gates.3, s32[2,2,192]{2,1,0:T(2,128)} %owners.5, s32[2,2,192]{2,1,0:T(2,128)} %slots.5), custom_call_target="tpu_custom_call" | custom-call | tf_op jit(solution)/shard_map/start/pallas_call | solution.py:334
  3.2 19.1 %all-to-all-start = ((bf16[16,72,128]{2,1,0:T(8,128)(2,1)}), bf16[16,72,128]{2,1,0:T(8,128)(2,1)S(1)}, u32[]{:S(2)}, u32[]{:S(2)}) async-start(bf16[16,72,128]{2,1,0:T(8,128)(2,1)} %bitcast.31), calls=%async_computation | async-start | bytes 589824 | tf_op jit(solution)/shard_map/all_to_all | solution.py:317
  22.3 3.1 %collective-permute-start = (bf16[768,768]{1,0:T(8,128)(2,1)S(1)}, bf16[768,768]{1,0:T(8,128)(2,1)}, u32[]{:S(2)}, u32[]{:S(2)}) collective-permute-start(bf16[768,768]{1,0:T(8,128)(2,1)S(1)} %bitcast.19), channel_id=1, source_target_pairs={{0,256},{256,0},{1,257},{257,1},{2,258},{258,2},{3,259},{259,3},{4... | collective-permute-start | bytes 3538952 | tf_op jit(solution)/shard_map/ppermute | solution.py:329
  25.5 1.9 %collective-permute-start.1 = (bf16[768,768]{1,0:T(8,128)(2,1)}, bf16[768,768]{1,0:T(8,128)(2,1)}, u32[]{:S(2)}, u32[]{:S(2)}) collective-permute-start(bf16[768,768]{1,0:T(8,128)(2,1)} %bitcast.22), channel_id=1, source_target_pairs={{0,256},{256,0},{1,257},{257,1},{2,258},{258,2},{3,259},{259,3},{4... | collective-permute-start | bytes 3538952 | tf_op jit(solution)/shard_map/ppermute | solution.py:330
  27.4 8.7 %all-to-all-done = bf16[16,72,128]{2,1,0:T(8,128)(2,1)S(1)} async-done(((bf16[16,72,128]{2,1,0:T(8,128)(2,1)}), bf16[16,72,128]{2,1,0:T(8,128)(2,1)S(1)}, u32[]{:S(2)}, u32[]{:S(2)}) %all-to-all-start) | async-done | bytes 294944 | tf_op jit(solution)/shard_map/all_to_all | solution.py:317
  36.1 1.4 spread3.1
  37.5 6.9 %all-to-all-start.1 = ((bf16[16,288,128]{2,1,0:T(8,128)(2,1)}), bf16[16,288,128]{2,1,0:T(8,128)(2,1)S(1)}, u32[]{:S(2)}, u32[]{:S(2)}) async-start(bf16[16,288,128]{2,1,0:T(8,128)(2,1)} %spread3.1), calls=%async_computation.1 | async-start | bytes 2359296 | tf_op jit(solution)/shard_map/all_to_all | solution.py:321
  44.4 17.0 %all-to-all-done.1.saved = bf16[16,288,128]{2,1,0:T(8,128)(2,1)S(1)} async-done(((bf16[16,288,128]{2,1,0:T(8,128)(2,1)}), bf16[16,288,128]{2,1,0:T(8,128)(2,1)S(1)}, u32[]{:S(2)}, u32[]{:S(2)}) %all-to-all-start.1) | async-done | bytes 1179680 | tf_op jit(solution)/shard_map/all_to_all | solution.py:321
  61.4 1.9 %upper.1 = (bf16[16,96,128]{2,1,0:T(8,128)(2,1)S(1)}, bf16[256,768]{1,0:T(8,128)(2,1)S(1)}, bf16[256,768]{1,0:T(8,128)(2,1)S(1)}, bf16[256,768]{1,0:T(8,128)(2,1)S(1)}, bf16[256,768]{1,0:T(8,128)(2,1)S(1)}) custom-call(s32[1]{0:T(128)} %bitcast.core_ref, bf16[16,288,128]{2,1,0:T(8,128)(2,1)S(1)} %all-to-all-done.1.saved, bf16[768,768]{1,0:T(8,128)(2,1)S(1)} %bitcast.20, ...), custom_call_target="tpu_custom_call" | custom-call | tf_op jit(solution)/shard_map/upper/pallas_call | solution.py:344
  63.3 12.6 %all_to_all.40.parts = bf16[16,96,128]{2,1,0:T(8,128)(2,1)S(1)} all-to-all(bf16[16,96,128]{2,1,0:T(8,128)(2,1)S(1)} %get-tuple-element.21), channel_id=1, replica_groups=mesh['segment'=2,'y'=4,'z'=16,'pair'=4] {'y','pair'}, dimensions={0} | all-to-all | bytes 786432 | tf_op jit(solution)/shard_map/all_to_all | solution.py:321
  76.2 16.3 %all_to_all.41 = bf16[16,24,128]{2,1,0:T(8,128)(2,1)S(1)} all-to-all(bf16[16,24,128]{2,1,0:T(8,128)(2,1)S(1)} %bitcast.28), channel_id=1, replica_groups={{32,36,40,44,48,52,56,60,0,4,8,12,16,20,24,28},{33,37,41,45,49,53,57,61..., dimensions={0} | all-to-all | bytes 196608 | tf_op jit(solution)/shard_map/all_to_all | solution.py:317
  93.3 15.1 %all_to_all.42 = bf16[16,24,128]{2,1,0:T(8,128)(2,1)S(1)} all-to-all(bf16[16,24,128]{2,1,0:T(8,128)(2,1)S(1)} %bitcast.30), channel_id=1, replica_groups={{32,36,40,44,48,52,56,60,0,4,8,12,16,20,24,28},{33,37,41,45,49,53,57,61..., dimensions={0} | all-to-all | bytes 196608 | tf_op jit(solution)/shard_map/all_to_all | solution.py:317
  108.7 10.9 %all_to_all.43.came = bf16[16,96,128]{2,1,0:T(8,128)(2,1)S(1)} all-to-all(bf16[16,96,128]{2,1,0:T(8,128)(2,1)S(1)} %spread1.1), channel_id=1, replica_groups=mesh['segment'=2,'y'=4,'z'=16,'pair'=4] {'y','pair'}, dimensions={0} | all-to-all | bytes 786432 | tf_op jit(solution)/shard_map/all_to_all | solution.py:321
  119.6 4.0 %lower.1 = (bf16[16,96,128]{2,1,0:T(8,128)(2,1)S(1)}, bf16[256,768]{1,0:T(8,128)(2,1)S(1)}, bf16[256,768]{1,0:T(8,128)(2,1)S(1)}, bf16[256,768]{1,0:T(8,128)(2,1...) custom-call(s32[1]{0:T(128)} %bitcast.core_ref, bf16[16,288,128]{2,1,0:T(8,128)(2,1)S(1)} %all-to-all-done.1.saved, ...), custom_call_target="tpu_custom_call" | custom-call | tf_op jit(solution)/shard_map/lower/pallas_call | solution.py:355
  123.6 0.7 copy-done.11
  124.3 7.0 %collective-permute-start.2 = (bf16[4,256,768]{2,1,0:T(8,128)(2,1)}, bf16[4,256,768]{2,1,0:T(8,128)(2,1)S(1)}, u32[]{:S(2)}, u32[]{:S(2)}) collective-permute-start(bf16[4,256,768]{2,1,0:T(8,128)(2,1)} %get-tuple-element.33), channel_id=1, source_target_pairs={{0,256},{256,0},{1,257},{257,1},{2,258},{258,2},{3,259},{259,3},{4... | collective-permute-start | bytes 4718600 | tf_op jit(solution)/shard_map/ppermute | solution.py:360
  131.3 12.3 %all_to_all.44.parts = bf16[16,96,128]{2,1,0:T(8,128)(2,1)S(1)} all-to-all(bf16[16,96,128]{2,1,0:T(8,128)(2,1)S(1)} %get-tuple-element.27), channel_id=1, replica_groups=mesh['segment'=2,'y'=4,'z'=16,'pair'=4] {'y','pair'}, dimensions={0} | all-to-all | bytes 786432 | tf_op jit(solution)/shard_map/all_to_all | solution.py:321
  143.6 0.9 gather.3
  144.5 11.8 %all-to-all-start.7 = ((bf16[16,24,128]{2,1,0:T(8,128)(2,1)}), bf16[16,24,128]{2,1,0:T(8,128)(2,1)S(1)}, u32[]{:S(2)}, u32[]{:S(2)}) async-start(bf16[16,24,128]{2,1,0:T(8,128)(2,1)} %bitcast.9), calls=%async_computation.7 | async-start | bytes 196608 | tf_op jit(solution)/shard_map/all_to_all | solution.py:317
  156.3 1.2 copy-done.12
  157.5 5.0 %weight.1 = (bf16[768,768]{1,0:T(8,128)(2,1)}, bf16[768,768]{1,0:T(8,128)(2,1)}, s32[1]{0:T(128)}) custom-call(bf16[256,768]{1,0:T(8,128)(2,1)} %copy-done.8, bf16[256,768]{1,0:T(8,128)(2,1)} %copy-done.9, bf16[256,768]{1,0:T(8,128)(2,1)} %copy-done.10, bf16[256,768]{1,0:T(8,128)(2,1)} %copy-done.11, bf16[4,256,768]{2,1,0:T(8,128)(2,1)} %copy-done.12), custom_call_target="tpu_custom_call" | custom-call | flops 2000000000 | bytes 6000000 | tf_op jit(solution)/shard_map/weight/pallas_call | solution.py:363
  162.5 1.0 end.1
  163.6 3.6 %collective-permute-start.3 = (bf16[192,192]{1,0:T(8,128)(2,1)S(1)}, bf16[192,192]{1,0:T(8,128)(2,1)S(1)}, u32[]{:S(2)}, u32[]{:S(2)}) collective-permute-start(bf16[192,192]{1,0:T(8,128)(2,1)S(1)} %get-tuple-element.35), channel_id=1, source_target_pairs={{0,256},{256,0},{1,257},{257,1},{2,258},{258,2},{3,259},{259,3},{4... | collective-permute-start | bytes 221192 | tf_op jit(solution)/shard_map/ppermute | solution.py:371
  167.2 0.9 collective-permute-done.3
  (33 shorter events, 2.0 us)
Async XLA Ops:
  0.6 21.7 %copy-start = (bf16[1,1,768,768]{3,2,1,0:T(8,128)(2,1)S(1)}, bf16[1,1,768,768]{3,2,1,0:T(8,128)(2,1)}, u32[]{:S(2)}) copy-start(bf16[1,1,768,768]{3,2,1,0:T(8,128)(2,1)} %param.12) | copy-start | bytes 3538948
  3.2 32.9 %all-to-all-start = ((bf16[16,72,128]{2,1,0:T(8,128)(2,1)}), bf16[16,72,128]{2,1,0:T(8,128)(2,1)S(1)}, u32[]{:S(2)}, u32[]{:S(2)}) async-start(bf16[16,72,128]{2,1,0:T(8,128)(2,1)} %bitcast.31), calls=%async_computation | async-start | bytes 589824 | tf_op jit(solution)/shard_map/all_to_all | solution.py:317
  22.3 22.1 %collective-permute-start = (bf16[768,768]{1,0:T(8,128)(2,1)S(1)}, bf16[768,768]{1,0:T(8,128)(2,1)}, u32[]{:S(2)}, u32[]{:S(2)}) collective-permute-start(bf16[768,768]{1,0:T(8,128)(2,1)S(1)} %bitcast.19), channel_id=1, source_target_pairs={{0,256},{256,0},{1,257},{257,1},{2,258},{258,2},{3,259},{259,3},{4... | collective-permute-start | bytes 3538952 | tf_op jit(solution)/shard_map/ppermute | solution.py:329
  25.5 18.9 %collective-permute-start.1 = (bf16[768,768]{1,0:T(8,128)(2,1)}, bf16[768,768]{1,0:T(8,128)(2,1)}, u32[]{:S(2)}, u32[]{:S(2)}) collective-permute-start(bf16[768,768]{1,0:T(8,128)(2,1)} %bitcast.22), channel_id=1, source_target_pairs={{0,256},{256,0},{1,257},{257,1},{2,258},{258,2},{3,259},{259,3},{4... | collective-permute-start | bytes 3538952 | tf_op jit(solution)/shard_map/ppermute | solution.py:330
  37.5 23.9 %copy-start.1 = (bf16[1,1,768,768]{3,2,1,0:T(8,128)(2,1)S(1)}, bf16[1,1,768,768]{3,2,1,0:T(8,128)(2,1)}, u32[]{:S(2)}) copy-start(bf16[1,1,768,768]{3,2,1,0:T(8,128)(2,1)} %param.13) | copy-start | bytes 3538948
  37.5 23.9 %all-to-all-start.1 = ((bf16[16,288,128]{2,1,0:T(8,128)(2,1)}), bf16[16,288,128]{2,1,0:T(8,128)(2,1)S(1)}, u32[]{:S(2)}, u32[]{:S(2)}) async-start(bf16[16,288,128]{2,1,0:T(8,128)(2,1)} %spread3.1), calls=%async_computation.1 | async-start | bytes 2359296 | tf_op jit(solution)/shard_map/all_to_all | solution.py:321
  63.3 29.3 %copy-start.2 = (bf16[2,192,192]{2,1,0:T(8,128)(2,1)S(1)}, bf16[2,192,192]{2,1,0:T(8,128)(2,1)}, u32[]{:S(2)}) copy-start(bf16[2,192,192]{2,1,0:T(8,128)(2,1)} %cot.3) | copy-start | bytes 442372
  63.3 29.2 %copy-start.5 = (s32[2,2,192]{2,1,0:T(2,128)S(1)}, s32[2,2,192]{2,1,0:T(2,128)}, u32[]{:S(2)}) copy-start(s32[2,2,192]{2,1,0:T(2,128)} %owners.5) | copy-start | bytes 9220
  63.3 29.2 %copy-start.6 = (s32[2,2,192]{2,1,0:T(2,128)S(1)}, s32[2,2,192]{2,1,0:T(2,128)}, u32[]{:S(2)}) copy-start(s32[2,2,192]{2,1,0:T(2,128)} %slots.5) | copy-start | bytes 9220
  63.3 29.2 %copy-start.7 = (f32[2,2,192]{2,1,0:T(2,128)S(1)}, f32[2,2,192]{2,1,0:T(2,128)}, u32[]{:S(2)}) copy-start(f32[2,2,192]{2,1,0:T(2,128)} %gates.3) | copy-start | bytes 9220
  93.3 15.1 %copy-start.3 = (bf16[192,192]{1,0:T(8,128)(2,1)}, bf16[192,192]{1,0:T(8,128)(2,1)S(1)}, u32[]{:S(2)}) copy-start(bf16[192,192]{1,0:T(8,128)(2,1)S(1)} %get-tuple-element.28.above) | copy-start | bytes 221188
  123.6 0.7 copy-start.11
  124.3 20.2 %copy-start.8 = (bf16[256,768]{1,0:T(8,128)(2,1)}, bf16[256,768]{1,0:T(8,128)(2,1)S(1)}, u32[]{:S(2)}) copy-start(bf16[256,768]{1,0:T(8,128)(2,1)S(1)} %get-tuple-element.29.k0) | copy-start | bytes 1179652
  124.3 20.2 %copy-start.9 = (bf16[256,768]{1,0:T(8,128)(2,1)}, bf16[256,768]{1,0:T(8,128)(2,1)S(1)}, u32[]{:S(2)}) copy-start(bf16[256,768]{1,0:T(8,128)(2,1)S(1)} %get-tuple-element.30.k1) | copy-start | bytes 1179652
  124.3 20.2 %copy-start.10 = (bf16[256,768]{1,0:T(8,128)(2,1)}, bf16[256,768]{1,0:T(8,128)(2,1)S(1)}, u32[]{:S(2)}) copy-start(bf16[256,768]{1,0:T(8,128)(2,1)S(1)} %get-tuple-element.31.k2) | copy-start | bytes 1179652
  124.3 32.0 %collective-permute-start.2 = (bf16[4,256,768]{2,1,0:T(8,128)(2,1)}, bf16[4,256,768]{2,1,0:T(8,128)(2,1)S(1)}, u32[]{:S(2)}, u32[]{:S(2)}) collective-permute-start(bf16[4,256,768]{2,1,0:T(8,128)(2,1)} %get-tuple-element.33), channel_id=1, source_target_pairs={{0,256},{256,0},{1,257},{257,1},{2,258},{258,2},{3,259},{259,3},{4... | collective-permute-start | bytes 4718600 | tf_op jit(solution)/shard_map/ppermute | solution.py:360
  144.5 18.0 %all-to-all-start.7 = ((bf16[16,24,128]{2,1,0:T(8,128)(2,1)}), bf16[16,24,128]{2,1,0:T(8,128)(2,1)S(1)}, u32[]{:S(2)}, u32[]{:S(2)}) async-start(bf16[16,24,128]{2,1,0:T(8,128)(2,1)} %bitcast.9), calls=%async_computation.7 | async-start | bytes 196608 | tf_op jit(solution)/shard_map/all_to_all | solution.py:317
  156.3 1.2 copy-start.12
  157.5 5.0 %copy-start.4 = (bf16[192,192]{1,0:T(8,128)(2,1)S(1)}, bf16[192,192]{1,0:T(8,128)(2,1)}, u32[]{:S(2)}) copy-start(bf16[192,192]{1,0:T(8,128)(2,1)} %copy-done.3) | copy-start | bytes 221188
  163.6 4.5 %collective-permute-start.3 = (bf16[192,192]{1,0:T(8,128)(2,1)S(1)}, bf16[192,192]{1,0:T(8,128)(2,1)S(1)}, u32[]{:S(2)}, u32[]{:S(2)}) collective-permute-start(bf16[192,192]{1,0:T(8,128)(2,1)S(1)} %get-tuple-element.35), channel_id=1, source_target_pairs={{0,256},{256,0},{1,257},{257,1},{2,258},{258,2},{3,259},{259,3},{4... | collective-permute-start | bytes 221192 | tf_op jit(solution)/shard_map/ppermute | solution.py:371

commit v6 on v5

--- a/solution.py
+++ b/solution.py
@@ -22,6 +22,7 @@
 LOW = 128
 ZROWS = NY * CAP + NY * CAP // 2
 YROWS = NZ * CAP + NZ * CAP // 2
+CUTS = 4
 ALL = NZ * ZROWS
 
 
@@ -49,12 +50,17 @@
     return base + y * CAP + slot, base + NY * CAP + y * 2 + (slot >> 1), slot & 1
 
 
-def pack(values, owner, slot):
+def routes(owner, slot):
     low_at, high_at, odd = targets(owner, slot)
     at = iota((ALL, TOK), 0)
     low = hot(at == low_at)
     even_hot = hot((at == high_at) & (odd == 0))
     odd_hot = hot((at == high_at) & (odd == 1))
+    return low, even_hot, odd_hot
+
+
+def pack(values, hots):
+    low, even_hot, odd_hot = hots
     out = []
     for v in values:
         high = v[:, LOW:]
@@ -98,31 +104,50 @@
     ]
     for copy in copies:
         copy.start()
-    for copy in copies:
+    copies[0].wait()
+    copies[1].wait()
+    upper = routes(row_of(owner_v, 1, core), row_of(slot_v, 1, core))
+    lower = routes(row_of(owner_v, 0, core), row_of(slot_v, 0, core))
+    for copy in copies[2:]:
         copy.wait()
     gate = column(row_of(gate_v, 1, core))
     scaled = (gate * tok[0].astype(F32)).astype(BF)
-    first = pack([tok[1], scaled], row_of(owner_v, 1, core), row_of(slot_v, 1, core))
-    second = pack([tok[2]], row_of(owner_v, 0, core), row_of(slot_v, 0, core))
+    first = pack([tok[1], scaled], upper)
+    second = pack([tok[2]], lower)
     parts = [p.reshape(NZ, ZROWS, LOW) for p in first + second]
     out[...] = jnp.concatenate(parts, axis=1).reshape(3 * ALL, LOW).astype(BF)
 
 
-def spread_kernel(count, rows, out):
+def spread_move():
     shape = (NY, YROWS, ALL)
     y, k, at = iota(shape, 0), iota(shape, 1), iota(shape, 2)
     z = (k & 31) >> 1
     half = k & 1
     low = z * ZROWS + y * CAP + half * 2 + (k >> 5)
     high = z * ZROWS + NY * CAP + y * 2 + half
-    move = hot((at == jnp.where(k < NZ * CAP, low, high)).reshape(ALL, ALL))
-    value = rows[...].astype(F32).reshape(NZ, count * ZROWS, LOW)
-    for a in range(count):
+    return hot((at == jnp.where(k < NZ * CAP, low, high)).reshape(ALL, ALL))
+
+
+def spread_kernel(rows, out):
+    moved = dot(spread_move(), rows[...]).astype(BF)
+    for j in range(NY):
+        for i in range(NX):
+            out[j * NX + i] = moved[j * YROWS : (j + 1) * YROWS]
+
+
+def spread3_kernel(rows, out, moved, sems):
+    move = spread_move()
+    value = rows[...].astype(F32).reshape(NZ, 3 * ZROWS, LOW)
+    copies = []
+    for a in range(3):
         part = value[:, a * ZROWS : (a + 1) * ZROWS].reshape(ALL, LOW).astype(BF)
-        moved = dot(move, part).astype(BF)
-        for j in range(NY):
-            for i in range(NX):
-                out[j * NX + i, a * YROWS : (a + 1) * YROWS, :] = moved[j * YROWS : (j + 1) * YROWS]
+        moved[a] = dot(move, part).astype(BF).reshape(NY, YROWS, LOW)
+        for i in range(NX):
+            copy = pltpu.make_async_copy(moved.at[a], out.at[:, i, a * YROWS : (a + 1) * YROWS], sems.at[a, i])
+            copy.start()
+            copies.append(copy)
+    for copy in copies:
+        copy.wait()
 
 
 def gather_kernel(parts, out):
@@ -183,14 +208,18 @@
     return lambda: ref[...]
 
 
-def fetched(source, buffer, sem):
-    copy = pltpu.make_async_copy(source, buffer, sem)
-    copy.start()
-    pending = [copy]
+def fetched(source, buffer, sems):
+    step = WIDTH // CUTS
+    copies = [
+        pltpu.make_async_copy(source.at[k * step : (k + 1) * step], buffer.at[k * step : (k + 1) * step], sems.at[k])
+        for k in range(CUTS)
+    ]
+    for copy in copies:
+        copy.start()
 
     def value():
-        if pending:
-            pending.pop().wait()
+        while copies:
+            copies.pop(0).wait()
         return buffer[...]
 
     return value
@@ -214,7 +243,7 @@
 
 def lower_kernel(
     core_ref, saved, came, n1, b1, h1, g1, own_in, other_in, own_out, other_out,
-    out, k0, k1, k2, k3, give, kept, in_buf, out_buf, sems,
+    out, k0, k1, k2, k3, give, kept, in_buf, out_buf, sems, more,
 ):
     keep, above = (k0, k1, k2, k3), (n1, b1, h1, g1)
 
@@ -236,7 +265,7 @@
 
     @pl.when(core_ref[0] != 0)
     def _():
-        w_in, w_out = fetched(other_in, in_buf, sems.at[4]), fetched(other_out, out_buf, sems.at[5])
+        w_in, w_out = fetched(other_in, in_buf, more.at[0]), fetched(other_out, out_buf, more.at[1])
         copies = [pltpu.make_async_copy(kept.at[k], give.at[k], sems.at[k]) for k in range(4)]
 
         def save(k, value):
@@ -249,7 +278,7 @@
             copy.wait()
 
 
-def weight_kernel(k0, k1, k2, k3, came, first, second, mark, rows, sums, sems):
+def weight_kernel(k0, k1, k2, k3, came, first, second, rows, sums, sems):
     half = NY * NZ * CAP
     loads = [
         [pltpu.make_async_copy(src, rows.at[k, n * half : (n + 1) * half], sems.at[2 * k + n])
@@ -269,7 +298,6 @@
         return copy
 
     stores = [product(0, 0, first), product(2, 1, second)]
-    mark[0] = 0
     for copy in stores:
         copy.wait()
 
@@ -281,11 +309,11 @@
     result[...] = res
     gate = column(row_of(gates, 0, core))
     scaled = (gate * res.astype(F32)).astype(BF)
-    (packed,) = pack([scaled], row_of(owners, 0, core), row_of(slots, 0, core))
+    (packed,) = pack([scaled], routes(row_of(owners, 0, core), row_of(slots, 0, core)))
     out[...] = packed.astype(BF)
 
 
-def end_kernel(core_ref, rows, above, owners, slots, mark, keep, give):
+def end_kernel(core_ref, rows, above, owners, slots, grad_in, keep, give, same):
     core = core_ref[0]
     branch = unpack(rows[...], row_of(owners, 0, core), row_of(slots, 0, core))
     res = (above[...].astype(F32) + branch).astype(BF)
@@ -298,7 +326,7 @@
 HB = pl.BlockSpec(memory_space=pltpu.HBM)
 
 
-def call(kernel, ins, outs, name, scratch=(), mib=16, cost=None, places=None):
+def call(kernel, ins, outs, name, scratch=(), mib=16, cost=None, places=None, alias=None):
     return pl.pallas_call(
         kernel,
         in_specs=list(ins),
@@ -307,6 +335,7 @@
         scratch_shapes=list(scratch),
         compiler_params=pltpu.CompilerParams(vmem_limit_bytes=mib << 20),
         cost_estimate=cost and pl.CostEstimate(flops=cost[0], bytes_accessed=cost[1], transcendentals=0),
+        input_output_aliases=alias or {},
         name=name,
     )
 
@@ -336,38 +365,40 @@
         [pltpu.VMEM((3, TOK, SHARE), BF), pltpu.VMEM(table, F32), pltpu.VMEM(table, I32),
          pltpu.VMEM(table, I32), pltpu.SemaphoreType.DMA((6,))], mib=60,
     )(core, acts, cotangent, gates, owners, slots)
-    (sent,) = call(functools.partial(spread_kernel, 3), [VM], [(NY * NX, 3 * YROWS, LOW)], "spread3", mib=16)(
-        over_z(packed)
-    )
-    saved = over_yx(sent)
+    (sent,) = call(
+        spread3_kernel, [VM], [(NY, NX, 3 * YROWS, LOW)], "spread3",
+        [pltpu.VMEM((3, NY, YROWS, LOW), BF), pltpu.SemaphoreType.DMA((3, NX))], places=[HB],
+    )(over_z(packed))
+    saved = over_yx(sent.reshape(NY * NX, 3 * YROWS, LOW))
     blocks, wide = (NY * NX, YROWS, LOW), (NY * NZ * CAP, WIDTH)
     parts, *kept1 = call(
         upper_kernel, [SM, VM] + [VM, HB] * 2, [blocks] + [wide] * 4, "upper",
-        [pltpu.VMEM((WIDTH, HID), BF), pltpu.VMEM((HID, WIDTH), BF), pltpu.SemaphoreType.DMA((2,))],
+        [pltpu.VMEM((WIDTH, HID), BF), pltpu.VMEM((HID, WIDTH), BF), pltpu.SemaphoreType.DMA((2, CUTS))],
     )(core, saved, *weights)
     (rows,) = call(gather_kernel, [VM], [(ALL, LOW)], "gather")(over_yx(parts))
     res1, packed = call(middle_kernel, [SM] + [VM] * 5, [(TOK, SHARE), (ALL, LOW)], "middle")(
         core, over_z(rows), cotangent, gates, owners, slots
     )
-    (sent,) = call(functools.partial(spread_kernel, 1), [VM], [(NY * NX, YROWS, LOW)], "spread1")(
+    (sent,) = call(spread_kernel, [VM], [(NY * NX, YROWS, LOW)], "spread1")(
         over_z(packed)
     )
     parts, *keep, give = call(
         lower_kernel, [SM] + [VM] * 6 + [VM, HB] * 2, [blocks] + [wide] * 4 + [(4,) + wide], "lower",
         [pltpu.VMEM((4,) + wide, BF), pltpu.VMEM((WIDTH, HID), BF), pltpu.VMEM((HID, WIDTH), BF),
-         pltpu.SemaphoreType.DMA((6,))], places=[VM] * 5 + [HB],
+         pltpu.SemaphoreType.DMA((4,)), pltpu.SemaphoreType.DMA((2, CUTS))], places=[VM] * 5 + [HB],
     )(core, saved, over_yx(sent), *kept1, *weights)
     came = lax.ppermute(give, "segment", SWAP)
     (rows,) = call(gather_kernel, [VM], [(ALL, LOW)], "gather")(over_yx(parts))
 
-    grad_in, grad_out, mark = call(
-        weight_kernel, [HB] * 5, [(WIDTH, HID), (HID, WIDTH), jax.ShapeDtypeStruct((1,), I32)], "weight",
+    grad_in, grad_out = call(
+        weight_kernel, [HB] * 5, [(WIDTH, HID), (HID, WIDTH)], "weight",
         [pltpu.VMEM((4, 2 * NY * NZ * CAP, WIDTH), BF), pltpu.VMEM((2, WIDTH, HID), BF), pltpu.SemaphoreType.DMA((10,))],
-        mib=56, cost=(2 * 10**9, 6 * 10**6), places=[HB, HB, SM],
+        mib=56, cost=(2 * 10**9, 6 * 10**6), places=[HB, HB],
     )(*keep, came)
-    mine, other = call(end_kernel, [SM] + [VM] * 4 + [SM], [(TOK, SHARE)] * 2, "end")(
-        core, over_z(rows), res1, owners, slots, mark
-    )
+    mine, other, grad_in = call(
+        end_kernel, [SM] + [VM] * 4 + [HB], [(TOK, SHARE)] * 2 + [(WIDTH, HID)], "end",
+        places=[VM, VM, HB], alias={5: 2},
+    )(core, over_z(rows), res1, owners, slots, grad_in)
     got = lax.ppermute(other, "segment", SWAP)
     grads = jnp.stack([jnp.where(top, got, mine), jnp.where(top, mine, got)])
     return grads[None], grad_in[None, None], grad_out[None, None]

time: 170 us -> 168 us (0.988)
  no operation moved by 1% of the time
where the time goes in v6:
time: 168 us
  blocking collectives  67.2 us (40%)
  starting transfers between devices  53.4 us (32%)
  waiting for transfers between devices  26.6 us (16%)
  Pallas kernels  17 us (10%)
  local copies, waits for them, and re-layouts  1.96 us (1%)
    all_to_all x3, blocking collectives, over_yx(): return lax.all_to_all(x, ('y', 'pair'), 0, 0, tiled=True)  35.7 us
    all_to_all x2, blocking collectives, over_z(): lax.all_to_all(x, 'z', 0, 0, axis_index_groups=ring, tiled=True)  31.5 us
    all_to_all x2, starting transfers between devices, over_z(): lax.all_to_all(x, 'z', 0, 0, axis_index_groups=ring, tiled=True)  30.9 us
    all_to_all x1, waiting for transfers between devices, over_yx(): return lax.all_to_all(x, ('y', 'pair'), 0, 0, tiled=True)  17 us
    all_to_all x2, waiting for transfers between devices, over_z(): lax.all_to_all(x, 'z', 0, 0, axis_index_groups=ring, tiled=True)  8.67 us
    ppermute x1, starting transfers between devices, body(): came = lax.ppermute(give, 'segment', SWAP)  6.94 us
    all_to_all x1, starting transfers between devices, over_yx(): return lax.all_to_all(x, ('y', 'pair'), 0, 0, tiled=True)  6.9 us
    pallas_call x1, Pallas kernels, body(): call(weight_kernel, [HB] * 5, [(WIDTH, HID), (HID, WIDTH)], 'weight', [pl...  4.51 us
  transfers between devices with their start and end apart: 7, of which 3 were waited for; matrix products, arithmetic and copies ran while one was open for 0% of the time, Pallas kernels for 4%

profile of v6, /device:TPU:1, one launch (start us, length us, event | category | flops | bytes accessed | tf_op | source)
XLA Modules:
  0.0 167.8 jit_solution(7733407017268334078)
XLA Ops:
  0.6 2.5 %start.1 = bf16[1152,128]{1,0:T(8,128)(2,1)} custom-call(s32[1]{0:T(128)} %bitcast.core_ref, bf16[2,2,192,192]{3,2,1,0:T(8,128)(2,1)} %acts.1, bf16[2,192,192]{2,1,0:T(8,128)(2,1)} %cot.3, f32[2,2,192]{2,1,0:T(2,128)} %gates.3, s32[2,2,192]{2,1,0:T(2,128)} %owners.5, s32[2,2,192]{2,1,0:T(2,128)} %slots.5), custom_call_target="tpu_custom_call" | custom-call | tf_op jit(solution)/shard_map/start/pallas_call | solution.py:363
  3.2 19.1 %all-to-all-start = ((bf16[16,72,128]{2,1,0:T(8,128)(2,1)}), bf16[16,72,128]{2,1,0:T(8,128)(2,1)S(1)}, u32[]{:S(2)}, u32[]{:S(2)}) async-start(bf16[16,72,128]{2,1,0:T(8,128)(2,1)} %bitcast.32), calls=%async_computation | async-start | bytes 589824 | tf_op jit(solution)/shard_map/all_to_all | solution.py:346
  22.3 3.1 %collective-permute-start = (bf16[768,768]{1,0:T(8,128)(2,1)S(1)}, bf16[768,768]{1,0:T(8,128)(2,1)}, u32[]{:S(2)}, u32[]{:S(2)}) collective-permute-start(bf16[768,768]{1,0:T(8,128)(2,1)S(1)} %bitcast.20), channel_id=1, source_target_pairs={{0,256},{256,0},{1,257},{257,1},{2,258},{258,2},{3,259},{259,3},{4... | collective-permute-start | bytes 3538952 | tf_op jit(solution)/shard_map/ppermute | solution.py:358
  25.5 1.9 %collective-permute-start.1 = (bf16[768,768]{1,0:T(8,128)(2,1)}, bf16[768,768]{1,0:T(8,128)(2,1)}, u32[]{:S(2)}, u32[]{:S(2)}) collective-permute-start(bf16[768,768]{1,0:T(8,128)(2,1)} %bitcast.23), channel_id=1, source_target_pairs={{0,256},{256,0},{1,257},{257,1},{2,258},{258,2},{3,259},{259,3},{4... | collective-permute-start | bytes 3538952 | tf_op jit(solution)/shard_map/ppermute | solution.py:359
  27.4 8.7 %all-to-all-done = bf16[16,72,128]{2,1,0:T(8,128)(2,1)S(1)} async-done(((bf16[16,72,128]{2,1,0:T(8,128)(2,1)}), bf16[16,72,128]{2,1,0:T(8,128)(2,1)S(1)}, u32[]{:S(2)}, u32[]{:S(2)}) %all-to-all-start) | async-done | bytes 294944 | tf_op jit(solution)/shard_map/all_to_all | solution.py:346
  36.1 1.4 spread3.1
  37.5 6.9 %all-to-all-start.1 = ((bf16[16,288,128]{2,1,0:T(8,128)(2,1)}), bf16[16,288,128]{2,1,0:T(8,128)(2,1)S(1)}, u32[]{:S(2)}, u32[]{:S(2)}) async-start(bf16[16,288,128]{2,1,0:T(8,128)(2,1)} %bitcast.3), calls=%async_computation.1 | async-start | bytes 2359296 | tf_op jit(solution)/shard_map/all_to_all | solution.py:350
  44.4 17.0 %all-to-all-done.1.saved = bf16[16,288,128]{2,1,0:T(8,128)(2,1)S(1)} async-done(((bf16[16,288,128]{2,1,0:T(8,128)(2,1)}), bf16[16,288,128]{2,1,0:T(8,128)(2,1)S(1)}, u32[]{:S(2)}, u32[]{:S(2)}) %all-to-all-start.1) | async-done | bytes 1179680 | tf_op jit(solution)/shard_map/all_to_all | solution.py:350
  61.4 1.9 %upper.1 = (bf16[16,96,128]{2,1,0:T(8,128)(2,1)S(1)}, bf16[256,768]{1,0:T(8,128)(2,1)S(1)}, bf16[256,768]{1,0:T(8,128)(2,1)S(1)}, bf16[256,768]{1,0:T(8,128)(2,1)S(1)}, bf16[256,768]{1,0:T(8,128)(2,1)S(1)}) custom-call(s32[1]{0:T(128)} %bitcast.core_ref, bf16[16,288,128]{2,1,0:T(8,128)(2,1)S(1)} %all-to-all-done.1.saved, bf16[768,768]{1,0:T(8,128)(2,1)S(1)} %bitcast.21, ...), custom_call_target="tpu_custom_call" | custom-call | tf_op jit(solution)/shard_map/upper/pallas_call | solution.py:374
  63.4 12.6 %all_to_all.40.parts = bf16[16,96,128]{2,1,0:T(8,128)(2,1)S(1)} all-to-all(bf16[16,96,128]{2,1,0:T(8,128)(2,1)S(1)} %get-tuple-element.21), channel_id=1, replica_groups=mesh['segment'=2,'y'=4,'z'=16,'pair'=4] {'y','pair'}, dimensions={0} | all-to-all | bytes 786432 | tf_op jit(solution)/shard_map/all_to_all | solution.py:350
  76.3 16.4 %all_to_all.41 = bf16[16,24,128]{2,1,0:T(8,128)(2,1)S(1)} all-to-all(bf16[16,24,128]{2,1,0:T(8,128)(2,1)S(1)} %bitcast.29), channel_id=1, replica_groups={{32,36,40,44,48,52,56,60,0,4,8,12,16,20,24,28},{33,37,41,45,49,53,57,61..., dimensions={0} | all-to-all | bytes 196608 | tf_op jit(solution)/shard_map/all_to_all | solution.py:346
  92.7 0.7 middle.1
  93.4 15.1 %all_to_all.42 = bf16[16,24,128]{2,1,0:T(8,128)(2,1)S(1)} all-to-all(bf16[16,24,128]{2,1,0:T(8,128)(2,1)S(1)} %bitcast.31), channel_id=1, replica_groups={{32,36,40,44,48,52,56,60,0,4,8,12,16,20,24,28},{33,37,41,45,49,53,57,61..., dimensions={0} | all-to-all | bytes 196608 | tf_op jit(solution)/shard_map/all_to_all | solution.py:346
  108.8 10.9 %all_to_all.43.came = bf16[16,96,128]{2,1,0:T(8,128)(2,1)S(1)} all-to-all(bf16[16,96,128]{2,1,0:T(8,128)(2,1)S(1)} %spread1.1), channel_id=1, replica_groups=mesh['segment'=2,'y'=4,'z'=16,'pair'=4] {'y','pair'}, dimensions={0} | all-to-all | bytes 786432 | tf_op jit(solution)/shard_map/all_to_all | solution.py:350
  119.6 4.1 %lower.1 = (bf16[16,96,128]{2,1,0:T(8,128)(2,1)S(1)}, bf16[256,768]{1,0:T(8,128)(2,1)S(1)}, bf16[256,768]{1,0:T(8,128)(2,1)S(1)}, bf16[256,768]{1,0:T(8,128)(2,1...) custom-call(s32[1]{0:T(128)} %bitcast.core_ref, bf16[16,288,128]{2,1,0:T(8,128)(2,1)S(1)} %all-to-all-done.1.saved, ...), custom_call_target="tpu_custom_call" | custom-call | tf_op jit(solution)/shard_map/lower/pallas_call | solution.py:385
  123.7 0.7 copy-done.11
  124.5 6.9 %collective-permute-start.2 = (bf16[4,256,768]{2,1,0:T(8,128)(2,1)}, bf16[4,256,768]{2,1,0:T(8,128)(2,1)S(1)}, u32[]{:S(2)}, u32[]{:S(2)}) collective-permute-start(bf16[4,256,768]{2,1,0:T(8,128)(2,1)} %get-tuple-element.33), channel_id=1, source_target_pairs={{0,256},{256,0},{1,257},{257,1},{2,258},{258,2},{3,259},{259,3},{4... | collective-permute-start | bytes 4718600 | tf_op jit(solution)/shard_map/ppermute | solution.py:390
  131.4 12.3 %all_to_all.44.parts = bf16[16,96,128]{2,1,0:T(8,128)(2,1)S(1)} all-to-all(bf16[16,96,128]{2,1,0:T(8,128)(2,1)S(1)} %get-tuple-element.27), channel_id=1, replica_groups=mesh['segment'=2,'y'=4,'z'=16,'pair'=4] {'y','pair'}, dimensions={0} | all-to-all | bytes 786432 | tf_op jit(solution)/shard_map/all_to_all | solution.py:350
  143.7 0.9 gather.3
  144.6 11.8 %all-to-all-start.7 = ((bf16[16,24,128]{2,1,0:T(8,128)(2,1)}), bf16[16,24,128]{2,1,0:T(8,128)(2,1)S(1)}, u32[]{:S(2)}, u32[]{:S(2)}) async-start(bf16[16,24,128]{2,1,0:T(8,128)(2,1)} %bitcast.10), calls=%async_computation.7 | async-start | bytes 196608 | tf_op jit(solution)/shard_map/all_to_all | solution.py:346
  156.4 1.2 copy-done.12
  157.5 4.5 %weight.1 = (bf16[768,768]{1,0:T(8,128)(2,1)}, bf16[768,768]{1,0:T(8,128)(2,1)}) custom-call(bf16[256,768]{1,0:T(8,128)(2,1)} %copy-done.8, bf16[256,768]{1,0:T(8,128)(2,1)} %copy-done.9, bf16[256,768]{1,0:T(8,128)(2,1)} %copy-done.10, bf16[256,768]{1,0:T(8,128)(2,1)} %copy-done.11, bf16[4,256,768]{2,1,0:T(8,128)(2,1)} %copy-done.12), custom_call_target="tpu_custom_call" | custom-call | flops 2000000000 | bytes 6000000 | tf_op jit(solution)/shard_map/weight/pallas_call | solution.py:393
  162.5 3.6 %collective-permute-start.3 = (bf16[192,192]{1,0:T(8,128)(2,1)S(1)}, bf16[192,192]{1,0:T(8,128)(2,1)S(1)}, u32[]{:S(2)}, u32[]{:S(2)}) collective-permute-start(bf16[192,192]{1,0:T(8,128)(2,1)S(1)} %get-tuple-element.35), channel_id=1, source_target_pairs={{0,256},{256,0},{1,257},{257,1},{2,258},{258,2},{3,259},{259,3},{4... | collective-permute-start | bytes 221192 | tf_op jit(solution)/shard_map/ppermute | solution.py:402
  166.1 0.9 collective-permute-done.3
  (33 shorter events, 1.7 us)
Async XLA Ops:
  0.6 21.7 %copy-start = (bf16[1,1,768,768]{3,2,1,0:T(8,128)(2,1)S(1)}, bf16[1,1,768,768]{3,2,1,0:T(8,128)(2,1)}, u32[]{:S(2)}) copy-start(bf16[1,1,768,768]{3,2,1,0:T(8,128)(2,1)} %param.12) | copy-start | bytes 3538948
  3.2 32.9 %all-to-all-start = ((bf16[16,72,128]{2,1,0:T(8,128)(2,1)}), bf16[16,72,128]{2,1,0:T(8,128)(2,1)S(1)}, u32[]{:S(2)}, u32[]{:S(2)}) async-start(bf16[16,72,128]{2,1,0:T(8,128)(2,1)} %bitcast.32), calls=%async_computation | async-start | bytes 589824 | tf_op jit(solution)/shard_map/all_to_all | solution.py:346
  22.3 22.1 %collective-permute-start = (bf16[768,768]{1,0:T(8,128)(2,1)S(1)}, bf16[768,768]{1,0:T(8,128)(2,1)}, u32[]{:S(2)}, u32[]{:S(2)}) collective-permute-start(bf16[768,768]{1,0:T(8,128)(2,1)S(1)} %bitcast.20), channel_id=1, source_target_pairs={{0,256},{256,0},{1,257},{257,1},{2,258},{258,2},{3,259},{259,3},{4... | collective-permute-start | bytes 3538952 | tf_op jit(solution)/shard_map/ppermute | solution.py:358
  25.5 18.9 %collective-permute-start.1 = (bf16[768,768]{1,0:T(8,128)(2,1)}, bf16[768,768]{1,0:T(8,128)(2,1)}, u32[]{:S(2)}, u32[]{:S(2)}) collective-permute-start(bf16[768,768]{1,0:T(8,128)(2,1)} %bitcast.23), channel_id=1, source_target_pairs={{0,256},{256,0},{1,257},{257,1},{2,258},{258,2},{3,259},{259,3},{4... | collective-permute-start | bytes 3538952 | tf_op jit(solution)/shard_map/ppermute | solution.py:359
  37.5 24.0 %copy-start.1 = (bf16[1,1,768,768]{3,2,1,0:T(8,128)(2,1)S(1)}, bf16[1,1,768,768]{3,2,1,0:T(8,128)(2,1)}, u32[]{:S(2)}) copy-start(bf16[1,1,768,768]{3,2,1,0:T(8,128)(2,1)} %param.13) | copy-start | bytes 3538948
  37.5 24.0 %all-to-all-start.1 = ((bf16[16,288,128]{2,1,0:T(8,128)(2,1)}), bf16[16,288,128]{2,1,0:T(8,128)(2,1)S(1)}, u32[]{:S(2)}, u32[]{:S(2)}) async-start(bf16[16,288,128]{2,1,0:T(8,128)(2,1)} %bitcast.3), calls=%async_computation.1 | async-start | bytes 2359296 | tf_op jit(solution)/shard_map/all_to_all | solution.py:350
  63.4 29.3 %copy-start.2 = (bf16[2,192,192]{2,1,0:T(8,128)(2,1)S(1)}, bf16[2,192,192]{2,1,0:T(8,128)(2,1)}, u32[]{:S(2)}) copy-start(bf16[2,192,192]{2,1,0:T(8,128)(2,1)} %cot.3) | copy-start | bytes 442372
  63.4 29.3 %copy-start.5 = (s32[2,2,192]{2,1,0:T(2,128)S(1)}, s32[2,2,192]{2,1,0:T(2,128)}, u32[]{:S(2)}) copy-start(s32[2,2,192]{2,1,0:T(2,128)} %owners.5) | copy-start | bytes 9220
  63.4 29.3 %copy-start.6 = (s32[2,2,192]{2,1,0:T(2,128)S(1)}, s32[2,2,192]{2,1,0:T(2,128)}, u32[]{:S(2)}) copy-start(s32[2,2,192]{2,1,0:T(2,128)} %slots.5) | copy-start | bytes 9220
  63.4 29.3 %copy-start.7 = (f32[2,2,192]{2,1,0:T(2,128)S(1)}, f32[2,2,192]{2,1,0:T(2,128)}, u32[]{:S(2)}) copy-start(f32[2,2,192]{2,1,0:T(2,128)} %gates.3) | copy-start | bytes 9220
  93.4 15.1 %copy-start.3 = (bf16[192,192]{1,0:T(8,128)(2,1)}, bf16[192,192]{1,0:T(8,128)(2,1)S(1)}, u32[]{:S(2)}) copy-start(bf16[192,192]{1,0:T(8,128)(2,1)S(1)} %get-tuple-element.28.above) | copy-start | bytes 221188
  123.7 0.7 copy-start.11
  124.5 20.1 %copy-start.8 = (bf16[256,768]{1,0:T(8,128)(2,1)}, bf16[256,768]{1,0:T(8,128)(2,1)S(1)}, u32[]{:S(2)}) copy-start(bf16[256,768]{1,0:T(8,128)(2,1)S(1)} %get-tuple-element.29.k0) | copy-start | bytes 1179652
  124.5 20.1 %copy-start.9 = (bf16[256,768]{1,0:T(8,128)(2,1)}, bf16[256,768]{1,0:T(8,128)(2,1)S(1)}, u32[]{:S(2)}) copy-start(bf16[256,768]{1,0:T(8,128)(2,1)S(1)} %get-tuple-element.30.k1) | copy-start | bytes 1179652
  124.5 20.1 %copy-start.10 = (bf16[256,768]{1,0:T(8,128)(2,1)}, bf16[256,768]{1,0:T(8,128)(2,1)S(1)}, u32[]{:S(2)}) copy-start(bf16[256,768]{1,0:T(8,128)(2,1)S(1)} %get-tuple-element.31.k2) | copy-start | bytes 1179652
  124.5 31.9 %collective-permute-start.2 = (bf16[4,256,768]{2,1,0:T(8,128)(2,1)}, bf16[4,256,768]{2,1,0:T(8,128)(2,1)S(1)}, u32[]{:S(2)}, u32[]{:S(2)}) collective-permute-start(bf16[4,256,768]{2,1,0:T(8,128)(2,1)} %get-tuple-element.33), channel_id=1, source_target_pairs={{0,256},{256,0},{1,257},{257,1},{2,258},{258,2},{3,259},{259,3},{4... | collective-permute-start | bytes 4718600 | tf_op jit(solution)/shard_map/ppermute | solution.py:390
  144.6 17.5 %all-to-all-start.7 = ((bf16[16,24,128]{2,1,0:T(8,128)(2,1)}), bf16[16,24,128]{2,1,0:T(8,128)(2,1)S(1)}, u32[]{:S(2)}, u32[]{:S(2)}) async-start(bf16[16,24,128]{2,1,0:T(8,128)(2,1)} %bitcast.10), calls=%async_computation.7 | async-start | bytes 196608 | tf_op jit(solution)/shard_map/all_to_all | solution.py:346
  156.4 1.2 copy-start.12
  157.5 4.5 %copy-start.4 = (bf16[192,192]{1,0:T(8,128)(2,1)S(1)}, bf16[192,192]{1,0:T(8,128)(2,1)}, u32[]{:S(2)}) copy-start(bf16[192,192]{1,0:T(8,128)(2,1)} %copy-done.3) | copy-start | bytes 221188
  162.5 4.5 %collective-permute-start.3 = (bf16[192,192]{1,0:T(8,128)(2,1)S(1)}, bf16[192,192]{1,0:T(8,128)(2,1)S(1)}, u32[]{:S(2)}, u32[]{:S(2)}) collective-permute-start(bf16[192,192]{1,0:T(8,128)(2,1)S(1)} %get-tuple-element.35), channel_id=1, source_target_pairs={{0,256},{256,0},{1,257},{257,1},{2,258},{258,2},{3,259},{259,3},{4... | collective-permute-start | bytes 221192 | tf_op jit(solution)/shard_map/ppermute | solution.py:402

commit v7 on v6

--- a/solution.py
+++ b/solution.py
@@ -87,6 +87,11 @@
     return jnp.where(core == 0, ref[layer, 0:1, :], ref[layer, 1:2, :])
 
 
+def joined(parts):
+    parts = [p.reshape(NZ, ZROWS, LOW) for p in parts]
+    return jnp.concatenate(parts, axis=1).reshape(len(parts) * ALL, LOW).astype(BF)
+
+
 def start_kernel(core_ref, acts, cot, gates, owners, slots, out, tok, gate_v, owner_v, slot_v, sems):
     core = core_ref[0]
     copies = [
@@ -98,7 +103,6 @@
                 (gates, gate_v),
                 (cot.at[core], tok.at[0]),
                 (acts.at[1, core], tok.at[1]),
-                (acts.at[0, core], tok.at[2]),
             ]
         )
     ]
@@ -107,15 +111,12 @@
     copies[0].wait()
     copies[1].wait()
     upper = routes(row_of(owner_v, 1, core), row_of(slot_v, 1, core))
-    lower = routes(row_of(owner_v, 0, core), row_of(slot_v, 0, core))
     for copy in copies[2:]:
         copy.wait()
     gate = column(row_of(gate_v, 1, core))
     scaled = (gate * tok[0].astype(F32)).astype(BF)
     first = pack([tok[1], scaled], upper)
-    second = pack([tok[2]], lower)
-    parts = [p.reshape(NZ, ZROWS, LOW) for p in first + second]
-    out[...] = jnp.concatenate(parts, axis=1).reshape(3 * ALL, LOW).astype(BF)
+    out[...] = joined(first)
 
 
 def spread_move():
@@ -128,22 +129,27 @@
     return hot((at == jnp.where(k < NZ * CAP, low, high)).reshape(ALL, ALL))
 
 
+def moved_parts(rows):
+    move = spread_move()
+    value = rows[...].astype(F32).reshape(NZ, 2 * ZROWS, LOW)
+    for a in range(2):
+        part = value[:, a * ZROWS : (a + 1) * ZROWS].reshape(ALL, LOW).astype(BF)
+        yield a, dot(move, part).astype(BF)
+
+
 def spread_kernel(rows, out):
-    moved = dot(spread_move(), rows[...]).astype(BF)
-    for j in range(NY):
+    for a, moved in moved_parts(rows):
+        for j in range(NY):
+            for i in range(NX):
+                out[j * NX + i, a * YROWS : (a + 1) * YROWS, :] = moved[j * YROWS : (j + 1) * YROWS]
+
+
+def sending_kernel(rows, out, held_rows, sems):
+    copies = []
+    for a, moved in moved_parts(rows):
+        held_rows[a] = moved.reshape(NY, YROWS, LOW)
         for i in range(NX):
-            out[j * NX + i] = moved[j * YROWS : (j + 1) * YROWS]
-
-
-def spread3_kernel(rows, out, moved, sems):
-    move = spread_move()
-    value = rows[...].astype(F32).reshape(NZ, 3 * ZROWS, LOW)
-    copies = []
-    for a in range(3):
-        part = value[:, a * ZROWS : (a + 1) * ZROWS].reshape(ALL, LOW).astype(BF)
-        moved[a] = dot(move, part).astype(BF).reshape(NY, YROWS, LOW)
-        for i in range(NX):
-            copy = pltpu.make_async_copy(moved.at[a], out.at[:, i, a * YROWS : (a + 1) * YROWS], sems.at[a, i])
+            copy = pltpu.make_async_copy(held_rows.at[a], out.at[:, i, a * YROWS : (a + 1) * YROWS], sems.at[a, i])
             copy.start()
             copies.append(copy)
     for copy in copies:
@@ -242,13 +248,13 @@
 
 
 def lower_kernel(
-    core_ref, saved, came, n1, b1, h1, g1, own_in, other_in, own_out, other_out,
+    core_ref, saved, n1, b1, h1, g1, own_in, other_in, own_out, other_out,
     out, k0, k1, k2, k3, give, kept, in_buf, out_buf, sems, more,
 ):
     keep, above = (k0, k1, k2, k3), (n1, b1, h1, g1)
 
     def run(w_in, w_out, save):
-        expert_step(assemble(saved, 2 * YROWS).astype(F32), assemble(came, 0), w_in, w_out, out, save)
+        expert_step(assemble(saved, 0).astype(F32), assemble(saved, YROWS), w_in, w_out, out, save)
 
     @pl.when(core_ref[0] == 0)
     def _():
@@ -302,15 +308,14 @@
         copy.wait()
 
 
-def middle_kernel(core_ref, rows, cot, gates, owners, slots, result, out):
+def middle_kernel(core_ref, rows, cot, acts, gates, owners, slots, result, out):
     core = core_ref[0]
     branch = unpack(rows[...], row_of(owners, 1, core), row_of(slots, 1, core))
     res = (cot[core].astype(F32) + branch).astype(BF)
     result[...] = res
     gate = column(row_of(gates, 0, core))
     scaled = (gate * res.astype(F32)).astype(BF)
-    (packed,) = pack([scaled], routes(row_of(owners, 0, core), row_of(slots, 0, core)))
-    out[...] = packed.astype(BF)
+    out[...] = joined(pack([acts[0, core], scaled], routes(row_of(owners, 0, core), row_of(slots, 0, core))))
 
 
 def end_kernel(core_ref, rows, above, owners, slots, grad_in, keep, give, same):
@@ -361,32 +366,32 @@
 
     table = (2, 2, TOK)
     (packed,) = call(
-        start_kernel, [SM] + [HB] * 5, [(3 * ALL, LOW)], "start",
-        [pltpu.VMEM((3, TOK, SHARE), BF), pltpu.VMEM(table, F32), pltpu.VMEM(table, I32),
+        start_kernel, [SM] + [HB] * 5, [(2 * ALL, LOW)], "start",
+        [pltpu.VMEM((2, TOK, SHARE), BF), pltpu.VMEM(table, F32), pltpu.VMEM(table, I32),
          pltpu.VMEM(table, I32), pltpu.SemaphoreType.DMA((6,))], mib=60,
     )(core, acts, cotangent, gates, owners, slots)
     (sent,) = call(
-        spread3_kernel, [VM], [(NY, NX, 3 * YROWS, LOW)], "spread3",
-        [pltpu.VMEM((3, NY, YROWS, LOW), BF), pltpu.SemaphoreType.DMA((3, NX))], places=[HB],
+        sending_kernel, [VM], [(NY, NX, 2 * YROWS, LOW)], "sending",
+        [pltpu.VMEM((2, NY, YROWS, LOW), BF), pltpu.SemaphoreType.DMA((2, NX))], places=[HB], mib=61,
     )(over_z(packed))
-    saved = over_yx(sent.reshape(NY * NX, 3 * YROWS, LOW))
+    saved = over_yx(sent.reshape(NY * NX, 2 * YROWS, LOW))
     blocks, wide = (NY * NX, YROWS, LOW), (NY * NZ * CAP, WIDTH)
     parts, *kept1 = call(
         upper_kernel, [SM, VM] + [VM, HB] * 2, [blocks] + [wide] * 4, "upper",
         [pltpu.VMEM((WIDTH, HID), BF), pltpu.VMEM((HID, WIDTH), BF), pltpu.SemaphoreType.DMA((2, CUTS))],
     )(core, saved, *weights)
     (rows,) = call(gather_kernel, [VM], [(ALL, LOW)], "gather")(over_yx(parts))
-    res1, packed = call(middle_kernel, [SM] + [VM] * 5, [(TOK, SHARE), (ALL, LOW)], "middle")(
-        core, over_z(rows), cotangent, gates, owners, slots
+    res1, packed = call(middle_kernel, [SM] + [VM] * 6, [(TOK, SHARE), (2 * ALL, LOW)], "middle")(
+        core, over_z(rows), cotangent, acts, gates, owners, slots
     )
-    (sent,) = call(spread_kernel, [VM], [(NY * NX, YROWS, LOW)], "spread1")(
+    (sent,) = call(spread_kernel, [VM], [(NY * NX, 2 * YROWS, LOW)], "spread")(
         over_z(packed)
     )
     parts, *keep, give = call(
-        lower_kernel, [SM] + [VM] * 6 + [VM, HB] * 2, [blocks] + [wide] * 4 + [(4,) + wide], "lower",
+        lower_kernel, [SM] + [VM] * 5 + [VM, HB] * 2, [blocks] + [wide] * 4 + [(4,) + wide], "lower",
         [pltpu.VMEM((4,) + wide, BF), pltpu.VMEM((WIDTH, HID), BF), pltpu.VMEM((HID, WIDTH), BF),
          pltpu.SemaphoreType.DMA((4,)), pltpu.SemaphoreType.DMA((2, CUTS))], places=[VM] * 5 + [HB],
-    )(core, saved, over_yx(sent), *kept1, *weights)
+    )(core, over_yx(sent), *kept1, *weights)
     came = lax.ppermute(give, "segment", SWAP)
     (rows,) = call(gather_kernel, [VM], [(ALL, LOW)], "gather")(over_yx(parts))
 

time: 168 us -> 166 us (0.988)
  waiting for transfers between devices: 26.6 us -> 18.3 us
  blocking collectives: 67.2 us -> 70.3 us
  Pallas kernels: 17 us -> 19 us
    all_to_all x2, waiting for transfers between devices: 8.67 us -> 4.46 us  [over_z(): lax.all_to_all(x, 'z', 0, 0, axis_index_groups=ring, tiled=True)]
    all_to_all x1, waiting for transfers between devices: 17 us -> 12.9 us  [over_yx(): return lax.all_to_all(x, ('y', 'pair'), 0, 0, tiled=True)]
    all_to_all x3, blocking collectives: 35.7 us -> 37.9 us  [over_yx(): return lax.all_to_all(x, ('y', 'pair'), 0, 0, tiled=True)]
  transfers between devices with their start and end apart: 7 -> 7, of which waited for: 3 -> 3; matrix products, arithmetic and copies ran while one was open for 0% -> 0% of each run, Pallas kernels for 4% -> 5%
where the time goes in v7:
time: 166 us; the launch traced here: 165 us
  blocking collectives  70.3 us (42%)
  starting transfers between devices  53.5 us (32%)
  Pallas kernels  19 us (11%)
  waiting for transfers between devices  18.3 us (11%)
  local copies, waits for them, and re-layouts  2.63 us (2%)
    all_to_all x3, blocking collectives, over_yx(): return lax.all_to_all(x, ('y', 'pair'), 0, 0, tiled=True)  37.9 us
    all_to_all x2, blocking collectives, over_z(): lax.all_to_all(x, 'z', 0, 0, axis_index_groups=ring, tiled=True)  32.4 us
    all_to_all x2, starting transfers between devices, over_z(): lax.all_to_all(x, 'z', 0, 0, axis_index_groups=ring, tiled=True)  30.6 us
    all_to_all x1, waiting for transfers between devices, over_yx(): return lax.all_to_all(x, ('y', 'pair'), 0, 0, tiled=True)  12.9 us
    ppermute x1, starting transfers between devices, body(): came = lax.ppermute(give, 'segment', SWAP)  7.09 us
    all_to_all x1, starting transfers between devices, over_yx(): return lax.all_to_all(x, ('y', 'pair'), 0, 0, tiled=True)  6.81 us
    pallas_call x1, Pallas kernels, body(): call(weight_kernel, [HB] * 5, [(WIDTH, HID), (HID, WIDTH)], 'weight', [pl...  4.47 us
    all_to_all x2, waiting for transfers between devices, over_z(): lax.all_to_all(x, 'z', 0, 0, axis_index_groups=ring, tiled=True)  4.46 us
  transfers between devices with their start and end apart: 7, of which 3 were waited for; matrix products, arithmetic and copies ran while one was open for 0% of the time, Pallas kernels for 5%

profile of v7, /device:TPU:1, one launch (start us, length us, event | category | flops | bytes accessed | tf_op | source)
XLA Modules:
  0.0 165.4 jit_solution(11276628035595339188)
XLA Ops:
  0.6 2.3 %start.1 = bf16[768,128]{1,0:T(8,128)(2,1)} custom-call(s32[1]{0:T(128)} %bitcast.core_ref, bf16[2,2,192,192]{3,2,1,0:T(8,128)(2,1)} %acts.3, bf16[2,192,192]{2,1,0:T(8,128)(2,1)} %cot.3, f32[2,2,192]{2,1,0:T(2,128)} %gates.3, s32[2,2,192]{2,1,0:T(2,128)} %owners.5, s32[2,2,192]{2,1,0:T(2,128)} %slots.5), custom_call_target="tpu_custom_call" | custom-call | tf_op jit(solution)/shard_map/start/pallas_call | solution.py:368
  3.0 19.1 %all-to-all-start = ((bf16[16,48,128]{2,1,0:T(8,128)(2,1)}), bf16[16,48,128]{2,1,0:T(8,128)(2,1)S(1)}, u32[]{:S(2)}, u32[]{:S(2)}) async-start(bf16[16,48,128]{2,1,0:T(8,128)(2,1)} %bitcast.33), calls=%async_computation | async-start | bytes 393216 | tf_op jit(solution)/shard_map/all_to_all | solution.py:351
  22.1 3.1 %collective-permute-start = (bf16[768,768]{1,0:T(8,128)(2,1)S(1)}, bf16[768,768]{1,0:T(8,128)(2,1)}, u32[]{:S(2)}, u32[]{:S(2)}) collective-permute-start(bf16[768,768]{1,0:T(8,128)(2,1)S(1)} %bitcast.20), channel_id=1, source_target_pairs={{0,256},{256,0},{1,257},{257,1},{2,258},{258,2},{3,259},{259,3},{4... | collective-permute-start | bytes 3538952 | tf_op jit(solution)/shard_map/ppermute | solution.py:363
  25.3 1.9 %collective-permute-start.1 = (bf16[768,768]{1,0:T(8,128)(2,1)}, bf16[768,768]{1,0:T(8,128)(2,1)}, u32[]{:S(2)}, u32[]{:S(2)}) collective-permute-start(bf16[768,768]{1,0:T(8,128)(2,1)} %bitcast.23), channel_id=1, source_target_pairs={{0,256},{256,0},{1,257},{257,1},{2,258},{258,2},{3,259},{259,3},{4... | collective-permute-start | bytes 3538952 | tf_op jit(solution)/shard_map/ppermute | solution.py:364
  27.2 4.5 %all-to-all-done = bf16[16,48,128]{2,1,0:T(8,128)(2,1)S(1)} async-done(((bf16[16,48,128]{2,1,0:T(8,128)(2,1)}), bf16[16,48,128]{2,1,0:T(8,128)(2,1)S(1)}, u32[]{:S(2)}, u32[]{:S(2)}) %all-to-all-start) | async-done | bytes 196640 | tf_op jit(solution)/shard_map/all_to_all | solution.py:351
  32.4 2.2 %sending.1 = bf16[4,4,192,128]{3,2,1,0:T(8,128)(2,1)} custom-call(bf16[768,128]{1,0:T(8,128)(2,1)} %bitcast.34), custom_call_target="tpu_custom_call" | custom-call | tf_op jit(solution)/shard_map/sending/pallas_call | solution.py:373
  34.6 6.8 %all-to-all-start.1 = ((bf16[16,192,128]{2,1,0:T(8,128)(2,1)}), bf16[16,192,128]{2,1,0:T(8,128)(2,1)}, u32[]{:S(2)}, u32[]{:S(2)}) async-start(bf16[16,192,128]{2,1,0:T(8,128)(2,1)} %bitcast.31), calls=%async_computation.1 | async-start | bytes 1572864 | tf_op jit(solution)/shard_map/all_to_all | solution.py:355
  41.5 12.9 %all-to-all-done.1.saved = bf16[16,192,128]{2,1,0:T(8,128)(2,1)} async-done(((bf16[16,192,128]{2,1,0:T(8,128)(2,1)}), bf16[16,192,128]{2,1,0:T(8,128)(2,1)}, u32[]{:S(2)}, u32[]{:S(2)}) %all-to-all-start.1) | async-done | bytes 786464 | tf_op jit(solution)/shard_map/all_to_all | solution.py:355
  54.3 3.0 %upper.1 = (bf16[16,96,128]{2,1,0:T(8,128)(2,1)S(1)}, bf16[256,768]{1,0:T(8,128)(2,1)S(1)}, bf16[256,768]{1,0:T(8,128)(2,1)S(1)}, bf16[256,768]{1,0:T(8,128)(2,1)S(1)}, bf16[256,768]{1,0:T(8,128)(2,1)S(1)}) custom-call(s32[1]{0:T(128)} %bitcast.core_ref, bf16[16,192,128]{2,1,0:T(8,128)(2,1)} %all-to-all-done.1.saved, bf16[768,768]{1,0:T(8,128)(2,1)S(1)} %bitcast.21, ...), custom_call_target="tpu_custom_call" | custom-call | tf_op jit(solution)/shard_map/upper/pallas_call | solution.py:379
  57.4 12.5 %all_to_all.40.parts = bf16[16,96,128]{2,1,0:T(8,128)(2,1)S(1)} all-to-all(bf16[16,96,128]{2,1,0:T(8,128)(2,1)S(1)} %get-tuple-element.21), channel_id=1, replica_groups=mesh['segment'=2,'y'=4,'z'=16,'pair'=4] {'y','pair'}, dimensions={0} | all-to-all | bytes 786432 | tf_op jit(solution)/shard_map/all_to_all | solution.py:355
  70.2 15.2 %all_to_all.41 = bf16[16,24,128]{2,1,0:T(8,128)(2,1)S(1)} all-to-all(bf16[16,24,128]{2,1,0:T(8,128)(2,1)S(1)} %bitcast.29), channel_id=1, replica_groups={{32,36,40,44,48,52,56,60,0,4,8,12,16,20,24,28},{33,37,41,45,49,53,57,61..., dimensions={0} | all-to-all | bytes 196608 | tf_op jit(solution)/shard_map/all_to_all | solution.py:351
  85.4 1.0 middle.1
  86.4 17.2 %all_to_all.42 = bf16[16,48,128]{2,1,0:T(8,128)(2,1)S(1)} all-to-all(bf16[16,48,128]{2,1,0:T(8,128)(2,1)S(1)} %bitcast.30), channel_id=1, replica_groups={{32,36,40,44,48,52,56,60,0,4,8,12,16,20,24,28},{33,37,41,45,49,53,57,61..., dimensions={0} | all-to-all | bytes 393216 | tf_op jit(solution)/shard_map/all_to_all | solution.py:351
  103.9 13.1 %all_to_all.43.saved = bf16[16,192,128]{2,1,0:T(8,128)(2,1)S(1)} all-to-all(bf16[16,192,128]{2,1,0:T(8,128)(2,1)S(1)} %spread.1), channel_id=1, replica_groups=mesh['segment'=2,'y'=4,'z'=16,'pair'=4] {'y','pair'}, dimensions={0} | all-to-all | bytes 1572864 | tf_op jit(solution)/shard_map/all_to_all | solution.py:355
  117.1 4.1 %lower.1 = (bf16[16,96,128]{2,1,0:T(8,128)(2,1)S(1)}, bf16[256,768]{1,0:T(8,128)(2,1)S(1)}, bf16[256,768]{1,0:T(8,128)(2,1)S(1)}, bf16[256,768]{1,0:T(8,128)(2,1...) custom-call(s32[1]{0:T(128)} %bitcast.core_ref, bf16[16,192,128]{2,1,0:T(8,128)(2,1)S(1)} %all_to_all.43.saved, ...), custom_call_target="tpu_custom_call" | custom-call | tf_op jit(solution)/shard_map/lower/pallas_call | solution.py:390
  121.2 0.7 copy-done.10
  122.0 7.1 %collective-permute-start.2 = (bf16[4,256,768]{2,1,0:T(8,128)(2,1)}, bf16[4,256,768]{2,1,0:T(8,128)(2,1)S(1)}, u32[]{:S(2)}, u32[]{:S(2)}) collective-permute-start(bf16[4,256,768]{2,1,0:T(8,128)(2,1)} %get-tuple-element.33), channel_id=1, source_target_pairs={{0,256},{256,0},{1,257},{257,1},{2,258},{258,2},{3,259},{259,3},{4... | collective-permute-start | bytes 4718600 | tf_op jit(solution)/shard_map/ppermute | solution.py:395
  129.1 12.3 %all_to_all.44.parts = bf16[16,96,128]{2,1,0:T(8,128)(2,1)S(1)} all-to-all(bf16[16,96,128]{2,1,0:T(8,128)(2,1)S(1)} %get-tuple-element.27), channel_id=1, replica_groups=mesh['segment'=2,'y'=4,'z'=16,'pair'=4] {'y','pair'}, dimensions={0} | all-to-all | bytes 786432 | tf_op jit(solution)/shard_map/all_to_all | solution.py:355
  141.3 0.9 gather.3
  142.2 11.5 %all-to-all-start.7 = ((bf16[16,24,128]{2,1,0:T(8,128)(2,1)}), bf16[16,24,128]{2,1,0:T(8,128)(2,1)S(1)}, u32[]{:S(2)}, u32[]{:S(2)}) async-start(bf16[16,24,128]{2,1,0:T(8,128)(2,1)} %bitcast.10), calls=%async_computation.7 | async-start | bytes 196608 | tf_op jit(solution)/shard_map/all_to_all | solution.py:351
  153.7 1.2 copy-done.12
  154.9 4.5 %weight.1 = (bf16[768,768]{1,0:T(8,128)(2,1)}, bf16[768,768]{1,0:T(8,128)(2,1)}) custom-call(bf16[256,768]{1,0:T(8,128)(2,1)} %copy-done.7, bf16[256,768]{1,0:T(8,128)(2,1)} %copy-done.8, bf16[256,768]{1,0:T(8,128)(2,1)} %copy-done.9, bf16[256,768]{1,0:T(8,128)(2,1)} %copy-done.10, bf16[4,256,768]{2,1,0:T(8,128)(2,1)} %copy-done.12), custom_call_target="tpu_custom_call" | custom-call | flops 2000000000 | bytes 6000000 | tf_op jit(solution)/shard_map/weight/pallas_call | solution.py:398
  159.8 3.9 %collective-permute-start.3 = (bf16[192,192]{1,0:T(8,128)(2,1)S(1)}, bf16[192,192]{1,0:T(8,128)(2,1)S(1)}, u32[]{:S(2)}, u32[]{:S(2)}) collective-permute-start(bf16[192,192]{1,0:T(8,128)(2,1)S(1)} %get-tuple-element.35), channel_id=1, source_target_pairs={{0,256},{256,0},{1,257},{257,1},{2,258},{258,2},{3,259},{259,3},{4... | collective-permute-start | bytes 221192 | tf_op jit(solution)/shard_map/ppermute | solution.py:407
  163.7 0.9 collective-permute-done.3
  (33 shorter events, 2.5 us)
Async XLA Ops:
  0.6 21.5 %copy-start = (bf16[1,1,768,768]{3,2,1,0:T(8,128)(2,1)S(1)}, bf16[1,1,768,768]{3,2,1,0:T(8,128)(2,1)}, u32[]{:S(2)}) copy-start(bf16[1,1,768,768]{3,2,1,0:T(8,128)(2,1)} %param.12) | copy-start | bytes 3538948
  3.0 28.7 %all-to-all-start = ((bf16[16,48,128]{2,1,0:T(8,128)(2,1)}), bf16[16,48,128]{2,1,0:T(8,128)(2,1)S(1)}, u32[]{:S(2)}, u32[]{:S(2)}) async-start(bf16[16,48,128]{2,1,0:T(8,128)(2,1)} %bitcast.33), calls=%async_computation | async-start | bytes 393216 | tf_op jit(solution)/shard_map/all_to_all | solution.py:351
  22.1 19.3 %collective-permute-start = (bf16[768,768]{1,0:T(8,128)(2,1)S(1)}, bf16[768,768]{1,0:T(8,128)(2,1)}, u32[]{:S(2)}, u32[]{:S(2)}) collective-permute-start(bf16[768,768]{1,0:T(8,128)(2,1)S(1)} %bitcast.20), channel_id=1, source_target_pairs={{0,256},{256,0},{1,257},{257,1},{2,258},{258,2},{3,259},{259,3},{4... | collective-permute-start | bytes 3538952 | tf_op jit(solution)/shard_map/ppermute | solution.py:363
  25.3 16.2 %collective-permute-start.1 = (bf16[768,768]{1,0:T(8,128)(2,1)}, bf16[768,768]{1,0:T(8,128)(2,1)}, u32[]{:S(2)}, u32[]{:S(2)}) collective-permute-start(bf16[768,768]{1,0:T(8,128)(2,1)} %bitcast.23), channel_id=1, source_target_pairs={{0,256},{256,0},{1,257},{257,1},{2,258},{258,2},{3,259},{259,3},{4... | collective-permute-start | bytes 3538952 | tf_op jit(solution)/shard_map/ppermute | solution.py:364
  31.7 0.7 copy-start.11
  32.4 22.0 %copy-start.1 = (bf16[1,1,768,768]{3,2,1,0:T(8,128)(2,1)S(1)}, bf16[1,1,768,768]{3,2,1,0:T(8,128)(2,1)}, u32[]{:S(2)}) copy-start(bf16[1,1,768,768]{3,2,1,0:T(8,128)(2,1)} %param.13) | copy-start | bytes 3538948
  34.6 19.7 %all-to-all-start.1 = ((bf16[16,192,128]{2,1,0:T(8,128)(2,1)}), bf16[16,192,128]{2,1,0:T(8,128)(2,1)}, u32[]{:S(2)}, u32[]{:S(2)}) async-start(bf16[16,192,128]{2,1,0:T(8,128)(2,1)} %bitcast.31), calls=%async_computation.1 | async-start | bytes 1572864 | tf_op jit(solution)/shard_map/all_to_all | solution.py:355
  57.3 28.1 %copy-start.2 = (bf16[2,2,192,192]{3,2,1,0:T(8,128)(2,1)S(1)}, bf16[2,2,192,192]{3,2,1,0:T(8,128)(2,1)}, u32[]{:S(2)}) copy-start(bf16[2,2,192,192]{3,2,1,0:T(8,128)(2,1)} %acts.3) | copy-start | bytes 884740
  57.3 28.1 %copy-start.3 = (bf16[2,192,192]{2,1,0:T(8,128)(2,1)S(1)}, bf16[2,192,192]{2,1,0:T(8,128)(2,1)}, u32[]{:S(2)}) copy-start(bf16[2,192,192]{2,1,0:T(8,128)(2,1)} %cot.3) | copy-start | bytes 442372
  57.4 28.0 %copy-start.4 = (s32[2,2,192]{2,1,0:T(2,128)S(1)}, s32[2,2,192]{2,1,0:T(2,128)}, u32[]{:S(2)}) copy-start(s32[2,2,192]{2,1,0:T(2,128)} %owners.5) | copy-start | bytes 9220
  57.4 28.0 %copy-start.5 = (s32[2,2,192]{2,1,0:T(2,128)S(1)}, s32[2,2,192]{2,1,0:T(2,128)}, u32[]{:S(2)}) copy-start(s32[2,2,192]{2,1,0:T(2,128)} %slots.5) | copy-start | bytes 9220
  57.4 28.0 %copy-start.6 = (f32[2,2,192]{2,1,0:T(2,128)S(1)}, f32[2,2,192]{2,1,0:T(2,128)}, u32[]{:S(2)}) copy-start(f32[2,2,192]{2,1,0:T(2,128)} %gates.3) | copy-start | bytes 9220
  121.2 0.7 copy-start.10
  122.0 20.3 %copy-start.7 = (bf16[256,768]{1,0:T(8,128)(2,1)}, bf16[256,768]{1,0:T(8,128)(2,1)S(1)}, u32[]{:S(2)}) copy-start(bf16[256,768]{1,0:T(8,128)(2,1)S(1)} %get-tuple-element.29.k0) | copy-start | bytes 1179652
  122.0 20.3 %copy-start.8 = (bf16[256,768]{1,0:T(8,128)(2,1)}, bf16[256,768]{1,0:T(8,128)(2,1)S(1)}, u32[]{:S(2)}) copy-start(bf16[256,768]{1,0:T(8,128)(2,1)S(1)} %get-tuple-element.30.k1) | copy-start | bytes 1179652
  122.0 20.3 %copy-start.9 = (bf16[256,768]{1,0:T(8,128)(2,1)}, bf16[256,768]{1,0:T(8,128)(2,1)S(1)}, u32[]{:S(2)}) copy-start(bf16[256,768]{1,0:T(8,128)(2,1)S(1)} %get-tuple-element.31.k2) | copy-start | bytes 1179652
  122.0 31.7 %collective-permute-start.2 = (bf16[4,256,768]{2,1,0:T(8,128)(2,1)}, bf16[4,256,768]{2,1,0:T(8,128)(2,1)S(1)}, u32[]{:S(2)}, u32[]{:S(2)}) collective-permute-start(bf16[4,256,768]{2,1,0:T(8,128)(2,1)} %get-tuple-element.33), channel_id=1, source_target_pairs={{0,256},{256,0},{1,257},{257,1},{2,258},{258,2},{3,259},{259,3},{4... | collective-permute-start | bytes 4718600 | tf_op jit(solution)/shard_map/ppermute | solution.py:395
  142.2 17.1 %all-to-all-start.7 = ((bf16[16,24,128]{2,1,0:T(8,128)(2,1)}), bf16[16,24,128]{2,1,0:T(8,128)(2,1)S(1)}, u32[]{:S(2)}, u32[]{:S(2)}) async-start(bf16[16,24,128]{2,1,0:T(8,128)(2,1)} %bitcast.10), calls=%async_computation.7 | async-start | bytes 196608 | tf_op jit(solution)/shard_map/all_to_all | solution.py:351
  153.7 1.2 copy-start.12
  159.8 4.8 %collective-permute-start.3 = (bf16[192,192]{1,0:T(8,128)(2,1)S(1)}, bf16[192,192]{1,0:T(8,128)(2,1)S(1)}, u32[]{:S(2)}, u32[]{:S(2)}) collective-permute-start(bf16[192,192]{1,0:T(8,128)(2,1)S(1)} %get-tuple-element.35), channel_id=1, source_target_pairs={{0,256},{256,0},{1,257},{257,1},{2,258},{258,2},{3,259},{259,3},{4... | collective-permute-start | bytes 221192 | tf_op jit(solution)/shard_map/ppermute | solution.py:407

commit v8 on v7

--- a/solution.py
+++ b/solution.py
@@ -144,16 +144,8 @@
                 out[j * NX + i, a * YROWS : (a + 1) * YROWS, :] = moved[j * YROWS : (j + 1) * YROWS]
 
 
-def sending_kernel(rows, out, held_rows, sems):
-    copies = []
-    for a, moved in moved_parts(rows):
-        held_rows[a] = moved.reshape(NY, YROWS, LOW)
-        for i in range(NX):
-            copy = pltpu.make_async_copy(held_rows.at[a], out.at[:, i, a * YROWS : (a + 1) * YROWS], sems.at[a, i])
-            copy.start()
-            copies.append(copy)
-    for copy in copies:
-        copy.wait()
+def spread_after_kernel(rows, one, two, out):
+    spread_kernel(rows, out)
 
 
 def gather_kernel(parts, out):
@@ -370,11 +362,10 @@
         [pltpu.VMEM((2, TOK, SHARE), BF), pltpu.VMEM(table, F32), pltpu.VMEM(table, I32),
          pltpu.VMEM(table, I32), pltpu.SemaphoreType.DMA((6,))], mib=60,
     )(core, acts, cotangent, gates, owners, slots)
-    (sent,) = call(
-        sending_kernel, [VM], [(NY, NX, 2 * YROWS, LOW)], "sending",
-        [pltpu.VMEM((2, NY, YROWS, LOW), BF), pltpu.SemaphoreType.DMA((2, NX))], places=[HB], mib=61,
-    )(over_z(packed))
-    saved = over_yx(sent.reshape(NY * NX, 2 * YROWS, LOW))
+    (sent,) = call(spread_after_kernel, [VM, HB, HB], [(NY * NX, 2 * YROWS, LOW)], "spread_after")(
+        over_z(packed), other_in, other_out
+    )
+    saved = over_yx(sent)
     blocks, wide = (NY * NX, YROWS, LOW), (NY * NZ * CAP, WIDTH)
     parts, *kept1 = call(
         upper_kernel, [SM, VM] + [VM, HB] * 2, [blocks] + [wide] * 4, "upper",

time: 166 us -> 167 us (level)
  blocking collectives: 70.3 us -> 112 us
  starting transfers between devices: 53.5 us -> 33.5 us
  waiting for transfers between devices: 18.3 us -> 0.93 us
  Pallas kernels: 19 us -> 15.7 us
    all_to_all x2 -> x3, blocking collectives: 32.4 us -> 55.9 us  [over_z(): lax.all_to_all(x, 'z', 0, 0, axis_index_groups=ring, tiled=True)]
    all_to_all x2 -> x1, starting transfers between devices: 30.6 us -> 11.5 us  [over_z(): lax.all_to_all(x, 'z', 0, 0, axis_index_groups=ring, tiled=True)]
    all_to_all x3 -> x4, blocking collectives: 37.9 us -> 56.5 us  [over_yx(): return lax.all_to_all(x, ('y', 'pair'), 0, 0, tiled=True)]
    all_to_all x1 -> x0, waiting for transfers between devices: 12.9 us -> none  [over_yx(): return lax.all_to_all(x, ('y', 'pair'), 0, 0, tiled=True)]
    all_to_all x1 -> x0, starting transfers between devices: 6.81 us -> none  [over_yx(): return lax.all_to_all(x, ('y', 'pair'), 0, 0, tiled=True)]
    ppermute x1, starting transfers between devices: 3.14 us -> 8.79 us  [body(): other_in = lax.ppermute(own_in, 'segment', SWAP)]
    all_to_all x2 -> x1, waiting for transfers between devices: 4.46 us -> 0.01 us  [over_z(): lax.all_to_all(x, 'z', 0, 0, axis_index_groups=ring, tiled=True)]
    pallas_call x1, Pallas kernels: 2.25 us -> 0.33 us  [body(): call(spread_after_kernel, [VM, HB, HB], [(NY * NX, 2 * YROWS, LOW)], 'spr...]
  transfers between devices with their start and end apart: 7 -> 5, of which waited for: 3 -> 1; matrix products, arithmetic and copies ran while one was open for 0% -> 0% of each run, Pallas kernels for 5% -> 5%
where the time goes in v8:
time: 167 us; the launch traced here: 166 us
  blocking collectives  112 us (67%)
  starting transfers between devices  33.5 us (20%)
  Pallas kernels  15.7 us (9%)
  local copies, waits for them, and re-layouts  1.94 us (1%)
    all_to_all x4, blocking collectives, over_yx(): return lax.all_to_all(x, ('y', 'pair'), 0, 0, tiled=True)  56.5 us
    all_to_all x3, blocking collectives, over_z(): lax.all_to_all(x, 'z', 0, 0, axis_index_groups=ring, tiled=True)  55.9 us
    all_to_all x1, starting transfers between devices, over_z(): lax.all_to_all(x, 'z', 0, 0, axis_index_groups=ring, tiled=True)  11.5 us
    ppermute x1, starting transfers between devices, body(): other_in = lax.ppermute(own_in, 'segment', SWAP)  8.79 us
    ppermute x1, starting transfers between devices, body(): came = lax.ppermute(give, 'segment', SWAP)  7.42 us
    pallas_call x1, Pallas kernels, body(): call(weight_kernel, [HB] * 5, [(WIDTH, HID), (HID, WIDTH)], 'weight', [pl...  4.47 us
    pallas_call x1, Pallas kernels, body(): call(lower_kernel, [SM] + [VM] * 5 + [VM, HB] * 2, [blocks] + [wide] * 4...  3.94 us
    ppermute x1, starting transfers between devices, body(): got = lax.ppermute(other, 'segment', SWAP)  3.88 us
  transfers between devices with their start and end apart: 5, of which 1 were waited for; matrix products, arithmetic and copies ran while one was open for 0% of the time, Pallas kernels for 5%

profile of v8, /device:TPU:1, one launch (start us, length us, event | category | flops | bytes accessed | tf_op | source)
XLA Modules:
  0.0 166.1 jit_solution(17614553090996240042)
XLA Ops:
  0.6 8.8 %collective-permute-start = (bf16[768,768]{1,0:T(8,128)(2,1)}, bf16[768,768]{1,0:T(8,128)(2,1)S(1)}, u32[]{:S(2)}, u32[]{:S(2)}) collective-permute-start(bf16[768,768]{1,0:T(8,128)(2,1)} %bitcast.19), channel_id=1, source_target_pairs={{0,256},{256,0},{1,257},{257,1},{2,258},{258,2},{3,259},{259,3},{4... | collective-permute-start | bytes 3538952 | tf_op jit(solution)/shard_map/ppermute | solution.py:355
  9.4 1.9 %collective-permute-start.1 = (bf16[768,768]{1,0:T(8,128)(2,1)}, bf16[768,768]{1,0:T(8,128)(2,1)S(1)}, u32[]{:S(2)}, u32[]{:S(2)}) collective-permute-start(bf16[768,768]{1,0:T(8,128)(2,1)} %bitcast.22), channel_id=1, source_target_pairs={{0,256},{256,0},{1,257},{257,1},{2,258},{258,2},{3,259},{259,3},{4... | collective-permute-start | bytes 3538952 | tf_op jit(solution)/shard_map/ppermute | solution.py:356
  11.4 2.2 %start.1 = bf16[768,128]{1,0:T(8,128)(2,1)} custom-call(s32[1]{0:T(128)} %bitcast.core_ref, bf16[2,2,192,192]{3,2,1,0:T(8,128)(2,1)} %acts.3, bf16[2,192,192]{2,1,0:T(8,128)(2,1)} %cot.3, f32[2,2,192]{2,1,0:T(2,128)} %gates.3, s32[2,2,192]{2,1,0:T(2,128)} %owners.5, s32[2,2,192]{2,1,0:T(2,128)} %slots.5), custom_call_target="tpu_custom_call" | custom-call | tf_op jit(solution)/shard_map/start/pallas_call | solution.py:360
  13.6 22.5 %all_to_all.40 = bf16[16,48,128]{2,1,0:T(8,128)(2,1)S(1)} all-to-all(bf16[16,48,128]{2,1,0:T(8,128)(2,1)} %bitcast.32), channel_id=1, replica_groups={{32,36,40,44,48,52,56,60,0,4,8,12,16,20,24,28},{33,37,41,45,49,53,57,61..., dimensions={0} | all-to-all | bytes 393216 | tf_op jit(solution)/shard_map/all_to_all | solution.py:343
  36.2 0.3 spread_after.1
  36.5 19.9 %all_to_all.41.saved = bf16[16,192,128]{2,1,0:T(8,128)(2,1)S(1)} all-to-all(bf16[16,192,128]{2,1,0:T(8,128)(2,1)S(1)} %spread_after.1), channel_id=1, replica_groups=mesh['segment'=2,'y'=4,'z'=16,'pair'=4] {'y','pair'}, dimensions={0} | all-to-all | bytes 1572864 | tf_op jit(solution)/shard_map/all_to_all | solution.py:347
  56.4 1.9 %upper.1 = (bf16[16,96,128]{2,1,0:T(8,128)(2,1)S(1)}, bf16[256,768]{1,0:T(8,128)(2,1)S(1)}, bf16[256,768]{1,0:T(8,128)(2,1)S(1)}, bf16[256,768]{1,0:T(8,128)(2,1)S(1)}, bf16[256,768]{1,0:T(8,128)(2,1)S(1)}) custom-call(s32[1]{0:T(128)} %bitcast.core_ref, bf16[16,192,128]{2,1,0:T(8,128)(2,1)S(1)} %all_to_all.41.saved, bf16[768,768]{1,0:T(8,128)(2,1)S(1)} %bitcast.20, ...), custom_call_target="tpu_custom_call" | custom-call | tf_op jit(solution)/shard_map/upper/pallas_call | solution.py:370
  58.4 11.1 %all_to_all.42.parts = bf16[16,96,128]{2,1,0:T(8,128)(2,1)S(1)} all-to-all(bf16[16,96,128]{2,1,0:T(8,128)(2,1)S(1)} %get-tuple-element.21), channel_id=1, replica_groups=mesh['segment'=2,'y'=4,'z'=16,'pair'=4] {'y','pair'}, dimensions={0} | all-to-all | bytes 786432 | tf_op jit(solution)/shard_map/all_to_all | solution.py:347
  69.7 16.1 %all_to_all.43 = bf16[16,24,128]{2,1,0:T(8,128)(2,1)S(1)} all-to-all(bf16[16,24,128]{2,1,0:T(8,128)(2,1)S(1)} %bitcast.29), channel_id=1, replica_groups={{32,36,40,44,48,52,56,60,0,4,8,12,16,20,24,28},{33,37,41,45,49,53,57,61..., dimensions={0} | all-to-all | bytes 196608 | tf_op jit(solution)/shard_map/all_to_all | solution.py:343
  85.8 0.9 middle.1
  86.8 17.2 %all_to_all.44 = bf16[16,48,128]{2,1,0:T(8,128)(2,1)S(1)} all-to-all(bf16[16,48,128]{2,1,0:T(8,128)(2,1)S(1)} %bitcast.30), channel_id=1, replica_groups={{32,36,40,44,48,52,56,60,0,4,8,12,16,20,24,28},{33,37,41,45,49,53,57,61..., dimensions={0} | all-to-all | bytes 393216 | tf_op jit(solution)/shard_map/all_to_all | solution.py:343
  104.3 13.1 %all_to_all.45.saved = bf16[16,192,128]{2,1,0:T(8,128)(2,1)S(1)} all-to-all(bf16[16,192,128]{2,1,0:T(8,128)(2,1)S(1)} %spread.1), channel_id=1, replica_groups=mesh['segment'=2,'y'=4,'z'=16,'pair'=4] {'y','pair'}, dimensions={0} | all-to-all | bytes 1572864 | tf_op jit(solution)/shard_map/all_to_all | solution.py:347
  117.5 3.9 %lower.1 = (bf16[16,96,128]{2,1,0:T(8,128)(2,1)S(1)}, bf16[256,768]{1,0:T(8,128)(2,1)S(1)}, bf16[256,768]{1,0:T(8,128)(2,1)S(1)}, bf16[256,768]{1,0:T(8,128)(2,1...) custom-call(s32[1]{0:T(128)} %bitcast.core_ref, bf16[16,192,128]{2,1,0:T(8,128)(2,1)S(1)} %all_to_all.45.saved, ...), custom_call_target="tpu_custom_call" | custom-call | tf_op jit(solution)/shard_map/lower/pallas_call | solution.py:381
  121.4 0.7 copy-done.10
  122.2 7.4 %collective-permute-start.2 = (bf16[4,256,768]{2,1,0:T(8,128)(2,1)}, bf16[4,256,768]{2,1,0:T(8,128)(2,1)S(1)}, u32[]{:S(2)}, u32[]{:S(2)}) collective-permute-start(bf16[4,256,768]{2,1,0:T(8,128)(2,1)} %get-tuple-element.33), channel_id=1, source_target_pairs={{0,256},{256,0},{1,257},{257,1},{2,258},{258,2},{3,259},{259,3},{4... | collective-permute-start | bytes 4718600 | tf_op jit(solution)/shard_map/ppermute | solution.py:386
  129.6 12.4 %all_to_all.46.parts = bf16[16,96,128]{2,1,0:T(8,128)(2,1)S(1)} all-to-all(bf16[16,96,128]{2,1,0:T(8,128)(2,1)S(1)} %get-tuple-element.27), channel_id=1, replica_groups=mesh['segment'=2,'y'=4,'z'=16,'pair'=4] {'y','pair'}, dimensions={0} | all-to-all | bytes 786432 | tf_op jit(solution)/shard_map/all_to_all | solution.py:347
  142.0 0.9 gather.3
  142.9 11.5 %all-to-all-start.7 = ((bf16[16,24,128]{2,1,0:T(8,128)(2,1)}), bf16[16,24,128]{2,1,0:T(8,128)(2,1)S(1)}, u32[]{:S(2)}, u32[]{:S(2)}) async-start(bf16[16,24,128]{2,1,0:T(8,128)(2,1)} %bitcast.9), calls=%async_computation.7 | async-start | bytes 196608 | tf_op jit(solution)/shard_map/all_to_all | solution.py:343
  154.4 1.2 copy-done.11
  155.6 4.5 %weight.1 = (bf16[768,768]{1,0:T(8,128)(2,1)}, bf16[768,768]{1,0:T(8,128)(2,1)}) custom-call(bf16[256,768]{1,0:T(8,128)(2,1)} %copy-done.7, bf16[256,768]{1,0:T(8,128)(2,1)} %copy-done.8, bf16[256,768]{1,0:T(8,128)(2,1)} %copy-done.9, bf16[256,768]{1,0:T(8,128)(2,1)} %copy-done.10, bf16[4,256,768]{2,1,0:T(8,128)(2,1)} %copy-done.11), custom_call_target="tpu_custom_call" | custom-call | flops 2000000000 | bytes 6000000 | tf_op jit(solution)/shard_map/weight/pallas_call | solution.py:389
  160.1 0.4 end.1
  160.5 3.9 %collective-permute-start.3 = (bf16[192,192]{1,0:T(8,128)(2,1)S(1)}, bf16[192,192]{1,0:T(8,128)(2,1)S(1)}, u32[]{:S(2)}, u32[]{:S(2)}) collective-permute-start(bf16[192,192]{1,0:T(8,128)(2,1)S(1)} %get-tuple-element.35), channel_id=1, source_target_pairs={{0,256},{256,0},{1,257},{257,1},{2,258},{258,2},{3,259},{259,3},{4... | collective-permute-start | bytes 221192 | tf_op jit(solution)/shard_map/ppermute | solution.py:398
  164.4 0.9 collective-permute-done.3
  165.3 0.7 maximum_bitcast_fusion
  (29 shorter events, 0.7 us)
Async XLA Ops:
  0.6 35.5 %collective-permute-start = (bf16[768,768]{1,0:T(8,128)(2,1)}, bf16[768,768]{1,0:T(8,128)(2,1)S(1)}, u32[]{:S(2)}, u32[]{:S(2)}) collective-permute-start(bf16[768,768]{1,0:T(8,128)(2,1)} %bitcast.19), channel_id=1, source_target_pairs={{0,256},{256,0},{1,257},{257,1},{2,258},{258,2},{3,259},{259,3},{4... | collective-permute-start | bytes 3538952 | tf_op jit(solution)/shard_map/ppermute | solution.py:355
  9.4 26.7 %collective-permute-start.1 = (bf16[768,768]{1,0:T(8,128)(2,1)}, bf16[768,768]{1,0:T(8,128)(2,1)S(1)}, u32[]{:S(2)}, u32[]{:S(2)}) collective-permute-start(bf16[768,768]{1,0:T(8,128)(2,1)} %bitcast.22), channel_id=1, source_target_pairs={{0,256},{256,0},{1,257},{257,1},{2,258},{258,2},{3,259},{259,3},{4... | collective-permute-start | bytes 3538952 | tf_op jit(solution)/shard_map/ppermute | solution.py:356
  36.2 20.2 %copy-start.1 = (bf16[1,1,768,768]{3,2,1,0:T(8,128)(2,1)S(1)}, bf16[1,1,768,768]{3,2,1,0:T(8,128)(2,1)}, u32[]{:S(2)}) copy-start(bf16[1,1,768,768]{3,2,1,0:T(8,128)(2,1)} %param.13) | copy-start | bytes 3538948
  36.5 19.9 %copy-start = (bf16[1,1,768,768]{3,2,1,0:T(8,128)(2,1)S(1)}, bf16[1,1,768,768]{3,2,1,0:T(8,128)(2,1)}, u32[]{:S(2)}) copy-start(bf16[1,1,768,768]{3,2,1,0:T(8,128)(2,1)} %param.12) | copy-start | bytes 3538948
  58.3 27.5 %copy-start.2 = (bf16[2,2,192,192]{3,2,1,0:T(8,128)(2,1)S(1)}, bf16[2,2,192,192]{3,2,1,0:T(8,128)(2,1)}, u32[]{:S(2)}) copy-start(bf16[2,2,192,192]{3,2,1,0:T(8,128)(2,1)} %acts.3) | copy-start | bytes 884740
  58.3 27.5 %copy-start.3 = (bf16[2,192,192]{2,1,0:T(8,128)(2,1)S(1)}, bf16[2,192,192]{2,1,0:T(8,128)(2,1)}, u32[]{:S(2)}) copy-start(bf16[2,192,192]{2,1,0:T(8,128)(2,1)} %cot.3) | copy-start | bytes 442372
  58.3 27.5 %copy-start.4 = (s32[2,2,192]{2,1,0:T(2,128)S(1)}, s32[2,2,192]{2,1,0:T(2,128)}, u32[]{:S(2)}) copy-start(s32[2,2,192]{2,1,0:T(2,128)} %owners.5) | copy-start | bytes 9220
  58.3 27.5 %copy-start.5 = (s32[2,2,192]{2,1,0:T(2,128)S(1)}, s32[2,2,192]{2,1,0:T(2,128)}, u32[]{:S(2)}) copy-start(s32[2,2,192]{2,1,0:T(2,128)} %slots.5) | copy-start | bytes 9220
  58.3 27.5 %copy-start.6 = (f32[2,2,192]{2,1,0:T(2,128)S(1)}, f32[2,2,192]{2,1,0:T(2,128)}, u32[]{:S(2)}) copy-start(f32[2,2,192]{2,1,0:T(2,128)} %gates.3) | copy-start | bytes 9220
  121.4 0.7 copy-start.10
  122.2 20.8 %copy-start.7 = (bf16[256,768]{1,0:T(8,128)(2,1)}, bf16[256,768]{1,0:T(8,128)(2,1)S(1)}, u32[]{:S(2)}) copy-start(bf16[256,768]{1,0:T(8,128)(2,1)S(1)} %get-tuple-element.29.k0) | copy-start | bytes 1179652
  122.2 20.8 %copy-start.8 = (bf16[256,768]{1,0:T(8,128)(2,1)}, bf16[256,768]{1,0:T(8,128)(2,1)S(1)}, u32[]{:S(2)}) copy-start(bf16[256,768]{1,0:T(8,128)(2,1)S(1)} %get-tuple-element.30.k1) | copy-start | bytes 1179652
  122.2 20.8 %copy-start.9 = (bf16[256,768]{1,0:T(8,128)(2,1)}, bf16[256,768]{1,0:T(8,128)(2,1)S(1)}, u32[]{:S(2)}) copy-start(bf16[256,768]{1,0:T(8,128)(2,1)S(1)} %get-tuple-element.31.k2) | copy-start | bytes 1179652
  122.2 32.2 %collective-permute-start.2 = (bf16[4,256,768]{2,1,0:T(8,128)(2,1)}, bf16[4,256,768]{2,1,0:T(8,128)(2,1)S(1)}, u32[]{:S(2)}, u32[]{:S(2)}) collective-permute-start(bf16[4,256,768]{2,1,0:T(8,128)(2,1)} %get-tuple-element.33), channel_id=1, source_target_pairs={{0,256},{256,0},{1,257},{257,1},{2,258},{258,2},{3,259},{259,3},{4... | collective-permute-start | bytes 4718600 | tf_op jit(solution)/shard_map/ppermute | solution.py:386
  142.9 17.1 %all-to-all-start.7 = ((bf16[16,24,128]{2,1,0:T(8,128)(2,1)}), bf16[16,24,128]{2,1,0:T(8,128)(2,1)S(1)}, u32[]{:S(2)}, u32[]{:S(2)}) async-start(bf16[16,24,128]{2,1,0:T(8,128)(2,1)} %bitcast.9), calls=%async_computation.7 | async-start | bytes 196608 | tf_op jit(solution)/shard_map/all_to_all | solution.py:343
  154.4 1.2 copy-start.11
  160.5 4.8 %collective-permute-start.3 = (bf16[192,192]{1,0:T(8,128)(2,1)S(1)}, bf16[192,192]{1,0:T(8,128)(2,1)S(1)}, u32[]{:S(2)}, u32[]{:S(2)}) collective-permute-start(bf16[192,192]{1,0:T(8,128)(2,1)S(1)} %get-tuple-element.35), channel_id=1, source_target_pairs={{0,256},{256,0},{1,257},{257,1},{2,258},{258,2},{3,259},{259,3},{4... | collective-permute-start | bytes 221192 | tf_op jit(solution)/shard_map/ppermute | solution.py:398

commit v9 on v8

--- a/solution.py
+++ b/solution.py
@@ -144,10 +144,6 @@
                 out[j * NX + i, a * YROWS : (a + 1) * YROWS, :] = moved[j * YROWS : (j + 1) * YROWS]
 
 
-def spread_after_kernel(rows, one, two, out):
-    spread_kernel(rows, out)
-
-
 def gather_kernel(parts, out):
     shape = (NZ, ZROWS, ALL)
     z, k, at = iota(shape, 0), iota(shape, 1), iota(shape, 2)
@@ -362,8 +358,8 @@
         [pltpu.VMEM((2, TOK, SHARE), BF), pltpu.VMEM(table, F32), pltpu.VMEM(table, I32),
          pltpu.VMEM(table, I32), pltpu.SemaphoreType.DMA((6,))], mib=60,
     )(core, acts, cotangent, gates, owners, slots)
-    (sent,) = call(spread_after_kernel, [VM, HB, HB], [(NY * NX, 2 * YROWS, LOW)], "spread_after")(
-        over_z(packed), other_in, other_out
+    (sent,) = call(spread_kernel, [VM], [(NY * NX, 2 * YROWS, LOW)], "spread", mib=60)(
+        over_z(packed)
     )
     saved = over_yx(sent)
     blocks, wide = (NY * NX, YROWS, LOW), (NY * NZ * CAP, WIDTH)

time: 167 us -> 166 us (level)
  blocking collectives: 112 us -> 70.8 us
  starting transfers between devices: 33.5 us -> 53.3 us
  waiting for transfers between devices: 0.93 us -> 18.3 us
  Pallas kernels: 15.7 us -> 18.7 us
    all_to_all x3 -> x2, blocking collectives: 55.9 us -> 32.5 us  [over_z(): lax.all_to_all(x, 'z', 0, 0, axis_index_groups=ring, tiled=True)]
    all_to_all x1 -> x2, starting transfers between devices: 11.5 us -> 30.6 us  [over_z(): lax.all_to_all(x, 'z', 0, 0, axis_index_groups=ring, tiled=True)]
    all_to_all x4 -> x3, blocking collectives: 56.5 us -> 38.3 us  [over_yx(): return lax.all_to_all(x, ('y', 'pair'), 0, 0, tiled=True)]
    all_to_all x0 -> x1, waiting for transfers between devices: none -> 12.9 us  [over_yx(): return lax.all_to_all(x, ('y', 'pair'), 0, 0, tiled=True)]
    all_to_all x0 -> x1, starting transfers between devices: none -> 6.8 us  [over_yx(): return lax.all_to_all(x, ('y', 'pair'), 0, 0, tiled=True)]
    ppermute x1, starting transfers between devices: 8.79 us -> 3.14 us  [body(): other_in = lax.ppermute(own_in, 'segment', SWAP)]
    all_to_all x1 -> x2, waiting for transfers between devices: 0.01 us -> 4.46 us  [over_z(): lax.all_to_all(x, 'z', 0, 0, axis_index_groups=ring, tiled=True)]
    pallas_call x1, Pallas kernels: 0.33 us -> 2.24 us  [body(): call(spread_kernel, [VM], [(NY * NX, 2 * YROWS, LOW)], 'spread', mib=60)]
  transfers between devices with their start and end apart: 5 -> 7, of which waited for: 1 -> 3; matrix products, arithmetic and copies ran while one was open for 0% -> 0% of each run, Pallas kernels for 5% -> 5%
where the time goes in v9:
time: 166 us; the launch traced here: 165 us
  blocking collectives  70.8 us (43%)
  starting transfers between devices  53.3 us (32%)
  Pallas kernels  18.7 us (11%)
  waiting for transfers between devices  18.3 us (11%)
  local copies, waits for them, and re-layouts  2.66 us (2%)
    all_to_all x3, blocking collectives, over_yx(): return lax.all_to_all(x, ('y', 'pair'), 0, 0, tiled=True)  38.3 us
    all_to_all x2, blocking collectives, over_z(): lax.all_to_all(x, 'z', 0, 0, axis_index_groups=ring, tiled=True)  32.5 us
    all_to_all x2, starting transfers between devices, over_z(): lax.all_to_all(x, 'z', 0, 0, axis_index_groups=ring, tiled=True)  30.6 us
    all_to_all x1, waiting for transfers between devices, over_yx(): return lax.all_to_all(x, ('y', 'pair'), 0, 0, tiled=True)  12.9 us
    ppermute x1, starting transfers between devices, body(): came = lax.ppermute(give, 'segment', SWAP)  7.05 us
    all_to_all x1, starting transfers between devices, over_yx(): return lax.all_to_all(x, ('y', 'pair'), 0, 0, tiled=True)  6.8 us
    pallas_call x1, Pallas kernels, body(): call(weight_kernel, [HB] * 5, [(WIDTH, HID), (HID, WIDTH)], 'weight', [pl...  4.51 us
    all_to_all x2, waiting for transfers between devices, over_z(): lax.all_to_all(x, 'z', 0, 0, axis_index_groups=ring, tiled=True)  4.46 us
  transfers between devices with their start and end apart: 7, of which 3 were waited for; matrix products, arithmetic and copies ran while one was open for 0% of the time, Pallas kernels for 5%

profile of v9, /device:TPU:1, one launch (start us, length us, event | category | flops | bytes accessed | tf_op | source)
XLA Modules:
  0.0 165.3 jit_solution(7159194953741820266)
XLA Ops:
  0.6 2.3 %start.1 = bf16[768,128]{1,0:T(8,128)(2,1)} custom-call(s32[1]{0:T(128)} %bitcast.core_ref, bf16[2,2,192,192]{3,2,1,0:T(8,128)(2,1)} %acts.3, bf16[2,192,192]{2,1,0:T(8,128)(2,1)} %cot.3, f32[2,2,192]{2,1,0:T(2,128)} %gates.3, s32[2,2,192]{2,1,0:T(2,128)} %owners.5, s32[2,2,192]{2,1,0:T(2,128)} %slots.5), custom_call_target="tpu_custom_call" | custom-call | tf_op jit(solution)/shard_map/start/pallas_call | solution.py:356
  3.0 19.1 %all-to-all-start = ((bf16[16,48,128]{2,1,0:T(8,128)(2,1)}), bf16[16,48,128]{2,1,0:T(8,128)(2,1)S(1)}, u32[]{:S(2)}, u32[]{:S(2)}) async-start(bf16[16,48,128]{2,1,0:T(8,128)(2,1)} %bitcast.31), calls=%async_computation | async-start | bytes 393216 | tf_op jit(solution)/shard_map/all_to_all | solution.py:339
  22.1 3.1 %collective-permute-start = (bf16[768,768]{1,0:T(8,128)(2,1)S(1)}, bf16[768,768]{1,0:T(8,128)(2,1)S(1)}, u32[]{:S(2)}, u32[]{:S(2)}) collective-permute-start(bf16[768,768]{1,0:T(8,128)(2,1)S(1)} %bitcast.19), channel_id=1, source_target_pairs={{0,256},{256,0},{1,257},{257,1},{2,258},{258,2},{3,259},{259,3},{4... | collective-permute-start | bytes 3538952 | tf_op jit(solution)/shard_map/ppermute | solution.py:351
  25.3 1.9 %collective-permute-start.1 = (bf16[768,768]{1,0:T(8,128)(2,1)}, bf16[768,768]{1,0:T(8,128)(2,1)}, u32[]{:S(2)}, u32[]{:S(2)}) collective-permute-start(bf16[768,768]{1,0:T(8,128)(2,1)} %bitcast.22), channel_id=1, source_target_pairs={{0,256},{256,0},{1,257},{257,1},{2,258},{258,2},{3,259},{259,3},{4... | collective-permute-start | bytes 3538952 | tf_op jit(solution)/shard_map/ppermute | solution.py:352
  27.2 4.5 %all-to-all-done = bf16[16,48,128]{2,1,0:T(8,128)(2,1)S(1)} async-done(((bf16[16,48,128]{2,1,0:T(8,128)(2,1)}), bf16[16,48,128]{2,1,0:T(8,128)(2,1)S(1)}, u32[]{:S(2)}, u32[]{:S(2)}) %all-to-all-start) | async-done | bytes 196640 | tf_op jit(solution)/shard_map/all_to_all | solution.py:339
  32.4 2.2 %spread.2 = bf16[16,192,128]{2,1,0:T(8,128)(2,1)} custom-call(bf16[768,128]{1,0:T(8,128)(2,1)} %bitcast.32), custom_call_target="tpu_custom_call" | custom-call | tf_op jit(solution)/shard_map/spread/pallas_call | solution.py:361
  34.6 6.8 %all-to-all-start.1 = ((bf16[16,192,128]{2,1,0:T(8,128)(2,1)}), bf16[16,192,128]{2,1,0:T(8,128)(2,1)}, u32[]{:S(2)}, u32[]{:S(2)}) async-start(bf16[16,192,128]{2,1,0:T(8,128)(2,1)} %spread.2), calls=%async_computation.1 | async-start | bytes 1572864 | tf_op jit(solution)/shard_map/all_to_all | solution.py:343
  41.4 12.9 %all-to-all-done.1.saved = bf16[16,192,128]{2,1,0:T(8,128)(2,1)} async-done(((bf16[16,192,128]{2,1,0:T(8,128)(2,1)}), bf16[16,192,128]{2,1,0:T(8,128)(2,1)}, u32[]{:S(2)}, u32[]{:S(2)}) %all-to-all-start.1) | async-done | bytes 786464 | tf_op jit(solution)/shard_map/all_to_all | solution.py:343
  54.3 3.0 %upper.1 = (bf16[16,96,128]{2,1,0:T(8,128)(2,1)S(1)}, bf16[256,768]{1,0:T(8,128)(2,1)S(1)}, bf16[256,768]{1,0:T(8,128)(2,1)S(1)}, bf16[256,768]{1,0:T(8,128)(2,1)S(1)}, bf16[256,768]{1,0:T(8,128)(2,1)S(1)}) custom-call(s32[1]{0:T(128)} %bitcast.core_ref, bf16[16,192,128]{2,1,0:T(8,128)(2,1)} %all-to-all-done.1.saved, bf16[768,768]{1,0:T(8,128)(2,1)S(1)} %bitcast.20, ...), custom_call_target="tpu_custom_call" | custom-call | tf_op jit(solution)/shard_map/upper/pallas_call | solution.py:366
  57.4 12.5 %all_to_all.40.parts = bf16[16,96,128]{2,1,0:T(8,128)(2,1)S(1)} all-to-all(bf16[16,96,128]{2,1,0:T(8,128)(2,1)S(1)} %get-tuple-element.21), channel_id=1, replica_groups=mesh['segment'=2,'y'=4,'z'=16,'pair'=4] {'y','pair'}, dimensions={0} | all-to-all | bytes 786432 | tf_op jit(solution)/shard_map/all_to_all | solution.py:343
  70.2 15.3 %all_to_all.41 = bf16[16,24,128]{2,1,0:T(8,128)(2,1)S(1)} all-to-all(bf16[16,24,128]{2,1,0:T(8,128)(2,1)S(1)} %bitcast.28), channel_id=1, replica_groups={{32,36,40,44,48,52,56,60,0,4,8,12,16,20,24,28},{33,37,41,45,49,53,57,61..., dimensions={0} | all-to-all | bytes 196608 | tf_op jit(solution)/shard_map/all_to_all | solution.py:339
  85.5 0.9 middle.1
  86.5 17.2 %all_to_all.42 = bf16[16,48,128]{2,1,0:T(8,128)(2,1)S(1)} all-to-all(bf16[16,48,128]{2,1,0:T(8,128)(2,1)S(1)} %bitcast.29), channel_id=1, replica_groups={{32,36,40,44,48,52,56,60,0,4,8,12,16,20,24,28},{33,37,41,45,49,53,57,61..., dimensions={0} | all-to-all | bytes 393216 | tf_op jit(solution)/shard_map/all_to_all | solution.py:339
  104.0 13.2 %all_to_all.43.saved = bf16[16,192,128]{2,1,0:T(8,128)(2,1)S(1)} all-to-all(bf16[16,192,128]{2,1,0:T(8,128)(2,1)S(1)} %spread.3), channel_id=1, replica_groups=mesh['segment'=2,'y'=4,'z'=16,'pair'=4] {'y','pair'}, dimensions={0} | all-to-all | bytes 1572864 | tf_op jit(solution)/shard_map/all_to_all | solution.py:343
  117.2 3.7 %lower.1 = (bf16[16,96,128]{2,1,0:T(8,128)(2,1)S(1)}, bf16[256,768]{1,0:T(8,128)(2,1)S(1)}, bf16[256,768]{1,0:T(8,128)(2,1)S(1)}, bf16[256,768]{1,0:T(8,128)(2,1...) custom-call(s32[1]{0:T(128)} %bitcast.core_ref, bf16[16,192,128]{2,1,0:T(8,128)(2,1)S(1)} %all_to_all.43.saved, ...), custom_call_target="tpu_custom_call" | custom-call | tf_op jit(solution)/shard_map/lower/pallas_call | solution.py:377
  120.9 0.7 copy-done.12
  121.6 7.1 %collective-permute-start.2 = (bf16[4,256,768]{2,1,0:T(8,128)(2,1)}, bf16[4,256,768]{2,1,0:T(8,128)(2,1)S(1)}, u32[]{:S(2)}, u32[]{:S(2)}) collective-permute-start(bf16[4,256,768]{2,1,0:T(8,128)(2,1)} %get-tuple-element.33), channel_id=1, source_target_pairs={{0,256},{256,0},{1,257},{257,1},{2,258},{258,2},{3,259},{259,3},{4... | collective-permute-start | bytes 4718600 | tf_op jit(solution)/shard_map/ppermute | solution.py:382
  128.7 12.6 %all_to_all.44.parts = bf16[16,96,128]{2,1,0:T(8,128)(2,1)S(1)} all-to-all(bf16[16,96,128]{2,1,0:T(8,128)(2,1)S(1)} %get-tuple-element.27), channel_id=1, replica_groups=mesh['segment'=2,'y'=4,'z'=16,'pair'=4] {'y','pair'}, dimensions={0} | all-to-all | bytes 786432 | tf_op jit(solution)/shard_map/all_to_all | solution.py:343
  141.3 0.9 gather.3
  142.2 11.5 %all-to-all-start.7 = ((bf16[16,24,128]{2,1,0:T(8,128)(2,1)}), bf16[16,24,128]{2,1,0:T(8,128)(2,1)S(1)}, u32[]{:S(2)}, u32[]{:S(2)}) async-start(bf16[16,24,128]{2,1,0:T(8,128)(2,1)} %bitcast.9), calls=%async_computation.7 | async-start | bytes 196608 | tf_op jit(solution)/shard_map/all_to_all | solution.py:339
  153.7 1.2 copy-done.14
  154.9 4.5 %weight.1 = (bf16[768,768]{1,0:T(8,128)(2,1)}, bf16[768,768]{1,0:T(8,128)(2,1)}) custom-call(bf16[256,768]{1,0:T(8,128)(2,1)} %copy-done.9, bf16[256,768]{1,0:T(8,128)(2,1)} %copy-done.10, bf16[256,768]{1,0:T(8,128)(2,1)} %copy-done.11, bf16[256,768]{1,0:T(8,128)(2,1)} %copy-done.12, bf16[4,256,768]{2,1,0:T(8,128)(2,1)} %copy-done.14), custom_call_target="tpu_custom_call" | custom-call | flops 2000000000 | bytes 6000000 | tf_op jit(solution)/shard_map/weight/pallas_call | solution.py:385
  159.9 3.7 %collective-permute-start.3 = (bf16[192,192]{1,0:T(8,128)(2,1)S(1)}, bf16[192,192]{1,0:T(8,128)(2,1)S(1)}, u32[]{:S(2)}, u32[]{:S(2)}) collective-permute-start(bf16[192,192]{1,0:T(8,128)(2,1)S(1)} %get-tuple-element.35), channel_id=1, source_target_pairs={{0,256},{256,0},{1,257},{257,1},{2,258},{258,2},{3,259},{259,3},{4... | collective-permute-start | bytes 221192 | tf_op jit(solution)/shard_map/ppermute | solution.py:394
  163.6 0.9 collective-permute-done.3
  (37 shorter events, 2.5 us)
Async XLA Ops:
  0.6 21.5 %copy-start = (bf16[1,1,768,768]{3,2,1,0:T(8,128)(2,1)S(1)}, bf16[1,1,768,768]{3,2,1,0:T(8,128)(2,1)}, u32[]{:S(2)}) copy-start(bf16[1,1,768,768]{3,2,1,0:T(8,128)(2,1)} %param.12) | copy-start | bytes 3538948
  3.0 28.7 %all-to-all-start = ((bf16[16,48,128]{2,1,0:T(8,128)(2,1)}), bf16[16,48,128]{2,1,0:T(8,128)(2,1)S(1)}, u32[]{:S(2)}, u32[]{:S(2)}) async-start(bf16[16,48,128]{2,1,0:T(8,128)(2,1)} %bitcast.31), calls=%async_computation | async-start | bytes 393216 | tf_op jit(solution)/shard_map/all_to_all | solution.py:339
  22.1 19.3 %collective-permute-start = (bf16[768,768]{1,0:T(8,128)(2,1)S(1)}, bf16[768,768]{1,0:T(8,128)(2,1)S(1)}, u32[]{:S(2)}, u32[]{:S(2)}) collective-permute-start(bf16[768,768]{1,0:T(8,128)(2,1)S(1)} %bitcast.19), channel_id=1, source_target_pairs={{0,256},{256,0},{1,257},{257,1},{2,258},{258,2},{3,259},{259,3},{4... | collective-permute-start | bytes 3538952 | tf_op jit(solution)/shard_map/ppermute | solution.py:351
  25.3 16.1 %collective-permute-start.1 = (bf16[768,768]{1,0:T(8,128)(2,1)}, bf16[768,768]{1,0:T(8,128)(2,1)}, u32[]{:S(2)}, u32[]{:S(2)}) collective-permute-start(bf16[768,768]{1,0:T(8,128)(2,1)} %bitcast.22), channel_id=1, source_target_pairs={{0,256},{256,0},{1,257},{257,1},{2,258},{258,2},{3,259},{259,3},{4... | collective-permute-start | bytes 3538952 | tf_op jit(solution)/shard_map/ppermute | solution.py:352
  31.7 0.7 copy-start.13
  32.4 22.0 %copy-start.1 = (bf16[1,1,768,768]{3,2,1,0:T(8,128)(2,1)S(1)}, bf16[1,1,768,768]{3,2,1,0:T(8,128)(2,1)}, u32[]{:S(2)}) copy-start(bf16[1,1,768,768]{3,2,1,0:T(8,128)(2,1)} %param.13) | copy-start | bytes 3538948
  34.6 19.7 %all-to-all-start.1 = ((bf16[16,192,128]{2,1,0:T(8,128)(2,1)}), bf16[16,192,128]{2,1,0:T(8,128)(2,1)}, u32[]{:S(2)}, u32[]{:S(2)}) async-start(bf16[16,192,128]{2,1,0:T(8,128)(2,1)} %spread.2), calls=%async_computation.1 | async-start | bytes 1572864 | tf_op jit(solution)/shard_map/all_to_all | solution.py:343
  57.3 28.1 %copy-start.2 = (bf16[2,2,192,192]{3,2,1,0:T(8,128)(2,1)S(1)}, bf16[2,2,192,192]{3,2,1,0:T(8,128)(2,1)}, u32[]{:S(2)}) copy-start(bf16[2,2,192,192]{3,2,1,0:T(8,128)(2,1)} %acts.3) | copy-start | bytes 884740
  57.4 28.1 %copy-start.3 = (bf16[2,192,192]{2,1,0:T(8,128)(2,1)S(1)}, bf16[2,192,192]{2,1,0:T(8,128)(2,1)}, u32[]{:S(2)}) copy-start(bf16[2,192,192]{2,1,0:T(8,128)(2,1)} %cot.3) | copy-start | bytes 442372
  57.4 28.1 %copy-start.6 = (s32[2,2,192]{2,1,0:T(2,128)S(1)}, s32[2,2,192]{2,1,0:T(2,128)}, u32[]{:S(2)}) copy-start(s32[2,2,192]{2,1,0:T(2,128)} %owners.5) | copy-start | bytes 9220
  57.4 28.1 %copy-start.7 = (s32[2,2,192]{2,1,0:T(2,128)S(1)}, s32[2,2,192]{2,1,0:T(2,128)}, u32[]{:S(2)}) copy-start(s32[2,2,192]{2,1,0:T(2,128)} %slots.5) | copy-start | bytes 9220
  57.4 28.1 %copy-start.8 = (f32[2,2,192]{2,1,0:T(2,128)S(1)}, f32[2,2,192]{2,1,0:T(2,128)}, u32[]{:S(2)}) copy-start(f32[2,2,192]{2,1,0:T(2,128)} %gates.3) | copy-start | bytes 9220
  86.4 17.2 %copy-start.4 = (bf16[192,192]{1,0:T(8,128)(2,1)}, bf16[192,192]{1,0:T(8,128)(2,1)S(1)}, u32[]{:S(2)}) copy-start(bf16[192,192]{1,0:T(8,128)(2,1)S(1)} %get-tuple-element.28.above) | copy-start | bytes 221188
  120.9 0.7 copy-start.12
  121.6 20.6 %copy-start.9 = (bf16[256,768]{1,0:T(8,128)(2,1)}, bf16[256,768]{1,0:T(8,128)(2,1)S(1)}, u32[]{:S(2)}) copy-start(bf16[256,768]{1,0:T(8,128)(2,1)S(1)} %get-tuple-element.29.k0) | copy-start | bytes 1179652
  121.6 20.6 %copy-start.10 = (bf16[256,768]{1,0:T(8,128)(2,1)}, bf16[256,768]{1,0:T(8,128)(2,1)S(1)}, u32[]{:S(2)}) copy-start(bf16[256,768]{1,0:T(8,128)(2,1)S(1)} %get-tuple-element.30.k1) | copy-start | bytes 1179652
  121.6 20.6 %copy-start.11 = (bf16[256,768]{1,0:T(8,128)(2,1)}, bf16[256,768]{1,0:T(8,128)(2,1)S(1)}, u32[]{:S(2)}) copy-start(bf16[256,768]{1,0:T(8,128)(2,1)S(1)} %get-tuple-element.31.k2) | copy-start | bytes 1179652
  121.6 32.1 %collective-permute-start.2 = (bf16[4,256,768]{2,1,0:T(8,128)(2,1)}, bf16[4,256,768]{2,1,0:T(8,128)(2,1)S(1)}, u32[]{:S(2)}, u32[]{:S(2)}) collective-permute-start(bf16[4,256,768]{2,1,0:T(8,128)(2,1)} %get-tuple-element.33), channel_id=1, source_target_pairs={{0,256},{256,0},{1,257},{257,1},{2,258},{258,2},{3,259},{259,3},{4... | collective-permute-start | bytes 4718600 | tf_op jit(solution)/shard_map/ppermute | solution.py:382
  142.2 17.2 %all-to-all-start.7 = ((bf16[16,24,128]{2,1,0:T(8,128)(2,1)}), bf16[16,24,128]{2,1,0:T(8,128)(2,1)S(1)}, u32[]{:S(2)}, u32[]{:S(2)}) async-start(bf16[16,24,128]{2,1,0:T(8,128)(2,1)} %bitcast.9), calls=%async_computation.7 | async-start | bytes 196608 | tf_op jit(solution)/shard_map/all_to_all | solution.py:339
  153.7 1.2 copy-start.14
  154.9 4.5 %copy-start.5 = (bf16[192,192]{1,0:T(8,128)(2,1)S(1)}, bf16[192,192]{1,0:T(8,128)(2,1)}, u32[]{:S(2)}) copy-start(bf16[192,192]{1,0:T(8,128)(2,1)} %copy-done.4) | copy-start | bytes 221188
  159.9 4.6 %collective-permute-start.3 = (bf16[192,192]{1,0:T(8,128)(2,1)S(1)}, bf16[192,192]{1,0:T(8,128)(2,1)S(1)}, u32[]{:S(2)}, u32[]{:S(2)}) collective-permute-start(bf16[192,192]{1,0:T(8,128)(2,1)S(1)} %get-tuple-element.35), channel_id=1, source_target_pairs={{0,256},{256,0},{1,257},{257,1},{2,258},{258,2},{3,259},{259,3},{4... | collective-permute-start | bytes 221192 | tf_op jit(solution)/shard_map/ppermute | solution.py:394

commit v10 on v9

--- a/solution.py
+++ b/solution.py
@@ -358,7 +358,7 @@
         [pltpu.VMEM((2, TOK, SHARE), BF), pltpu.VMEM(table, F32), pltpu.VMEM(table, I32),
          pltpu.VMEM(table, I32), pltpu.SemaphoreType.DMA((6,))], mib=60,
     )(core, acts, cotangent, gates, owners, slots)
-    (sent,) = call(spread_kernel, [VM], [(NY * NX, 2 * YROWS, LOW)], "spread", mib=60)(
+    (sent,) = call(spread_kernel, [VM], [(NY * NX, 2 * YROWS, LOW)], "spread", mib=62)(
         over_z(packed)
     )
     saved = over_yx(sent)

time: 166 us -> 165 us (level)
  no operation moved by 1% of the time
where the time goes in v10:
time: 165 us; the launch traced here: 164 us
  blocking collectives  70.3 us (43%)
  starting transfers between devices  53.5 us (32%)
  waiting for transfers between devices  18.2 us (11%)
  Pallas kernels  17.9 us (11%)
  local copies, waits for them, and re-layouts  2.63 us (2%)
    all_to_all x3, blocking collectives, over_yx(): return lax.all_to_all(x, ('y', 'pair'), 0, 0, tiled=True)  37.9 us
    all_to_all x2, blocking collectives, over_z(): lax.all_to_all(x, 'z', 0, 0, axis_index_groups=ring, tiled=True)  32.4 us
    all_to_all x2, starting transfers between devices, over_z(): lax.all_to_all(x, 'z', 0, 0, axis_index_groups=ring, tiled=True)  30.6 us
    all_to_all x1, waiting for transfers between devices, over_yx(): return lax.all_to_all(x, ('y', 'pair'), 0, 0, tiled=True)  12.8 us
    ppermute x1, starting transfers between devices, body(): came = lax.ppermute(give, 'segment', SWAP)  7.07 us
    all_to_all x1, starting transfers between devices, over_yx(): return lax.all_to_all(x, ('y', 'pair'), 0, 0, tiled=True)  6.88 us
    pallas_call x1, Pallas kernels, body(): call(weight_kernel, [HB] * 5, [(WIDTH, HID), (HID, WIDTH)], 'weight', [pl...  4.47 us
    all_to_all x2, waiting for transfers between devices, over_z(): lax.all_to_all(x, 'z', 0, 0, axis_index_groups=ring, tiled=True)  4.46 us
  transfers between devices with their start and end apart: 7, of which 3 were waited for; matrix products, arithmetic and copies ran while one was open for 0% of the time, Pallas kernels for 5%

profile of v10, /device:TPU:1, one launch (start us, length us, event | category | flops | bytes accessed | tf_op | source)
XLA Modules:
  0.0 164.2 jit_solution(14227903265196304274)
XLA Ops:
  0.6 2.3 %start.1 = bf16[768,128]{1,0:T(8,128)(2,1)} custom-call(s32[1]{0:T(128)} %bitcast.core_ref, bf16[2,2,192,192]{3,2,1,0:T(8,128)(2,1)} %acts.3, bf16[2,192,192]{2,1,0:T(8,128)(2,1)} %cot.3, f32[2,2,192]{2,1,0:T(2,128)} %gates.3, s32[2,2,192]{2,1,0:T(2,128)} %owners.5, s32[2,2,192]{2,1,0:T(2,128)} %slots.5), custom_call_target="tpu_custom_call" | custom-call | tf_op jit(solution)/shard_map/start/pallas_call | solution.py:356
  3.0 19.1 %all-to-all-start = ((bf16[16,48,128]{2,1,0:T(8,128)(2,1)}), bf16[16,48,128]{2,1,0:T(8,128)(2,1)S(1)}, u32[]{:S(2)}, u32[]{:S(2)}) async-start(bf16[16,48,128]{2,1,0:T(8,128)(2,1)} %bitcast.31), calls=%async_computation | async-start | bytes 393216 | tf_op jit(solution)/shard_map/all_to_all | solution.py:339
  22.1 3.1 %collective-permute-start = (bf16[768,768]{1,0:T(8,128)(2,1)S(1)}, bf16[768,768]{1,0:T(8,128)(2,1)}, u32[]{:S(2)}, u32[]{:S(2)}) collective-permute-start(bf16[768,768]{1,0:T(8,128)(2,1)S(1)} %bitcast.19), channel_id=1, source_target_pairs={{0,256},{256,0},{1,257},{257,1},{2,258},{258,2},{3,259},{259,3},{4... | collective-permute-start | bytes 3538952 | tf_op jit(solution)/shard_map/ppermute | solution.py:351
  25.3 1.9 %collective-permute-start.1 = (bf16[768,768]{1,0:T(8,128)(2,1)}, bf16[768,768]{1,0:T(8,128)(2,1)}, u32[]{:S(2)}, u32[]{:S(2)}) collective-permute-start(bf16[768,768]{1,0:T(8,128)(2,1)} %bitcast.22), channel_id=1, source_target_pairs={{0,256},{256,0},{1,257},{257,1},{2,258},{258,2},{3,259},{259,3},{4... | collective-permute-start | bytes 3538952 | tf_op jit(solution)/shard_map/ppermute | solution.py:352
  27.2 4.5 %all-to-all-done = bf16[16,48,128]{2,1,0:T(8,128)(2,1)S(1)} async-done(((bf16[16,48,128]{2,1,0:T(8,128)(2,1)}), bf16[16,48,128]{2,1,0:T(8,128)(2,1)S(1)}, u32[]{:S(2)}, u32[]{:S(2)}) %all-to-all-start) | async-done | bytes 196640 | tf_op jit(solution)/shard_map/all_to_all | solution.py:339
  32.4 2.1 %spread.2 = bf16[16,192,128]{2,1,0:T(8,128)(2,1)} custom-call(bf16[768,128]{1,0:T(8,128)(2,1)} %bitcast.32), custom_call_target="tpu_custom_call" | custom-call | tf_op jit(solution)/shard_map/spread/pallas_call | solution.py:361
  34.5 6.9 %all-to-all-start.1 = ((bf16[16,192,128]{2,1,0:T(8,128)(2,1)}), bf16[16,192,128]{2,1,0:T(8,128)(2,1)S(1)}, u32[]{:S(2)}, u32[]{:S(2)}) async-start(bf16[16,192,128]{2,1,0:T(8,128)(2,1)} %spread.2), calls=%async_computation.1 | async-start | bytes 1572864 | tf_op jit(solution)/shard_map/all_to_all | solution.py:343
  41.4 12.8 %all-to-all-done.1.saved = bf16[16,192,128]{2,1,0:T(8,128)(2,1)S(1)} async-done(((bf16[16,192,128]{2,1,0:T(8,128)(2,1)}), bf16[16,192,128]{2,1,0:T(8,128)(2,1)S(1)}, u32[]{:S(2)}, u32[]{:S(2)}) %all-to-all-start.1) | async-done | bytes 786464 | tf_op jit(solution)/shard_map/all_to_all | solution.py:343
  54.2 1.9 %upper.1 = (bf16[16,96,128]{2,1,0:T(8,128)(2,1)S(1)}, bf16[256,768]{1,0:T(8,128)(2,1)S(1)}, bf16[256,768]{1,0:T(8,128)(2,1)S(1)}, bf16[256,768]{1,0:T(8,128)(2,1)S(1)}, bf16[256,768]{1,0:T(8,128)(2,1)S(1)}) custom-call(s32[1]{0:T(128)} %bitcast.core_ref, bf16[16,192,128]{2,1,0:T(8,128)(2,1)S(1)} %all-to-all-done.1.saved, bf16[768,768]{1,0:T(8,128)(2,1)S(1)} %bitcast.20, ...), custom_call_target="tpu_custom_call" | custom-call | tf_op jit(solution)/shard_map/upper/pallas_call | solution.py:366
  56.2 12.5 %all_to_all.40.parts = bf16[16,96,128]{2,1,0:T(8,128)(2,1)S(1)} all-to-all(bf16[16,96,128]{2,1,0:T(8,128)(2,1)S(1)} %get-tuple-element.21), channel_id=1, replica_groups=mesh['segment'=2,'y'=4,'z'=16,'pair'=4] {'y','pair'}, dimensions={0} | all-to-all | bytes 786432 | tf_op jit(solution)/shard_map/all_to_all | solution.py:343
  69.0 15.2 %all_to_all.41 = bf16[16,24,128]{2,1,0:T(8,128)(2,1)S(1)} all-to-all(bf16[16,24,128]{2,1,0:T(8,128)(2,1)S(1)} %bitcast.28), channel_id=1, replica_groups={{32,36,40,44,48,52,56,60,0,4,8,12,16,20,24,28},{33,37,41,45,49,53,57,61..., dimensions={0} | all-to-all | bytes 196608 | tf_op jit(solution)/shard_map/all_to_all | solution.py:339
  84.2 0.9 middle.1
  85.2 17.2 %all_to_all.42 = bf16[16,48,128]{2,1,0:T(8,128)(2,1)S(1)} all-to-all(bf16[16,48,128]{2,1,0:T(8,128)(2,1)S(1)} %bitcast.29), channel_id=1, replica_groups={{32,36,40,44,48,52,56,60,0,4,8,12,16,20,24,28},{33,37,41,45,49,53,57,61..., dimensions={0} | all-to-all | bytes 393216 | tf_op jit(solution)/shard_map/all_to_all | solution.py:339
  102.8 13.1 %all_to_all.43.saved = bf16[16,192,128]{2,1,0:T(8,128)(2,1)S(1)} all-to-all(bf16[16,192,128]{2,1,0:T(8,128)(2,1)S(1)} %spread.3), channel_id=1, replica_groups=mesh['segment'=2,'y'=4,'z'=16,'pair'=4] {'y','pair'}, dimensions={0} | all-to-all | bytes 1572864 | tf_op jit(solution)/shard_map/all_to_all | solution.py:343
  115.9 4.1 %lower.1 = (bf16[16,96,128]{2,1,0:T(8,128)(2,1)S(1)}, bf16[256,768]{1,0:T(8,128)(2,1)S(1)}, bf16[256,768]{1,0:T(8,128)(2,1)S(1)}, bf16[256,768]{1,0:T(8,128)(2,1...) custom-call(s32[1]{0:T(128)} %bitcast.core_ref, bf16[16,192,128]{2,1,0:T(8,128)(2,1)S(1)} %all_to_all.43.saved, ...), custom_call_target="tpu_custom_call" | custom-call | tf_op jit(solution)/shard_map/lower/pallas_call | solution.py:377
  120.0 0.7 copy-done.10
  120.8 7.1 %collective-permute-start.2 = (bf16[4,256,768]{2,1,0:T(8,128)(2,1)}, bf16[4,256,768]{2,1,0:T(8,128)(2,1)S(1)}, u32[]{:S(2)}, u32[]{:S(2)}) collective-permute-start(bf16[4,256,768]{2,1,0:T(8,128)(2,1)} %get-tuple-element.33), channel_id=1, source_target_pairs={{0,256},{256,0},{1,257},{257,1},{2,258},{258,2},{3,259},{259,3},{4... | collective-permute-start | bytes 4718600 | tf_op jit(solution)/shard_map/ppermute | solution.py:382
  127.9 12.3 %all_to_all.44.parts = bf16[16,96,128]{2,1,0:T(8,128)(2,1)S(1)} all-to-all(bf16[16,96,128]{2,1,0:T(8,128)(2,1)S(1)} %get-tuple-element.27), channel_id=1, replica_groups=mesh['segment'=2,'y'=4,'z'=16,'pair'=4] {'y','pair'}, dimensions={0} | all-to-all | bytes 786432 | tf_op jit(solution)/shard_map/all_to_all | solution.py:343
  140.1 0.9 gather.3
  141.0 11.5 %all-to-all-start.7 = ((bf16[16,24,128]{2,1,0:T(8,128)(2,1)}), bf16[16,24,128]{2,1,0:T(8,128)(2,1)S(1)}, u32[]{:S(2)}, u32[]{:S(2)}) async-start(bf16[16,24,128]{2,1,0:T(8,128)(2,1)} %bitcast.9), calls=%async_computation.7 | async-start | bytes 196608 | tf_op jit(solution)/shard_map/all_to_all | solution.py:339
  152.5 1.2 copy-done.12
  153.7 4.5 %weight.1 = (bf16[768,768]{1,0:T(8,128)(2,1)}, bf16[768,768]{1,0:T(8,128)(2,1)}) custom-call(bf16[256,768]{1,0:T(8,128)(2,1)} %copy-done.7, bf16[256,768]{1,0:T(8,128)(2,1)} %copy-done.8, bf16[256,768]{1,0:T(8,128)(2,1)} %copy-done.9, bf16[256,768]{1,0:T(8,128)(2,1)} %copy-done.10, bf16[4,256,768]{2,1,0:T(8,128)(2,1)} %copy-done.12), custom_call_target="tpu_custom_call" | custom-call | flops 2000000000 | bytes 6000000 | tf_op jit(solution)/shard_map/weight/pallas_call | solution.py:385
  158.6 3.9 %collective-permute-start.3 = (bf16[192,192]{1,0:T(8,128)(2,1)S(1)}, bf16[192,192]{1,0:T(8,128)(2,1)S(1)}, u32[]{:S(2)}, u32[]{:S(2)}) collective-permute-start(bf16[192,192]{1,0:T(8,128)(2,1)S(1)} %get-tuple-element.35), channel_id=1, source_target_pairs={{0,256},{256,0},{1,257},{257,1},{2,258},{258,2},{3,259},{259,3},{4... | collective-permute-start | bytes 221192 | tf_op jit(solution)/shard_map/ppermute | solution.py:394
  162.5 0.9 collective-permute-done.3
  (33 shorter events, 2.5 us)
Async XLA Ops:
  0.6 21.5 %copy-start = (bf16[1,1,768,768]{3,2,1,0:T(8,128)(2,1)S(1)}, bf16[1,1,768,768]{3,2,1,0:T(8,128)(2,1)}, u32[]{:S(2)}) copy-start(bf16[1,1,768,768]{3,2,1,0:T(8,128)(2,1)} %param.12) | copy-start | bytes 3538948
  3.0 28.7 %all-to-all-start = ((bf16[16,48,128]{2,1,0:T(8,128)(2,1)}), bf16[16,48,128]{2,1,0:T(8,128)(2,1)S(1)}, u32[]{:S(2)}, u32[]{:S(2)}) async-start(bf16[16,48,128]{2,1,0:T(8,128)(2,1)} %bitcast.31), calls=%async_computation | async-start | bytes 393216 | tf_op jit(solution)/shard_map/all_to_all | solution.py:339
  22.1 19.3 %collective-permute-start = (bf16[768,768]{1,0:T(8,128)(2,1)S(1)}, bf16[768,768]{1,0:T(8,128)(2,1)}, u32[]{:S(2)}, u32[]{:S(2)}) collective-permute-start(bf16[768,768]{1,0:T(8,128)(2,1)S(1)} %bitcast.19), channel_id=1, source_target_pairs={{0,256},{256,0},{1,257},{257,1},{2,258},{258,2},{3,259},{259,3},{4... | collective-permute-start | bytes 3538952 | tf_op jit(solution)/shard_map/ppermute | solution.py:351
  25.3 16.1 %collective-permute-start.1 = (bf16[768,768]{1,0:T(8,128)(2,1)}, bf16[768,768]{1,0:T(8,128)(2,1)}, u32[]{:S(2)}, u32[]{:S(2)}) collective-permute-start(bf16[768,768]{1,0:T(8,128)(2,1)} %bitcast.22), channel_id=1, source_target_pairs={{0,256},{256,0},{1,257},{257,1},{2,258},{258,2},{3,259},{259,3},{4... | collective-permute-start | bytes 3538952 | tf_op jit(solution)/shard_map/ppermute | solution.py:352
  31.7 0.7 copy-start.11
  34.5 19.7 %copy-start.1 = (bf16[1,1,768,768]{3,2,1,0:T(8,128)(2,1)S(1)}, bf16[1,1,768,768]{3,2,1,0:T(8,128)(2,1)}, u32[]{:S(2)}) copy-start(bf16[1,1,768,768]{3,2,1,0:T(8,128)(2,1)} %param.13) | copy-start | bytes 3538948
  34.5 19.7 %all-to-all-start.1 = ((bf16[16,192,128]{2,1,0:T(8,128)(2,1)}), bf16[16,192,128]{2,1,0:T(8,128)(2,1)S(1)}, u32[]{:S(2)}, u32[]{:S(2)}) async-start(bf16[16,192,128]{2,1,0:T(8,128)(2,1)} %spread.2), calls=%async_computation.1 | async-start | bytes 1572864 | tf_op jit(solution)/shard_map/all_to_all | solution.py:343
  56.2 28.1 %copy-start.2 = (bf16[2,2,192,192]{3,2,1,0:T(8,128)(2,1)S(1)}, bf16[2,2,192,192]{3,2,1,0:T(8,128)(2,1)}, u32[]{:S(2)}) copy-start(bf16[2,2,192,192]{3,2,1,0:T(8,128)(2,1)} %acts.3) | copy-start | bytes 884740
  56.2 28.1 %copy-start.3 = (bf16[2,192,192]{2,1,0:T(8,128)(2,1)S(1)}, bf16[2,192,192]{2,1,0:T(8,128)(2,1)}, u32[]{:S(2)}) copy-start(bf16[2,192,192]{2,1,0:T(8,128)(2,1)} %cot.3) | copy-start | bytes 442372
  56.2 28.0 %copy-start.4 = (s32[2,2,192]{2,1,0:T(2,128)S(1)}, s32[2,2,192]{2,1,0:T(2,128)}, u32[]{:S(2)}) copy-start(s32[2,2,192]{2,1,0:T(2,128)} %owners.5) | copy-start | bytes 9220
  56.2 28.0 %copy-start.5 = (s32[2,2,192]{2,1,0:T(2,128)S(1)}, s32[2,2,192]{2,1,0:T(2,128)}, u32[]{:S(2)}) copy-start(s32[2,2,192]{2,1,0:T(2,128)} %slots.5) | copy-start | bytes 9220
  56.2 28.0 %copy-start.6 = (f32[2,2,192]{2,1,0:T(2,128)S(1)}, f32[2,2,192]{2,1,0:T(2,128)}, u32[]{:S(2)}) copy-start(f32[2,2,192]{2,1,0:T(2,128)} %gates.3) | copy-start | bytes 9220
  120.0 0.7 copy-start.10
  120.8 20.2 %copy-start.7 = (bf16[256,768]{1,0:T(8,128)(2,1)}, bf16[256,768]{1,0:T(8,128)(2,1)S(1)}, u32[]{:S(2)}) copy-start(bf16[256,768]{1,0:T(8,128)(2,1)S(1)} %get-tuple-element.29.k0) | copy-start | bytes 1179652
  120.8 20.2 %copy-start.8 = (bf16[256,768]{1,0:T(8,128)(2,1)}, bf16[256,768]{1,0:T(8,128)(2,1)S(1)}, u32[]{:S(2)}) copy-start(bf16[256,768]{1,0:T(8,128)(2,1)S(1)} %get-tuple-element.30.k1) | copy-start | bytes 1179652
  120.8 20.2 %copy-start.9 = (bf16[256,768]{1,0:T(8,128)(2,1)}, bf16[256,768]{1,0:T(8,128)(2,1)S(1)}, u32[]{:S(2)}) copy-start(bf16[256,768]{1,0:T(8,128)(2,1)S(1)} %get-tuple-element.31.k2) | copy-start | bytes 1179652
  120.8 31.7 %collective-permute-start.2 = (bf16[4,256,768]{2,1,0:T(8,128)(2,1)}, bf16[4,256,768]{2,1,0:T(8,128)(2,1)S(1)}, u32[]{:S(2)}, u32[]{:S(2)}) collective-permute-start(bf16[4,256,768]{2,1,0:T(8,128)(2,1)} %get-tuple-element.33), channel_id=1, source_target_pairs={{0,256},{256,0},{1,257},{257,1},{2,258},{258,2},{3,259},{259,3},{4... | collective-permute-start | bytes 4718600 | tf_op jit(solution)/shard_map/ppermute | solution.py:382
  141.0 17.1 %all-to-all-start.7 = ((bf16[16,24,128]{2,1,0:T(8,128)(2,1)}), bf16[16,24,128]{2,1,0:T(8,128)(2,1)S(1)}, u32[]{:S(2)}, u32[]{:S(2)}) async-start(bf16[16,24,128]{2,1,0:T(8,128)(2,1)} %bitcast.9), calls=%async_computation.7 | async-start | bytes 196608 | tf_op jit(solution)/shard_map/all_to_all | solution.py:339
  152.5 1.2 copy-start.12
  158.6 4.8 %collective-permute-start.3 = (bf16[192,192]{1,0:T(8,128)(2,1)S(1)}, bf16[192,192]{1,0:T(8,128)(2,1)S(1)}, u32[]{:S(2)}, u32[]{:S(2)}) collective-permute-start(bf16[192,192]{1,0:T(8,128)(2,1)S(1)} %get-tuple-element.35), channel_id=1, source_target_pairs={{0,256},{256,0},{1,257},{257,1},{2,258},{258,2},{3,259},{259,3},{4... | collective-permute-start | bytes 221192 | tf_op jit(solution)/shard_map/ppermute | solution.py:394
